TPU v7x, 32 devices: a whole 2x2x4 slice. The times are simulated.
32 devices in a mesh: dp: 8 (over y, x, core), expert: 4 (over z).
Axes of the slice: x: 2, y: 2, z: 4, core: 2. Of those that a mesh axis runs over, the one named last changes fastest.
Arguments:
- tokens: bfloat16 [4096, 2048], P(('dp', 'expert')), may hold values from -6 to 6
- teacher: bfloat16 [4096, 2048], P(('dp', 'expert')), may hold values from -6 to 6
- attn_routes: int32 [4096, 2], P(('dp', 'expert')), may hold values from 0 to 3, all different within a row; in each aligned block of 128 rows (0 to 127, 128 to 255, ...) at most 96 rows name the same one
- mlp_routes: int32 [4096, 2], P(('dp', 'expert')), may hold values from 0 to 3, all different within a row; in each aligned block of 128 rows (0 to 127, 128 to 255, ...) at most 96 rows name the same one
- image_mask: int32 [4096], P(('dp', 'expert')), may hold values from 0 to 1, as said below
- valid: int32 [4096], P(('dp', 'expert')), may hold values from 0 to 1
- master_query: float32 [2048, 8192], P('dp', 'expert'), may hold values from -0.125 to 0.125
- moment_query: float32 [2048, 8192], P('dp', 'expert'), may hold values from -0.01875 to 0.01875
- square_query: float32 [2048, 8192], P('dp', 'expert'), may hold values from 1.953125e-05 to 0.0001953125
- master_project: float32 [8192, 2048], P('expert', 'dp'), may hold values from -0.5 to 0.5
- moment_project: float32 [8192, 2048], P('expert', 'dp'), may hold values from -0.00515625 to 0.00515625
- square_project: float32 [8192, 2048], P('expert', 'dp'), may hold values from 1.4648438e-06 to 1.4648437e-05
- master_gate_up: float32 [2, 2048, 22528], P(None, 'dp', 'expert'), may hold values from -0.125 to 0.125
- moment_gate_up: float32 [2, 2048, 22528], P(None, 'dp', 'expert'), may hold values from -0.0075 to 0.0075
- square_gate_up: float32 [2, 2048, 22528], P(None, 'dp', 'expert'), may hold values from 3.125e-06 to 3.125e-05
- master_down: float32 [22528, 2048], P('expert', 'dp'), may hold values from -0.109375 to 0.109375
- moment_down: float32 [22528, 2048], P('expert', 'dp'), may hold values from -0.0103125 to 0.0103125
- square_down: float32 [22528, 2048], P('expert', 'dp'), may hold values from 5.859375e-06 to 5.859375e-05
- master_key_value: float32 [2048, 4096], P(('dp', 'expert')), may hold values from -0.125 to 0.125
- moment_key_value: float32 [2048, 4096], P(('dp', 'expert')), may hold values from -0.080625 to 0.080625
- square_key_value: float32 [2048, 4096], P(('dp', 'expert')), may hold values from 0.00036621094 to 0.0036621094
- master_router: float32 [2048, 8], P(('dp', 'expert')), may hold values from -0.09375 to 0.09375
- moment_router: float32 [2048, 8], P(('dp', 'expert')), may hold values from -2.25 to 2.25
- square_router: float32 [2048, 8], P(('dp', 'expert')), may hold values from 0.28076172 to 2.8076172
- master_gains: float32 [2, 2048], P(None, ('dp', 'expert')), may hold values from 0.5 to 1.5
- moment_gains: float32 [2, 2048], P(None, ('dp', 'expert')), may hold values from -0.6 to 0.6
- square_gains: float32 [2, 2048], P(None, ('dp', 'expert')), may hold values from 0.02 to 0.2
Outputs:
- output: float32 [4096, 2048], P(('dp', 'expert'))
- loss: float32 [], replicated
- input_grad: float32 [4096, 2048], P(('dp', 'expert'))
- query_grad: float32 [2048, 8192], P('dp', 'expert')
- query_direction: float32 [2048, 8192], P('dp', 'expert')
- query_moment: float32 [2048, 8192], P('dp', 'expert')
- query_square: float32 [2048, 8192], P('dp', 'expert')
- project_grad: float32 [8192, 2048], P('expert', 'dp')
- project_direction: float32 [8192, 2048], P('expert', 'dp')
- project_moment: float32 [8192, 2048], P('expert', 'dp')
- project_square: float32 [8192, 2048], P('expert', 'dp')
- gate_up_grad: float32 [2, 2048, 22528], P(None, 'dp', 'expert')
- gate_up_direction: float32 [2, 2048, 22528], P(None, 'dp', 'expert')
- gate_up_moment: float32 [2, 2048, 22528], P(None, 'dp', 'expert')
- gate_up_square: float32 [2, 2048, 22528], P(None, 'dp', 'expert')
- down_grad: float32 [22528, 2048], P('expert', 'dp')
- down_direction: float32 [22528, 2048], P('expert', 'dp')
- down_moment: float32 [22528, 2048], P('expert', 'dp')
- down_square: float32 [22528, 2048], P('expert', 'dp')
- key_value_grad: float32 [2048, 4096], P(('dp', 'expert'))
- key_value_direction: float32 [2048, 4096], P(('dp', 'expert'))
- key_value_moment: float32 [2048, 4096], P(('dp', 'expert'))
- key_value_square: float32 [2048, 4096], P(('dp', 'expert'))
- router_grad: float32 [2048, 8], P(('dp', 'expert'))
- router_direction: float32 [2048, 8], P(('dp', 'expert'))
- router_moment: float32 [2048, 8], P(('dp', 'expert'))
- router_square: float32 [2048, 8], P(('dp', 'expert'))
- gains_grad: float32 [2, 2048], P(None, ('dp', 'expert'))
- gains_direction: float32 [2, 2048], P(None, ('dp', 'expert'))
- gains_moment: float32 [2, 2048], P(None, ('dp', 'expert'))
- gains_square: float32 [2, 2048], P(None, ('dp', 'expert'))
Inputs may be any that keep to these rules, and one draw needn't show every extreme that they name: `attn_routes`: in the rows of one device no expert is named by more than 96 rows; the two entries of a row differ. `mlp_routes`: in the rows of one device no expert is named by more than 96 rows; the two entries of a row differ. `image_mask`: in each sequence of 128 tokens the ones form one run of exactly 32 tokens.
All inputs are finite; a program needn't handle non-finite values.
Results may differ from a plain program's by a relative error of at most 0.022.
Values may be sent and summed in bfloat16 or wider, within the bound.
No kernel may reach another device: no remote copies, remote signals or barrier semaphores. Data moves between devices by JAX's collectives and lax.ppermute only.
A program may use at most 344 MiB of HBM per device.

v0:
```python
import jax
import jax.numpy as jnp
from jax import lax
from jax.sharding import PartitionSpec as P

D = 2048
HEADS = 16
HD = 128
EXPERTS = 4
TOP = 2
STEP = 10
QW = 2048
CAP = 96


NORM_EPS = 1e-05
ADAM_EPS = 1e-08
BETA_FIRST = 0.9
BETA_SECOND = 0.95
ROPE_BASE = 10000.0
MASK_FILL = -1000000000.0
HIGHEST = lax.Precision.HIGHEST


def matmul(left_side, right_side):
    return jnp.dot(left_side, right_side, preferred_element_type=jnp.float32)


def matmul_back(left_side, right_side):
    return lax.dot_general(
        left_side, right_side, (((1,), (1,)), ((), ())), preferred_element_type=jnp.float32
    )


def matmul_rows(left_side, right_side):
    return lax.dot_general(
        left_side, right_side, (((0,), (0,)), ((), ())), preferred_element_type=jnp.float32
    )


def exact_back(left_side, right_side):
    return lax.dot_general(
        left_side,
        right_side,
        (((1,), (1,)), ((), ())),
        precision=HIGHEST,
        preferred_element_type=jnp.float32,
    )


def exact_rows(left_side, right_side):
    return lax.dot_general(
        left_side,
        right_side,
        (((0,), (0,)), ((), ())),
        precision=HIGHEST,
        preferred_element_type=jnp.float32,
    )


def rope_tables(length):
    half_dim = HD // 2
    frequency = ROPE_BASE ** (-(2.0 * jnp.arange(half_dim, dtype=jnp.float32)) / HD)
    angles = jnp.arange(length, dtype=jnp.float32)[:, None] * frequency[None, :]
    return (jnp.cos(angles), jnp.sin(angles))


def rotate(values, cosine_table, sine_table, direction):
    half_dim = values.shape[-1] // 2
    lower_half = values[..., :half_dim]
    upper_half = values[..., half_dim:]
    cos_wide = cosine_table[:, None, :]
    sin_wide = direction * sine_table[:, None, :]
    return jnp.concatenate(
        [
            lower_half * cos_wide - upper_half * sin_wide,
            upper_half * cos_wide + lower_half * sin_wide,
        ],
        axis=-1,
    )


def chosen_gates(logits, routes):
    picked = jnp.take_along_axis(logits, routes, axis=-1)
    return jax.nn.softmax(picked, axis=-1)


def gate_back(gates, grad_gates, hit_table):
    centred = gates * (grad_gates - jnp.sum(gates * grad_gates, axis=-1, keepdims=True))
    return jnp.sum(centred[:, :, None] * hit_table, axis=1)


def norm_back(values, inverse, gain_row, grad_normed):
    scaled = gain_row * grad_normed
    grad_values = inverse * scaled - values * inverse**3 * jnp.mean(
        scaled * values, axis=-1, keepdims=True
    )
    grad_gain = jnp.sum(grad_normed * values * inverse, axis=0)
    return (grad_values, grad_gain)


def slot_tables(routes):
    token_count = routes.shape[0]
    hit_bool = routes[:, :, None] == jnp.arange(EXPERTS, dtype=jnp.int32)[None, None, :]
    per_token = jnp.sum(hit_bool.astype(jnp.int32), axis=1)
    before = jnp.cumsum(per_token, axis=0) - per_token
    slot_index = jnp.sum(jnp.where(hit_bool, before[:, None, :], 0), axis=2)
    flat_index = routes * CAP + slot_index
    chooser = (
        flat_index[:, :, None] == jnp.arange(EXPERTS * CAP, dtype=jnp.int32)[None, None, :]
    ).astype(jnp.bfloat16)
    return (
        flat_index,
        chooser.reshape(token_count, TOP, EXPERTS, CAP),
        hit_bool.astype(jnp.float32),
    )


def dispatch(buffer):
    return lax.all_to_all(buffer, "expert", split_axis=0, concat_axis=0, tiled=True)


def give_back(buffer):
    return lax.all_to_all(buffer, "expert", split_axis=0, concat_axis=0, tiled=True)


def send_rows(chooser, values, halves):
    placed = jnp.einsum(
        "tjec,tjw->ecw", chooser, values, preferred_element_type=jnp.float32
    ).astype(jnp.bfloat16)
    spread = jnp.broadcast_to(placed[:, None], (EXPERTS, halves) + placed.shape[1:])
    return dispatch(spread.reshape((EXPERTS * halves,) + placed.shape[1:]))


def send_heads(chooser, values, halves):
    pieces = values.reshape(values.shape[0], values.shape[1], halves, values.shape[2] // halves)
    placed = jnp.einsum(
        "tjec,tjsw->escw", chooser, pieces, preferred_element_type=jnp.float32
    ).astype(jnp.bfloat16)
    return dispatch(placed.reshape((EXPERTS * halves,) + placed.shape[2:]))


def collect_sum(returned, flat_index, halves):
    merged = jnp.sum(returned.reshape((EXPERTS, halves) + returned.shape[1:]), axis=1)
    return jnp.take(merged.reshape(EXPERTS * CAP, returned.shape[-1]), flat_index, axis=0)


def collect_heads(returned, flat_index, halves):
    part_width = returned.shape[-1]
    arranged = (
        returned.reshape(EXPERTS, halves, CAP, part_width)
        .transpose(0, 2, 1, 3)
        .reshape(EXPERTS * CAP, halves * part_width)
    )
    return jnp.take(arranged, flat_index, axis=0)


def attend_scores(queries, key_rows, allowed):
    scores = jnp.einsum(
        "qjhd,khd->jhqk", queries, key_rows, preferred_element_type=jnp.float32
    ) * HD ** (-0.5)
    return jnp.where(allowed[None, None], scores, MASK_FILL)


def adam_step(moment, square, gradient):
    moment_new = BETA_FIRST * moment + (1.0 - BETA_FIRST) * gradient
    square_new = BETA_SECOND * square + (1.0 - BETA_SECOND) * gradient * gradient
    moment_hat = moment_new / (1.0 - BETA_FIRST**STEP)
    square_hat = square_new / (1.0 - BETA_SECOND**STEP)
    direction = moment_hat / (jnp.sqrt(square_hat) + ADAM_EPS)
    return (direction, moment_new, square_new)


def body(
    tokens,
    teacher,
    attn_routes,
    mlp_routes,
    image_mask,
    valid,
    master_query,
    moment_query,
    square_query,
    master_project,
    moment_project,
    square_project,
    master_gate_up,
    moment_gate_up,
    square_gate_up,
    master_down,
    moment_down,
    square_down,
    master_key_value,
    moment_key_value,
    square_key_value,
    master_router,
    moment_router,
    square_router,
    master_gains,
    moment_gains,
    square_gains,
):
    halves = lax.axis_size("expert") // EXPERTS
    token_count = tokens.shape[0]
    query_low = master_query.astype(jnp.bfloat16)
    project_low = master_project.astype(jnp.bfloat16)
    gate_up_low = master_gate_up.astype(jnp.bfloat16)
    down_low = master_down.astype(jnp.bfloat16)
    weights_query, weights_project, weights_gate_up, weights_down = (
        lax.all_gather(query_low, "dp", axis=0, tiled=True),
        lax.all_gather(project_low, "dp", axis=1, tiled=True),
        lax.all_gather(gate_up_low, "dp", axis=1, tiled=True),
        lax.all_gather(down_low, "dp", axis=1, tiled=True),
    )
    kv_whole, router_whole, gains_whole = (
        lax.all_gather(master_key_value.astype(jnp.bfloat16), ("dp", "expert"), axis=0, tiled=True),
        lax.all_gather(master_router.astype(jnp.bfloat16), ("dp", "expert"), axis=0, tiled=True),
        lax.all_gather(master_gains.astype(jnp.bfloat16), ("dp", "expert"), axis=1, tiled=True),
    )
    gains_f = gains_whole.astype(jnp.float32)
    router_f = router_whole.astype(jnp.float32)
    cosine_table, sine_table = rope_tables(token_count)
    inputs_f = tokens.astype(jnp.float32)
    inverse_one = lax.rsqrt(jnp.mean(inputs_f * inputs_f, axis=-1, keepdims=True) + NORM_EPS)
    normed_one = (inputs_f * inverse_one * gains_f[0]).astype(jnp.bfloat16)
    kv_proj = matmul(normed_one, kv_whole)
    key_rows = rotate(
        kv_proj[:, :QW].reshape(token_count, HEADS, HD), cosine_table, sine_table, 1.0
    ).astype(jnp.bfloat16)
    value_rows = kv_proj[:, QW:].reshape(token_count, HEADS, HD).astype(jnp.bfloat16)
    flat_attn, chooser_attn, hits_attn = slot_tables(attn_routes)
    gates_attn = chosen_gates(matmul(normed_one, router_whole[:, :EXPERTS]), attn_routes)
    sent_normed = send_rows(
        chooser_attn, jnp.broadcast_to(normed_one[:, None, :], (token_count, TOP, D)), halves
    )
    rows_normed = sent_normed.reshape(-1, D)
    query_back = give_back(
        matmul(rows_normed, weights_query).reshape(sent_normed.shape[0], CAP, -1)
    )
    query_pre = collect_heads(query_back, flat_attn, halves)
    queries = (
        rotate(query_pre.reshape(token_count, TOP * HEADS, HD), cosine_table, sine_table, 1.0)
        .astype(jnp.bfloat16)
        .reshape(token_count, TOP, HEADS, HD)
    )
    position = jnp.arange(token_count, dtype=jnp.int32)
    image_on = image_mask > 0
    allowed = (position[:, None] >= position[None, :]) | image_on[:, None] & image_on[None, :]
    scores = attend_scores(queries, key_rows, allowed)
    log_total = jax.nn.logsumexp(scores, axis=-1, keepdims=True)
    prob_low = jnp.exp(scores - log_total).astype(jnp.bfloat16)
    attended = (
        jnp.einsum("jhqk,khd->qjhd", prob_low, value_rows, preferred_element_type=jnp.float32)
        .astype(jnp.bfloat16)
        .reshape(token_count, TOP, QW)
    )
    sent_attended = send_heads(chooser_attn, attended, halves)
    rows_attended = sent_attended.reshape(-1, sent_attended.shape[-1])
    branch_back = give_back(
        matmul(rows_attended, weights_project).reshape(sent_attended.shape[0], CAP, D)
    )
    branch = collect_sum(branch_back, flat_attn, halves)
    hidden = inputs_f + jnp.sum(gates_attn[:, :, None] * branch, axis=1)
    inverse_two = lax.rsqrt(jnp.mean(hidden * hidden, axis=-1, keepdims=True) + NORM_EPS)
    normed_two = (hidden * inverse_two * gains_f[1]).astype(jnp.bfloat16)
    flat_mlp, chooser_mlp, hits_mlp = slot_tables(mlp_routes)
    gates_mlp = chosen_gates(matmul(normed_two, router_whole[:, EXPERTS:]), mlp_routes)
    sent_two = send_rows(
        chooser_mlp, jnp.broadcast_to(normed_two[:, None, :], (token_count, TOP, D)), halves
    )
    rows_two = sent_two.reshape(-1, D)
    gate_val = matmul(rows_two, weights_gate_up[0])
    up_val = matmul(rows_two, weights_gate_up[1])
    active = (jax.nn.silu(gate_val) * up_val).astype(jnp.bfloat16)
    mlp_back = give_back(matmul(active, weights_down).reshape(sent_two.shape[0], CAP, D))
    mlp_branch = collect_sum(mlp_back, flat_mlp, halves)
    outputs = hidden + jnp.sum(gates_mlp[:, :, None] * mlp_branch, axis=1)
    deviation = outputs - teacher.astype(jnp.float32)
    valid_f = valid.astype(jnp.float32)
    total_count, total_error = lax.psum(
        (jnp.sum(valid_f), jnp.sum(valid_f[:, None] * deviation * deviation)), ("dp", "expert")
    )
    loss_value = total_error / total_count
    grad_out = 2.0 * valid_f[:, None] * deviation / total_count
    weights_query, weights_project, weights_gate_up, weights_down = (
        lax.all_gather(query_low, "dp", axis=0, tiled=True),
        lax.all_gather(project_low, "dp", axis=1, tiled=True),
        lax.all_gather(gate_up_low, "dp", axis=1, tiled=True),
        lax.all_gather(down_low, "dp", axis=1, tiled=True),
    )
    grad_branch_mlp = (gates_mlp[:, :, None] * grad_out[:, None, :]).astype(jnp.bfloat16)
    sent_grad_mlp = send_rows(chooser_mlp, grad_branch_mlp, halves)
    rows_grad_mlp = sent_grad_mlp.reshape(-1, D)
    grad_active = matmul_back(rows_grad_mlp, weights_down)
    sigmoid_gate = jax.nn.sigmoid(gate_val)
    grad_gate = (
        grad_active * up_val * sigmoid_gate * (1.0 + gate_val * (1.0 - sigmoid_gate))
    ).astype(jnp.bfloat16)
    grad_up = (grad_active * gate_val * sigmoid_gate).astype(jnp.bfloat16)
    grad_down = matmul_rows(active, rows_grad_mlp)
    grad_gate_up = jnp.stack([matmul_rows(rows_two, grad_gate), matmul_rows(rows_two, grad_up)])
    normed_two_back = give_back(
        (
            matmul_back(grad_gate, weights_gate_up[0]) + matmul_back(grad_up, weights_gate_up[1])
        ).reshape(sent_two.shape[0], CAP, D)
    )
    grad_gates_mlp = jnp.sum(grad_out[:, None, :] * mlp_branch, axis=-1)
    grad_logits_mlp = gate_back(gates_mlp, grad_gates_mlp, hits_mlp)
    grad_normed_two = jnp.sum(collect_sum(normed_two_back, flat_mlp, halves), axis=1) + exact_back(
        grad_logits_mlp, router_f[:, EXPERTS:]
    )
    grad_hidden_norm, grad_gain_two = norm_back(hidden, inverse_two, gains_f[1], grad_normed_two)
    grad_hidden = grad_out + grad_hidden_norm
    grad_router_two = exact_rows(normed_two.astype(jnp.float32), grad_logits_mlp)
    grad_branch_attn = (gates_attn[:, :, None] * grad_hidden[:, None, :]).astype(jnp.bfloat16)
    sent_grad_attn = send_rows(chooser_attn, grad_branch_attn, halves)
    rows_grad_attn = sent_grad_attn.reshape(-1, D)
    grad_project = matmul_rows(rows_attended, rows_grad_attn)
    attended_back = give_back(
        matmul_back(rows_grad_attn, weights_project).reshape(sent_grad_attn.shape[0], CAP, -1)
    )
    grad_attended = (
        collect_heads(attended_back, flat_attn, halves)
        .astype(jnp.bfloat16)
        .reshape(token_count, TOP, HEADS, HD)
    )
    grad_gates_attn = jnp.sum(grad_hidden[:, None, :] * branch, axis=-1)
    grad_logits_attn = gate_back(gates_attn, grad_gates_attn, hits_attn)
    scores_again = attend_scores(queries, key_rows, allowed)
    prob_table = jnp.exp(scores_again - log_total)
    grad_probs = jnp.einsum(
        "qjhd,khd->jhqk", grad_attended, value_rows, preferred_element_type=jnp.float32
    )
    grad_scores = (
        prob_table * (grad_probs - jnp.sum(prob_table * grad_probs, axis=-1, keepdims=True))
    ).astype(jnp.bfloat16)
    score_scale = HD ** (-0.5)
    grad_queries = (
        jnp.einsum("jhqk,khd->qjhd", grad_scores, key_rows, preferred_element_type=jnp.float32)
        * score_scale
    )
    grad_keys = (
        jnp.einsum("jhqk,qjhd->khd", grad_scores, queries, preferred_element_type=jnp.float32)
        * score_scale
    )
    grad_values = jnp.einsum(
        "jhqk,qjhd->khd",
        prob_table.astype(jnp.bfloat16),
        grad_attended,
        preferred_element_type=jnp.float32,
    )
    grad_query_pre = (
        rotate(grad_queries.reshape(token_count, TOP * HEADS, HD), cosine_table, sine_table, -1.0)
        .astype(jnp.bfloat16)
        .reshape(token_count, TOP, QW)
    )
    grad_key_pre = rotate(grad_keys, cosine_table, sine_table, -1.0)
    grad_kv = jnp.concatenate(
        [grad_key_pre.reshape(token_count, QW), grad_values.reshape(token_count, QW)], axis=1
    ).astype(jnp.bfloat16)
    sent_grad_query = send_heads(chooser_attn, grad_query_pre, halves)
    rows_grad_query = sent_grad_query.reshape(-1, sent_grad_query.shape[-1])
    grad_query = matmul_rows(rows_normed, rows_grad_query)
    normed_one_back = give_back(
        matmul_back(rows_grad_query, weights_query).reshape(sent_grad_query.shape[0], CAP, D)
    )
    grad_kv_weight = matmul_rows(normed_one, grad_kv)
    grad_normed_one = (
        jnp.sum(collect_sum(normed_one_back, flat_attn, halves), axis=1)
        + matmul_back(grad_kv, kv_whole)
        + exact_back(grad_logits_attn, router_f[:, :EXPERTS])
    )
    grad_inputs_norm, grad_gain_one = norm_back(inputs_f, inverse_one, gains_f[0], grad_normed_one)
    input_grad = grad_hidden + grad_inputs_norm
    grad_router = jnp.concatenate(
        [exact_rows(normed_one.astype(jnp.float32), grad_logits_attn), grad_router_two], axis=1
    )
    grad_gains = jnp.stack([grad_gain_one, grad_gain_two])
    reduced_query, reduced_project, reduced_gate_up, reduced_down = (
        lax.psum_scatter(
            grad_query.astype(jnp.bfloat16), "dp", scatter_dimension=0, tiled=True
        ).astype(jnp.float32),
        lax.psum_scatter(
            grad_project.astype(jnp.bfloat16), "dp", scatter_dimension=1, tiled=True
        ).astype(jnp.float32),
        lax.psum_scatter(
            grad_gate_up.astype(jnp.bfloat16), "dp", scatter_dimension=1, tiled=True
        ).astype(jnp.float32),
        lax.psum_scatter(
            grad_down.astype(jnp.bfloat16), "dp", scatter_dimension=1, tiled=True
        ).astype(jnp.float32),
    )
    reduced_kv, reduced_router, reduced_gains = (
        lax.psum_scatter(grad_kv_weight, ("dp", "expert"), scatter_dimension=0, tiled=True),
        lax.psum_scatter(grad_router, ("dp", "expert"), scatter_dimension=0, tiled=True),
        lax.psum_scatter(grad_gains, ("dp", "expert"), scatter_dimension=1, tiled=True),
    )
    upd_query = adam_step(moment_query, square_query, reduced_query)
    upd_project = adam_step(moment_project, square_project, reduced_project)
    upd_gate_up = adam_step(moment_gate_up, square_gate_up, reduced_gate_up)
    upd_down = adam_step(moment_down, square_down, reduced_down)
    upd_kv = adam_step(moment_key_value, square_key_value, reduced_kv)
    upd_router = adam_step(moment_router, square_router, reduced_router)
    upd_gains = adam_step(moment_gains, square_gains, reduced_gains)
    return (
        outputs,
        loss_value,
        input_grad,
        reduced_query,
        upd_query[0],
        upd_query[1],
        upd_query[2],
        reduced_project,
        upd_project[0],
        upd_project[1],
        upd_project[2],
        reduced_gate_up,
        upd_gate_up[0],
        upd_gate_up[1],
        upd_gate_up[2],
        reduced_down,
        upd_down[0],
        upd_down[1],
        upd_down[2],
        reduced_kv,
        upd_kv[0],
        upd_kv[1],
        upd_kv[2],
        reduced_router,
        upd_router[0],
        upd_router[1],
        upd_router[2],
        reduced_gains,
        upd_gains[0],
        upd_gains[1],
        upd_gains[2],
    )


def solution(mesh):
    placed = (
        P(("dp", "expert"), None),
        P(("dp", "expert"), None),
        P(("dp", "expert"), None),
        P(("dp", "expert"), None),
        P(("dp", "expert")),
        P(("dp", "expert")),
        P("dp", "expert"),
        P("dp", "expert"),
        P("dp", "expert"),
        P("expert", "dp"),
        P("expert", "dp"),
        P("expert", "dp"),
        P(None, "dp", "expert"),
        P(None, "dp", "expert"),
        P(None, "dp", "expert"),
        P("expert", "dp"),
        P("expert", "dp"),
        P("expert", "dp"),
        P(("dp", "expert"), None),
        P(("dp", "expert"), None),
        P(("dp", "expert"), None),
        P(("dp", "expert"), None),
        P(("dp", "expert"), None),
        P(("dp", "expert"), None),
        P(None, ("dp", "expert")),
        P(None, ("dp", "expert")),
        P(None, ("dp", "expert")),
    )
    return jax.shard_map(
        body,
        mesh=mesh,
        in_specs=placed,
        out_specs=(
            P(("dp", "expert"), None),
            P(),
            P(("dp", "expert"), None),
            P("dp", "expert"),
            P("dp", "expert"),
            P("dp", "expert"),
            P("dp", "expert"),
            P("expert", "dp"),
            P("expert", "dp"),
            P("expert", "dp"),
            P("expert", "dp"),
            P(None, "dp", "expert"),
            P(None, "dp", "expert"),
            P(None, "dp", "expert"),
            P(None, "dp", "expert"),
            P("expert", "dp"),
            P("expert", "dp"),
            P("expert", "dp"),
            P("expert", "dp"),
            P(("dp", "expert"), None),
            P(("dp", "expert"), None),
            P(("dp", "expert"), None),
            P(("dp", "expert"), None),
            P(("dp", "expert"), None),
            P(("dp", "expert"), None),
            P(("dp", "expert"), None),
            P(("dp", "expert"), None),
            P(None, ("dp", "expert")),
            P(None, ("dp", "expert")),
            P(None, ("dp", "expert")),
            P(None, ("dp", "expert")),
        ),
        check_vma=False,
    )
```

profile of v0, /device:TPU:0, one launch (start us, length us, event | category | flops | bytes accessed | tf_op | source)
XLA Modules:
  0.0 2739.6 jit_solution(9584839311294527922)
XLA Ops:
  13.0 7.4 convert_element_type.169
  26.2 69.2 %all-gather = bf16[32,64,2]{1,2,0:T(2,128)(2,1)S(1)} all-gather(bf16[1,64,2]{1,2,0:T(2,128)(2,1)S(1)} %convert_bitcast_fusion.3), channel_id=1, replica_groups=mesh['dp'=8,'expert'=4] {'dp','expert'}, dimensions={0}, use_global_device_ids=true | all-gather | bytes 8448 | tf_op jit(solution)/shard_map/all_gather | solution.py:218
  98.7 57.8 %all_to_all.60 = bf16[4,96,2048]{2,1,0:T(8,128)(2,1)S(1)} all-to-all(bf16[4,96,2048]{2,1,0:T(8,128)(2,1)S(1)} %bitcast_convert_fusion.7), channel_id=1, replica_groups=mesh['dp'=8,'expert'=4] {'expert'}, dimensions={0} | all-to-all | bytes 3145728 | tf_op jit(solution)/shard_map/all_to_all | solution.py:120
  156.6 9.1 fusion.11
  172.3 98.8 %all-to-all-done.1 = f32[4,96,2048]{2,1,0:T(8,128)S(1)} async-done(((f32[4,96,2048]{2,1,0:T(8,128)}), f32[4,96,2048]{2,1,0:T(8,128)S(1)}, u32[]{:S(2)}, u32[]{:S(2)}) %all-to-all-start.1) | async-done | bytes 3145760 | tf_op jit(solution)/shard_map/all_to_all | solution.py:124
  282.7 9.5 fusion.106
  302.5 12.5 all-gather.12.cloned.1.call-done
  315.0 24.5 all-to-all-done.2
  339.5 9.0 fusion.7
  352.5 129.0 %all-gather.1 = bf16[32,64,8]{1,2,0:T(8,128)(2,1)S(1)} all-gather(bf16[1,64,8]{1,2,0:T(8,128)(2,1)S(1)} %convert_bitcast_fusion.2), channel_id=1, replica_groups=mesh['dp'=8,'expert'=4] {'dp','expert'}, dimensions={0}, use_global_device_ids=true | all-gather | bytes 33792 | tf_op jit(solution)/shard_map/all_gather | solution.py:217
  496.4 34.9 %all_to_all.61 = bf16[4,96,2048]{2,1,0:T(8,128)(2,1)S(1)} all-to-all(bf16[4,96,2048]{2,1,0:T(8,128)(2,1)S(1)} %bitcast_convert_fusion.5), channel_id=1, replica_groups=mesh['dp'=8,'expert'=4] {'expert'}, dimensions={0} | all-to-all | bytes 3145728 | tf_op jit(solution)/shard_map/all_to_all | solution.py:120
  531.8 15.6 fusion.1
  547.5 18.3 multiply_convert_fusion.2
  565.8 89.4 %all-gather.16.cloned.1.call-done = bf16[5632,2048]{1,0:T(8,128)(2,1)} async-done(((bf16[5632,256]{1,0:T(8,128)(2,1)}), bf16[5632,2048]{1,0:T(8,128)(2,1)}) %all-gather.16.cloned.1.call-update) | async-done | bytes 23068688 | tf_op jit(solution)/shard_map/all_gather | solution.py:213
  655.1 15.9 fusion.107
  671.0 5.2 all-to-all-start.5
  681.4 66.0 %all-to-all-done.5 = f32[4,96,2048]{2,1,0:T(8,128)S(1)} async-done(((f32[4,96,2048]{2,1,0:T(8,128)}), f32[4,96,2048]{2,1,0:T(8,128)S(1)}, u32[]{:S(2)}, u32[]{:S(2)}) %all-to-all-start.5) | async-done | bytes 3145760 | tf_op jit(solution)/shard_map/all_to_all | solution.py:124
  755.7 37.1 %all-reduce = (f32[]{:T(128)}, f32[]{:T(128)}) all-reduce(f32[]{:T(128)} %get-tuple-element.64, f32[]{:T(128)} %get-tuple-element.100), channel_id=1, replica_groups=mesh['dp'=8,'expert'=4] {'dp','expert'}, use_global_device_ids=true, to_apply=%region_17.20 | all-reduce | flops 2 | bytes 16 | tf_op jit(solution)/shard_map/psum | solution.py:280
  795.4 40.6 %all_to_all.62 = bf16[4,96,2048]{2,1,0:T(8,128)(2,1)S(1)} all-to-all(bf16[4,96,2048]{2,1,0:T(8,128)(2,1)S(1)} %bitcast_convert_fusion.4), channel_id=1, replica_groups=mesh['dp'=8,'expert'=4] {'expert'}, dimensions={0} | all-to-all | bytes 3145728 | tf_op jit(solution)/shard_map/all_to_all | solution.py:120
  836.0 27.8 %multiply_convert_fusion = (bf16[384,5632]{1,0:T(8,128)(2,1)}, bf16[384,5632]{1,0:T(8,128)(2,1)}) fusion(f32[384,5632]{1,0:T(8,128)} %fusion.1, f32[384,5632]{1,0:T(8,128)} %get-tuple-element.104, bf16[384,2048]{1,0:T(8,128)(2,1)S(1)} %bitcast.236, bf16[5632,2048]{1,0:T(8,128)(2,1)} %all-gather.16.cloned.1.call-done), kind=kOutput, calls=%fused_computation.24 | convolution fusion | flops 8886484992 | bytes 50593792 | tf_op jit(solution)/shard_map/dot_general | solution.py:30
  863.8 13.9 fusion
  877.7 16.0 fusion.14
  901.0 66.3 %all-to-all-done.7 = f32[4,96,2048]{2,1,0:T(8,128)S(1)} async-done(((f32[4,96,2048]{2,1,0:T(8,128)}), f32[4,96,2048]{2,1,0:T(8,128)S(1)}, u32[]{:S(2)}, u32[]{:S(2)}) %all-to-all-start.7) | async-done | bytes 3145760 | tf_op jit(solution)/shard_map/all_to_all | solution.py:124
  980.3 39.4 %all_to_all.63 = bf16[4,96,2048]{2,1,0:T(8,128)(2,1)S(1)} all-to-all(bf16[4,96,2048]{2,1,0:T(8,128)(2,1)S(1)} %bitcast_convert_fusion.3), channel_id=1, replica_groups=mesh['dp'=8,'expert'=4] {'expert'}, dimensions={0} | all-to-all | bytes 3145728 | tf_op jit(solution)/shard_map/all_to_all | solution.py:120
  1019.6 7.4 fusion.5
  1027.1 38.9 %all_to_all.64 = bf16[4,96,2048]{2,1,0:T(8,128)(2,1)S(1)} all-to-all(bf16[4,96,2048]{2,1,0:T(8,128)(2,1)S(1)} %fusion.5), channel_id=1, replica_groups=mesh['dp'=8,'expert'=4] {'expert'}, dimensions={0} | all-to-all | bytes 3145728 | tf_op jit(solution)/shard_map/all_to_all | solution.py:124
  1090.9 39.2 %all_to_all.65 = bf16[4,96,2048]{2,1,0:T(8,128)(2,1)S(1)} all-to-all(bf16[4,96,2048]{2,1,0:T(8,128)(2,1)S(1)} %fusion.16), channel_id=1, replica_groups=mesh['dp'=8,'expert'=4] {'expert'}, dimensions={0} | all-to-all | bytes 3145728 | tf_op jit(solution)/shard_map/all_to_all | solution.py:120
  1131.3 8.5 fusion.9
  1159.6 60.3 %all-to-all-done.11 = f32[4,96,2048]{2,1,0:T(8,128)S(1)} async-done(((f32[4,96,2048]{2,1,0:T(8,128)}), f32[4,96,2048]{2,1,0:T(8,128)S(1)}, u32[]{:S(2)}, u32[]{:S(2)}) %all-to-all-start.11) | async-done | bytes 3145760 | tf_op jit(solution)/shard_map/all_to_all | solution.py:124
  1225.2 5.3 select_reduce_fusion
  1230.5 11.8 convolution_add_fusion.2
  1246.1 9.9 bitcast_convert_fusion
  1256.0 9.9 bitcast_convert_fusion.1
  1266.0 18.8 convolution_convert_fusion
  1285.0 18.8 convert_bitcast_fusion
  1303.7 18.9 convert_bitcast_fusion.1
  1322.6 31.4 %pad_maximum_fusion = bf16[2,2048,5632]{2,1,0:T(8,128)(2,1)} fusion(bf16[1,2048,5632]{2,1,0:T(8,128)(2,1)} %convert_bitcast_fusion, bf16[1,2048,5632]{2,1,0:T(8,128)(2,1)} %convert_bitcast_fusion.1), kind=kLoop, calls=%fused_computation.8 | loop fusion | flops 23068672 | bytes 92274688 | tf_op jit(solution)/shard_map/stack | solution.py:301
  1355.1 13.7 fusion.53
  1373.3 75.0 %reduce-scatter.24.cloned.1.call-done = f32[64,2]{1,0:T(8,128)} async-done(((f32[2048,2]{1,0:T(8,128)}), f32[64,2]{1,0:T(8,128)}) %reduce-scatter.24.cloned.1.call-update) | async-done | bytes 528
  1449.6 70.5 %reduce-scatter.14.cloned.1.call-done = bf16[2048,256]{1,0:T(8,128)(2,1)} async-done(((bf16[2048,2048]{1,0:T(8,128)(2,1)}), bf16[2048,256]{1,0:T(8,128)(2,1)}) %reduce-scatter.14.cloned.1.call-update) | async-done | bytes 1048592 | tf_op jit(solution)/shard_map/reduce_scatter | solution.py:383
  1520.1 6.3 add_divide_fusion.3
  1526.4 69.5 %reduce-scatter.12.cloned.1.call-done = bf16[256,2048]{1,0:T(8,128)(2,1)} async-done(((bf16[2048,2048]{1,0:T(8,128)(2,1)}), bf16[256,2048]{1,0:T(8,128)(2,1)}) %reduce-scatter.12.cloned.1.call-update) | async-done | bytes 1048592 | tf_op jit(solution)/shard_map/reduce_scatter | solution.py:380
  1595.9 5.8 add_divide_fusion.4
  1601.7 143.6 %reduce-scatter.18.cloned.1.call-done = bf16[5632,256]{1,0:T(8,128)(2,1)} async-done(((bf16[5632,2048]{1,0:T(8,128)(2,1)}), bf16[5632,256]{1,0:T(8,128)(2,1)}) %reduce-scatter.18.cloned.1.call-update) | async-done | bytes 2883600 | tf_op jit(solution)/shard_map/reduce_scatter | solution.py:389
  1745.3 13.6 add_divide_fusion.2
  1759.0 254.3 %reduce-scatter.16.cloned.1.call-done = bf16[2,256,5632]{2,1,0:T(8,128)(2,1)} async-done(((bf16[2,2048,5632]{2,1,0:T(8,128)(2,1)}), bf16[2,256,5632]{2,1,0:T(8,128)(2,1)}) %reduce-scatter.16.cloned.1.call-update) | async-done | bytes 5767184 | tf_op jit(solution)/shard_map/reduce_scatter | solution.py:386
  2013.3 24.6 add_divide_fusion
  2037.9 690.2 %reduce-scatter.20.cloned.1.call-done = f32[64,4096]{1,0:T(8,128)} async-done(((f32[2048,4096]{1,0:T(8,128)}), f32[64,4096]{1,0:T(8,128)}) %reduce-scatter.20.cloned.1.call-update) | async-done | bytes 1048592 | tf_op jit(solution)/shard_map/reduce_scatter | solution.py:394
  (370 shorter events, 161.9 us)
Async XLA Ops:
  7.2 149.3 %all-gather.10.cloned.1.call-start = ((), (), s32[]{:S(2)}) async-start(), calls=%async_computation.20 | async-start | bytes 9437184 | tf_op jit(solution)/shard_map/all_gather | solution.py:210
  10.1 272.6 %all-gather.8.cloned.1.call-start = ((), (), s32[]{:S(2)}) async-start(), calls=%async_computation.19 | async-start | bytes 17301504 | tf_op jit(solution)/shard_map/all_gather | solution.py:216
  11.0 304.0 %all-gather.12.cloned.1.call-start = ((), (), s32[]{:S(2)}) async-start(), calls=%async_computation.21 | async-start | bytes 9437184 | tf_op jit(solution)/shard_map/all_gather | solution.py:211
  12.9 518.9 %all-gather.14.cloned.1.call-start = ((), (), s32[]{:S(2)}) async-start(), calls=%async_computation.22 | async-start | bytes 51904512 | tf_op jit(solution)/shard_map/all_gather | solution.py:212
  20.4 634.7 %all-gather.16.cloned.1.call-start = ((), (), s32[]{:S(2)}) async-start(), calls=%async_computation.23 | async-start | bytes 25952256 | tf_op jit(solution)/shard_map/all_gather | solution.py:213
  25.5 70.0 %copy-start.62 = (s32[128,2]{0,1:T(2,128)S(1)}, s32[128,2]{0,1:T(2,128)}, u32[]{:S(2)}) copy-start(s32[128,2]{0,1:T(2,128)} %param.33) | copy-start | bytes 3076
  25.5 70.4 %copy-start.17 = (bf16[128,2048]{1,0:T(8,128)(2,1)S(1)}, bf16[128,2048]{1,0:T(8,128)(2,1)}, u32[]{:S(2)}) copy-start(bf16[128,2048]{1,0:T(8,128)(2,1)} %param.31) | copy-start | bytes 1572868
  96.6 200.3 %copy-start.66 = (s32[128,2]{0,1:T(2,128)}, s32[128,2]{0,1:T(2,128)S(1)}, u32[]{:S(2)}) copy-start(s32[128,2]{0,1:T(2,128)S(1)} %get-tuple-element.75) | copy-start | bytes 3076
  96.7 395.4 %copy-start.69 = (pred[128,2]{0,1:T(4,128)(4,1)}, pred[128,2]{0,1:T(4,128)(4,1)S(1)}, u32[]{:S(2)}) copy-start(pred[128,2]{0,1:T(4,128)(4,1)S(1)} %get-tuple-element.74) | copy-start | bytes 772
  96.7 397.7 %copy-start.59 = (f32[1,2048]{1,0:T(1,128)}, f32[1,2048]{1,0:T(1,128)S(1)}, u32[]{:S(2)}) copy-start(f32[1,2048]{1,0:T(1,128)S(1)} %get-tuple-element.90) | copy-start | bytes 24580
  156.6 9.1 copy-start.39
  165.6 105.4 %all-to-all-start.1 = ((f32[4,96,2048]{2,1,0:T(8,128)}), f32[4,96,2048]{2,1,0:T(8,128)S(1)}, u32[]{:S(2)}, u32[]{:S(2)}) async-start(f32[4,96,2048]{2,1,0:T(8,128)} %fusion.11), calls=%async_computation.1 | async-start | bytes 6291456 | tf_op jit(solution)/shard_map/all_to_all | solution.py:124
  170.8 105.4 %copy-start.55 = (pred[128,2]{1,0:T(8,128)(4,1)}, pred[128,2]{1,0:T(8,128)(4,1)S(1)}, u32[]{:S(2)}) copy-start(pred[128,2]{1,0:T(8,128)(4,1)S(1)} %copy.241) | copy-start | bytes 772
  171.9 109.4 %copy-start.50 = (f32[128,64]{0,1:T(8,128)}, f32[128,64]{0,1:T(8,128)S(1)}, u32[]{:S(2)}) copy-start(f32[128,64]{0,1:T(8,128)S(1)} %get-tuple-element.96) | copy-start | bytes 98308
  172.0 121.0 %copy-start.48 = (f32[128,64]{1,0:T(8,128)}, f32[128,64]{1,0:T(8,128)S(1)}, u32[]{:S(2)}) copy-start(f32[128,64]{1,0:T(8,128)S(1)} %copy.238) | copy-start | bytes 98308
  172.2 314.7 %copy-start.11 = (s32[1024]{0:T(1024)}, s32[1024]{0:T(1024)S(1)}, u32[]{:S(2)}) copy-start(s32[1024]{0:T(1024)S(1)} %pad_clamp_fusion.1) | copy-start | bytes 12292
  282.1 11.6 copy-start.21
  282.6 11.1 copy-start.22
  298.7 40.8 %all-to-all-start.2 = ((bf16[4,96,2048]{2,1,0:T(8,128)(2,1)}), bf16[4,96,2048]{2,1,0:T(8,128)(2,1)S(1)}, u32[]{:S(2)}, u32[]{:S(2)}) async-start(bf16[4,96,2048]{2,1,0:T(8,128)(2,1)} %fusion.15), calls=%async_computation.2 | async-start | bytes 3145728 | tf_op jit(solution)/shard_map/all_to_all | solution.py:120
  339.5 9.0 copy-start.40
  348.6 138.3 %all-to-all-start.3 = ((f32[4,96,2048]{2,1,0:T(8,128)}), f32[4,96,2048]{2,1,0:T(8,128)S(1)}, u32[]{:S(2)}, u32[]{:S(2)}) async-start(f32[4,96,2048]{2,1,0:T(8,128)} %fusion.7), calls=%async_computation.3 | async-start | bytes 6291456 | tf_op jit(solution)/shard_map/all_to_all | solution.py:124
  494.4 36.9 %copy-start.77 = (f32[128]{0:T(128)}, f32[128]{0:T(128)S(1)}, u32[]{:S(2)}) copy-start(f32[128]{0:T(128)S(1)} %get-tuple-element.98) | copy-start | bytes 1540
  531.3 16.2 copy-start.41
  671.0 76.3 %all-to-all-start.5 = ((f32[4,96,2048]{2,1,0:T(8,128)}), f32[4,96,2048]{2,1,0:T(8,128)S(1)}, u32[]{:S(2)}, u32[]{:S(2)}) async-start(f32[4,96,2048]{2,1,0:T(8,128)} %bitcast.228), calls=%async_computation.5 | async-start | bytes 6291456 | tf_op jit(solution)/shard_map/all_to_all | solution.py:124
  755.7 39.7 %copy-start.35 = (f32[128,2048]{1,0:T(8,128)}, f32[128,2048]{1,0:T(8,128)S(1)}, u32[]{:S(2)}) copy-start(f32[128,2048]{1,0:T(8,128)S(1)} %get-tuple-element.65) | copy-start | bytes 3145732
  794.7 41.3 %copy-start.15 = (f32[128,2048]{1,0:T(8,128)}, f32[128,2048]{1,0:T(8,128)S(1)}, u32[]{:S(2)}) copy-start(f32[128,2048]{1,0:T(8,128)S(1)} %multiply_divide_fusion) | copy-start | bytes 3145732
  836.0 27.8 %copy-start.42 = (bf16[4,96,2048]{2,1,0:T(8,128)(2,1)}, bf16[4,96,2048]{2,1,0:T(8,128)(2,1)S(1)}, u32[]{:S(2)}) copy-start(bf16[4,96,2048]{2,1,0:T(8,128)(2,1)S(1)} %all_to_all.62) | copy-start | bytes 4718596
  893.7 73.6 %all-to-all-start.7 = ((f32[4,96,2048]{2,1,0:T(8,128)}), f32[4,96,2048]{2,1,0:T(8,128)S(1)}, u32[]{:S(2)}, u32[]{:S(2)}) async-start(f32[4,96,2048]{2,1,0:T(8,128)} %bitcast.229), calls=%async_computation.7 | async-start | bytes 6291456 | tf_op jit(solution)/shard_map/all_to_all | solution.py:124
  1019.6 7.4 copy-start.43
  1027.1 39.0 %copy-start.12 = (s32[1024]{0:T(1024)S(1)}, s32[1024]{0:T(1024)}, u32[]{:S(2)}) copy-start(s32[1024]{0:T(1024)} %copy-done.11) | copy-start | bytes 12292
  1139.7 80.1 %all-to-all-start.11 = ((f32[4,96,2048]{2,1,0:T(8,128)}), f32[4,96,2048]{2,1,0:T(8,128)S(1)}, u32[]{:S(2)}, u32[]{:S(2)}) async-start(f32[4,96,2048]{2,1,0:T(8,128)} %fusion.9), calls=%async_computation.11 | async-start | bytes 6291456 | tf_op jit(solution)/shard_map/all_to_all | solution.py:124
  1143.5 226.9 %reduce-scatter.22.cloned.1.call-start = ((), (), s32[]{:S(2)}) async-start(), calls=%async_computation.29 | async-start | bytes 1081344
  1150.0 298.2 %reduce-scatter.24.cloned.1.call-start = ((), (), s32[]{:S(2)}) async-start(), calls=%async_computation.30 | async-start | bytes 1081344
  1230.5 11.8 copy-start.19
  1230.5 11.8 copy-start.58
  1230.5 11.9 copy-start.80
  1245.6 274.5 %reduce-scatter.14.cloned.1.call-start = ((), (), s32[]{:S(2)}) async-start(), calls=%async_computation.25 | async-start | bytes 9437184 | tf_op jit(solution)/shard_map/reduce_scatter | solution.py:383
  1256.0 339.9 %reduce-scatter.12.cloned.1.call-start = ((), (), s32[]{:S(2)}) async-start(), calls=%async_computation.24 | async-start | bytes 9437184 | tf_op jit(solution)/shard_map/reduce_scatter | solution.py:380
  1265.9 479.4 %reduce-scatter.18.cloned.1.call-start = ((), (), s32[]{:S(2)}) async-start(), calls=%async_computation.27 | async-start | bytes 25952256 | tf_op jit(solution)/shard_map/reduce_scatter | solution.py:389
  1284.8 728.5 %reduce-scatter.16.cloned.1.call-start = ((), (), s32[]{:S(2)}) async-start(), calls=%async_computation.26 | async-start | bytes 51904512 | tf_op jit(solution)/shard_map/reduce_scatter | solution.py:386
  1354.1 1373.9 %reduce-scatter.20.cloned.1.call-start = ((), (), s32[]{:S(2)}) async-start(), calls=%async_computation.28 | async-start | bytes 34603008 | tf_op jit(solution)/shard_map/reduce_scatter | solution.py:394
  1368.8 80.2 %copy-start.85 = (f32[2,64]{1,0:T(2,128)S(1)}, f32[2,64]{1,0:T(2,128)}, u32[]{:S(2)}) copy-start(f32[2,64]{1,0:T(2,128)} %param.56) | copy-start | bytes 1540
  1368.8 80.2 %copy-start.86 = (f32[2,64]{1,0:T(2,128)S(1)}, f32[2,64]{1,0:T(2,128)}, u32[]{:S(2)}) copy-start(f32[2,64]{1,0:T(2,128)} %param.57) | copy-start | bytes 1540
  1371.2 155.2 %copy-start.68 = (f32[64,8]{0,1:T(8,128)}, f32[64,8]{0,1:T(8,128)S(1)}, u32[]{:S(2)}) copy-start(f32[64,8]{0,1:T(8,128)S(1)} %copy.310) | copy-start | bytes 6148
  1449.0 77.4 %copy-start.82 = (f32[2,64]{1,0:T(2,128)}, f32[2,64]{1,0:T(2,128)S(1)}, u32[]{:S(2)}) copy-start(f32[2,64]{1,0:T(2,128)S(1)} %copy.312) | copy-start | bytes 1540
  1449.6 146.2 %copy-start.38 = (f32[256,2048]{1,0:T(8,128)S(1)}, f32[256,2048]{1,0:T(8,128)}, u32[]{:S(2)}) copy-start(f32[256,2048]{1,0:T(8,128)} %param.38) | copy-start | bytes 6291460
  1758.9 969.1 %copy-start.46 = (f32[64,4096]{1,0:T(8,128)S(1)}, f32[64,4096]{1,0:T(8,128)}, u32[]{:S(2)}) copy-start(f32[64,4096]{1,0:T(8,128)} %param.50) | copy-start | bytes 3145732
  1758.9 969.1 %copy-start.47 = (f32[64,4096]{1,0:T(8,128)S(1)}, f32[64,4096]{1,0:T(8,128)}, u32[]{:S(2)}) copy-start(f32[64,4096]{1,0:T(8,128)} %param.51) | copy-start | bytes 3145732
  (62 other events, 166.5 us)
Sparse Core Ops, SparseCore 0:
  10.5 57.1 all-gather.9
  71.2 166.9 all-gather.7
  240.7 74.2 all-gather.11
  317.3 214.4 all-gather.13
  534.1 120.9 all-gather.15
  1150.2 160.8 reduce-scatter.21
  1314.0 134.2 reduce-scatter.23
  1452.2 67.8 reduce-scatter.13
  1524.6 71.2 reduce-scatter.11
  1599.3 145.9 reduce-scatter.17
  1748.9 264.3 reduce-scatter.15
  2016.1 711.8 reduce-scatter.19
where the time goes:
time: 2750 us; the launch traced here: 2740 us
  waiting for transfers between devices  1720 us (63%)
  blocking collectives  486 us (18%)
  matrix products  275 us (10%)
  other arithmetic  140 us (5%)
  local copies, waits for them, and re-layouts  71.4 us (3%)
    reduce_scatter x1, waiting for transfers between devices, body(): lax.psum_scatter(grad_kv_weight, ('dp', 'expert'), scatter_dimension=0, t...  690 us
    all_to_all x5, waiting for transfers between devices, give_back(): lax.all_to_all(buffer, 'expert', split_axis=0, concat_axis=0, tiled=True)  291 us
    reduce_scatter x1, waiting for transfers between devices, body(): lax.psum_scatter(grad_gate_up.astype(jnp.bfloat16), 'dp', scatter_dimensi...  254 us
    all_to_all x5, blocking collectives, dispatch(): lax.all_to_all(buffer, 'expert', split_axis=0, concat_axis=0, tiled=True)  212 us
    reduce_scatter x1, waiting for transfers between devices, body(): lax.psum_scatter(grad_down.astype(jnp.bfloat16), 'dp', scatter_dimension=...  144 us
    all_gather x1, blocking collectives, body(): lax.all_gather(master_router.astype(jnp.bfloat16), ('dp', 'expert'), axis...  129 us
    dot_general x6, matrix products, matmul_rows(): lax.dot_general(left_side, right_side, (((0,), (0,)), ((), ())), preferre...  89.8 us
    all_gather x1, waiting for transfers between devices, body(): lax.all_gather(down_low, 'dp', axis=1, tiled=True)  89.4 us
  transfers between devices with their start and end apart: 18, of which 14 were waited for; matrix products, arithmetic and copies ran while one was open for 12% of the time, Pallas kernels for 0%

commit v1 on v0

v1 whole, which is shorter than its diff:
```python
import jax
import jax.numpy as jnp
from jax import lax
from jax.sharding import PartitionSpec as P

D = 2048
HD = 128
EXPERTS = 4
TOP = 2
STEP = 10
QW = 2048
CAP = 96
LANES = 128

NORM_EPS = 1e-05
ADAM_EPS = 1e-08
BETA_FIRST = 0.9
BETA_SECOND = 0.95
ROPE_BASE = 10000.0
MASK_FILL = -1000000000.0
SCALE = HD ** (-0.5)
HIGHEST = lax.Precision.HIGHEST
F32 = jnp.float32
BF16 = jnp.bfloat16


def matmul(left_side, right_side):
    return jnp.dot(left_side, right_side, preferred_element_type=F32)


def matmul_back(left_side, right_side):
    return lax.dot_general(
        left_side, right_side, (((1,), (1,)), ((), ())), preferred_element_type=F32
    )


def matmul_rows(left_side, right_side):
    return lax.dot_general(
        left_side, right_side, (((0,), (0,)), ((), ())), preferred_element_type=F32
    )


def exact_back(left_side, right_side):
    return lax.dot_general(
        left_side,
        right_side,
        (((1,), (1,)), ((), ())),
        precision=HIGHEST,
        preferred_element_type=F32,
    )


def exact_rows(left_side, right_side):
    return lax.dot_general(
        left_side,
        right_side,
        (((0,), (0,)), ((), ())),
        precision=HIGHEST,
        preferred_element_type=F32,
    )


def rope_tables(length):
    half_dim = HD // 2
    frequency = ROPE_BASE ** (-(2.0 * jnp.arange(half_dim, dtype=F32)) / HD)
    angles = jnp.arange(length, dtype=F32)[:, None] * frequency[None, :]
    cosine, sine = jnp.cos(angles), jnp.sin(angles)
    return (
        jnp.concatenate([cosine, cosine], axis=1),
        jnp.concatenate([-sine, sine], axis=1),
    )


def swap_perm(count, bits):
    return [(place, place ^ bits) for place in range(count)]


def core_swap(value):
    return lax.ppermute(value, "dp", swap_perm(lax.axis_size("dp"), 1))


def over_expert(value, bits):
    if bits == 0:
        return value
    return lax.ppermute(value, "expert", swap_perm(lax.axis_size("expert"), bits))


def chip_groups():
    count = lax.axis_size("dp")
    return [[2 * place + core for place in range(count // 2)] for core in range(2)]


def gather_chips(block):
    return lax.all_gather(block, "dp", axis=0, tiled=True, axis_index_groups=chip_groups())


def scatter_chips(partial):
    return lax.psum_scatter(
        partial, "dp", scatter_dimension=0, tiled=True, axis_index_groups=chip_groups()
    )


def in_core_order(core, mine, other, axis):
    return jnp.where(
        core == 0,
        jnp.concatenate([mine, other], axis=axis),
        jnp.concatenate([other, mine], axis=axis),
    )


def stack_rows(core, mine, got):
    both = jnp.concatenate([mine, mine], axis=0)
    return lax.dynamic_update_slice_in_dim(both, got, (1 - core) * mine.shape[0], 0)


def halves_of(core, whole):
    width = whole.shape[-1] // 2
    low, high = whole[..., :width], whole[..., width:]
    return (jnp.where(core == 0, low, high), jnp.where(core == 0, high, low))


def exchange_rows(core, summed):
    rows = summed.shape[0] // 2
    low, high = summed[:rows], summed[rows:]
    mine = jnp.where(core == 0, low, high)
    return (mine, core_swap(jnp.where(core == 0, high, low)))


def slots_before(hits):
    count = hits.shape[-2]
    place = jnp.arange(count, dtype=jnp.int32)
    earlier = (place[:, None] > place[None, :]).astype(BF16)
    return jnp.einsum(
        "ts,...sn->...tn", earlier, hits.astype(BF16), preferred_element_type=F32
    ).astype(jnp.int32)


def route_tables(routes, names):
    hit = routes[:, :, None] == names[None, None, :]
    named = jnp.any(hit, axis=1)
    slot = slots_before(named)
    at_slot = slot[:, :, None] == jnp.arange(CAP, dtype=jnp.int32)[None, None, :]
    pick = (named[:, :, None] & at_slot).astype(BF16).transpose(1, 2, 0)
    back = (hit[:, :, :, None] & at_slot[:, None]).astype(BF16)
    back = back.transpose(1, 0, 2, 3).reshape(TOP, routes.shape[0], -1)
    return (pick, back, hit.astype(F32))


def chosen_gates(logits, routes):
    hit = routes[:, :, None] == jnp.arange(EXPERTS, dtype=jnp.int32)[None, None, :]
    picked = jnp.sum(jnp.where(hit, logits[:, None, :], 0.0), axis=2)
    return jax.nn.softmax(picked, axis=-1)


def gate_back(gates, grad_gates, routes):
    hit = routes[:, :, None] == jnp.arange(EXPERTS, dtype=jnp.int32)[None, None, :]
    centred = gates * (grad_gates - jnp.sum(gates * grad_gates, axis=-1, keepdims=True))
    return jnp.sum(centred[:, :, None] * hit.astype(F32), axis=1)


def norm_back(values, inverse, gain_row, grad_normed):
    scaled = gain_row * grad_normed
    grad_values = inverse * scaled - values * inverse**3 * jnp.mean(
        scaled * values, axis=-1, keepdims=True
    )
    grad_gain = jnp.sum(grad_normed * values * inverse, axis=0)
    return (grad_values, grad_gain)


def send_rows(blocks):
    got = jnp.concatenate([over_expert(block, bits) for bits, block in enumerate(blocks)])
    return jnp.concatenate([got, core_swap(got)])


def return_rows(partial, partners):
    count = partial.shape[0] // 2
    got = core_swap(partial[count:].astype(BF16))
    summed = (partial[:count] + got.astype(F32)).astype(BF16)
    summed = summed.reshape((partners, count // partners) + summed.shape[1:])
    return [over_expert(summed[bits], bits) for bits in range(partners)]


def rotate(value, cosine, sine):
    half_dim = HD // 2
    swapped = jnp.concatenate([value[..., half_dim:], value[..., :half_dim]], axis=-1)
    return value * cosine + swapped * sine


def by_heads(rows, sequences):
    return rows.reshape(sequences, -1, rows.shape[1] // HD, HD).transpose(0, 2, 1, 3)


def from_heads(blocks):
    sequences, heads, tokens, _ = blocks.shape
    return blocks.transpose(0, 2, 1, 3).reshape(sequences * tokens, heads * HD)


def heads_dot(left_side, right_side, left_axis, right_axis):
    return lax.dot_general(
        left_side,
        right_side,
        (((left_axis,), (right_axis,)), ((0, 1), (0, 1))),
        preferred_element_type=F32,
    )


def xor_blocks(value, axis, bits):
    count, step = value.shape[axis], 1
    while step < count:
        if bits & step:
            split = value.shape[:axis] + (count // (2 * step), 2, step) + value.shape[axis + 1 :]
            value = jnp.flip(value.reshape(split), axis + 1).reshape(value.shape)
        step *= 2
    return value


def partner_columns(expert, rows):
    width = rows.shape[1] // EXPERTS
    return jnp.concatenate(
        [
            lax.dynamic_slice_in_dim(rows, (expert ^ at) * width, width, 1)
            for at in range(EXPERTS)
        ],
        axis=1,
    )


def all_sum(value):
    bits = 1
    while bits < lax.axis_size("dp"):
        value = value + lax.ppermute(value, "dp", swap_perm(lax.axis_size("dp"), bits))
        bits *= 2
    bits = 1
    while bits < lax.axis_size("expert"):
        value = value + over_expert(value, bits)
        bits *= 2
    return value


def after(value, *others):
    return lax.optimization_barrier((value, *others))[0]


def adam_step(moment, square, gradient):
    moment_new = BETA_FIRST * moment + (1.0 - BETA_FIRST) * gradient
    square_new = BETA_SECOND * square + (1.0 - BETA_SECOND) * gradient * gradient
    moment_hat = moment_new / (1.0 - BETA_FIRST**STEP)
    square_hat = square_new / (1.0 - BETA_SECOND**STEP)
    direction = moment_hat / (jnp.sqrt(square_hat) + ADAM_EPS)
    return (gradient, direction, moment_new, square_new)


def body(
    tokens,
    teacher,
    attn_routes,
    mlp_routes,
    image_mask,
    valid,
    master_query,
    moment_query,
    square_query,
    master_project,
    moment_project,
    square_project,
    master_gate_up,
    moment_gate_up,
    square_gate_up,
    master_down,
    moment_down,
    square_down,
    master_key_value,
    moment_key_value,
    square_key_value,
    master_router,
    moment_router,
    square_router,
    master_gains,
    moment_gains,
    square_gains,
):
    partners = lax.axis_size("expert")
    halves = partners // EXPERTS
    core = lax.axis_index("dp") % 2
    expert_at = lax.axis_index("expert")
    expert, half = expert_at // halves, expert_at % halves
    names = (expert_at ^ jnp.arange(partners, dtype=jnp.int32)) // halves
    token_count = tokens.shape[0]
    sequences = 2 * partners
    sixth = master_query.shape[1] // (2 * EXPERTS)

    valid_f = valid.astype(F32)
    marks = jnp.concatenate([attn_routes, image_mask[:, None]], axis=1).astype(BF16)
    marks = jnp.pad(marks, ((0, 0), (0, LANES - marks.shape[1])))
    payload = jnp.concatenate([tokens, marks], axis=1)
    everyone = send_rows([payload] * partners)

    query_mine, query_theirs = halves_of(core, master_query.astype(BF16))
    project_mine, project_theirs = halves_of(core, master_project.astype(BF16).T)
    attn_got = core_swap(jnp.concatenate([query_theirs, project_theirs], axis=1))
    attn_mine = jnp.concatenate([query_mine, project_mine], axis=1)
    width_attn = query_mine.shape[1]

    def arranged(rows):
        return jnp.concatenate(
            [
                partner_columns(expert, rows[:, :width_attn]),
                partner_columns(expert, rows[:, width_attn:]),
            ],
            axis=1,
        )

    weight_attn = gather_chips(stack_rows(core, arranged(attn_mine), arranged(attn_got)))
    weight_query, weight_project = weight_attn[:, :width_attn], weight_attn[:, width_attn:]

    local_rows = master_key_value.shape[0]
    shared_low = master_key_value.astype(BF16).reshape(local_rows, 2, halves, 2, EXPERTS, sixth)
    small = jnp.concatenate(
        [
            master_router,
            master_gains.T,
            jnp.full((local_rows, 1), jnp.sum(valid_f)),
        ],
        axis=1,
    ).astype(BF16)
    small = jnp.pad(small, ((0, 0), (0, LANES - small.shape[1])))
    for_cores = [
        jnp.concatenate([shared_low[:, :, :, at].reshape(local_rows, -1), small], axis=1)
        for at in range(2)
    ]
    pair = jnp.stack(
        [
            jnp.where(core == 0, for_cores[0], for_cores[1]),
            core_swap(jnp.where(core == 0, for_cores[1], for_cores[0])),
        ]
    )
    pair_kv = pair[:, :, :-LANES].reshape(2, local_rows, 2, halves * EXPERTS, sixth)

    def block_for(bits):
        other = expert_at ^ bits
        column = (other % halves) * EXPERTS + other // halves
        picked = lax.dynamic_index_in_dim(pair_kv, column, 3, keepdims=False)
        return jnp.concatenate([picked.reshape(2, local_rows, -1), pair[:, :, -LANES:]], axis=2)

    arrived = jnp.stack([over_expert(block_for(bits), bits) for bits in range(partners)])
    arrived = jnp.stack(
        [lax.dynamic_index_in_dim(arrived, expert_at ^ at, 0, keepdims=False) for at in range(partners)]
    )
    arrived = jnp.where(core == 0, arrived, arrived[:, ::-1]).transpose(1, 0, 2, 3)
    shared_whole = gather_chips(arrived.reshape(2 * partners * local_rows, -1))
    kv_weight = shared_whole[:, : 2 * sixth]
    small_whole = shared_whole[:, 2 * sixth :]
    router_low = small_whole[:, : 2 * EXPERTS]
    router_f = router_low.astype(F32)
    gains_f = small_whole[:, 2 * EXPERTS : 2 * EXPERTS + 2].astype(F32).T
    total_count = jnp.sum(small_whole[:, 2 * EXPERTS + 2].astype(F32)) / local_rows

    width_ff = master_gate_up.shape[2] // 2
    gate_mine, gate_theirs = halves_of(core, master_gate_up[0].astype(BF16))
    up_mine, up_theirs = halves_of(core, master_gate_up[1].astype(BF16))
    gate_up_got = core_swap(jnp.concatenate([gate_theirs, up_theirs], axis=1))
    weight_gate_up = gather_chips(
        stack_rows(core, jnp.concatenate([gate_mine, up_mine], axis=1), gate_up_got)
    )
    down_mine, down_theirs = halves_of(core, master_down.astype(BF16).T)
    weight_down = gather_chips(stack_rows(core, down_mine, core_swap(down_theirs)))

    tables = rope_tables(token_count)
    inputs_all = everyone[:, :D].astype(F32)
    inverse_all = lax.rsqrt(jnp.mean(inputs_all * inputs_all, axis=-1, keepdims=True) + NORM_EPS)
    normed_all = (inputs_all * inverse_all * gains_f[0]).astype(BF16)
    inputs_f = tokens.astype(F32)
    inverse_one, normed_one = inverse_all[:token_count], normed_all[:token_count]
    marks_all = everyone[:, D:].astype(F32).reshape(sequences, token_count, LANES)
    named_all = jnp.any(marks_all[:, :, :TOP] == expert.astype(F32), axis=2)
    slot_all = slots_before(named_all[:, :, None])[:, :, 0]
    slots = jnp.arange(CAP, dtype=jnp.int32)
    pick_all = (named_all[:, None, :] & (slot_all[:, None, :] == slots[None, :, None])).astype(BF16)
    image_on = marks_all[:, :, TOP] > 0.0
    position = jnp.arange(token_count, dtype=jnp.int32)
    allowed = (position[:, None] >= position[None, :])[None] | (
        image_on[:, :, None] & image_on[:, None, :]
    )

    def regroup(rows, bits):
        blocks = rows.reshape((2, partners, token_count) + rows.shape[1:])
        return xor_blocks(blocks, 1, bits).reshape(rows.shape)

    kv_proj = matmul(normed_all, kv_weight)
    key_own = rotate(by_heads(kv_proj[:, :sixth], sequences), *tables).astype(BF16)
    kv_own = jnp.concatenate([from_heads(key_own), kv_proj[:, sixth:].astype(BF16)], axis=1)
    kv_shared = [
        regroup(over_expert(kv_own, step * halves), step * halves) for step in range(EXPERTS)
    ]
    key_heads = by_heads(jnp.concatenate([part[:, :sixth] for part in kv_shared], axis=1), sequences)
    value_heads = by_heads(
        jnp.concatenate([part[:, sixth:] for part in kv_shared], axis=1), sequences
    )
    query_pre = matmul(normed_all, weight_query)
    query_heads = rotate(by_heads(query_pre, sequences), *tables).astype(BF16)
    scores = heads_dot(query_heads, key_heads, 3, 3) * SCALE
    scores = jnp.where(allowed[:, None], scores, MASK_FILL)
    probs = jax.nn.softmax(scores, axis=-1)
    probs_low = probs.astype(BF16)
    attended_all = from_heads(heads_dot(probs_low, value_heads, 3, 2).astype(BF16))

    def per_sequence(table, rows, left_axis):
        blocks = rows.reshape(sequences, -1, rows.shape[1])
        picked = lax.dot_general(
            table, blocks, (((left_axis,), (1,)), ((0,), (0,))), preferred_element_type=F32
        )
        return picked.astype(BF16).reshape(-1, rows.shape[1])

    attended = per_sequence(pick_all, attended_all, 2)

    attn_pick, attn_back, attn_hit = route_tables(attn_routes, names)
    gates_attn = chosen_gates(matmul(normed_one, router_low[:, :EXPERTS]), attn_routes)
    branch_rows = jnp.concatenate(
        return_rows(matmul_back(attended, weight_project), partners)
    )
    branch = [matmul(attn_back[choice], branch_rows) for choice in range(TOP)]
    hidden = inputs_f + sum(gates_attn[:, choice, None] * branch[choice] for choice in range(TOP))

    inverse_two = lax.rsqrt(jnp.mean(hidden * hidden, axis=-1, keepdims=True) + NORM_EPS)
    normed_two = (hidden * inverse_two * gains_f[1]).astype(BF16)
    mlp_pick, mlp_back, mlp_hit = route_tables(mlp_routes, names)
    gates_mlp = chosen_gates(matmul(normed_two, router_low[:, EXPERTS:]), mlp_routes)
    placed = matmul(mlp_pick.reshape(-1, token_count), normed_two).astype(BF16)
    rows_two = send_rows(list(placed.reshape(partners, CAP, D)))
    gate_up_val = matmul(rows_two, weight_gate_up)
    gate_val, up_val = gate_up_val[:, :width_ff], gate_up_val[:, width_ff:]
    active = (jax.nn.silu(gate_val) * up_val).astype(BF16)
    mlp_rows = jnp.concatenate(return_rows(matmul_back(active, weight_down), partners))
    mlp_branch = [matmul(mlp_back[choice], mlp_rows) for choice in range(TOP)]
    outputs = hidden + sum(gates_mlp[:, choice, None] * mlp_branch[choice] for choice in range(TOP))

    deviation = outputs - teacher.astype(F32)
    local_error = jnp.sum(valid_f[:, None] * deviation * deviation)
    total_error = all_sum(local_error.reshape(1, 1))[0, 0]
    grad_out = 2.0 * valid_f[:, None] * deviation / total_count

    def send_grads(pick, gates, hit, grad):
        gate_of = jnp.sum(gates[:, :, None] * hit, axis=1)
        rows = (gate_of.T[:, :, None] * grad[None]).astype(BF16)
        sent = jnp.einsum("kct,ktd->kcd", pick, rows, preferred_element_type=F32).astype(BF16)
        return send_rows(list(sent))

    rows_grad = send_grads(mlp_pick, gates_mlp, mlp_hit, grad_out)
    grad_down = matmul_rows(rows_grad, active).astype(BF16)
    grad_active = matmul(rows_grad, weight_down)
    sigmoid_gate = jax.nn.sigmoid(gate_val)
    grad_gate = (
        grad_active * up_val * sigmoid_gate * (1.0 + gate_val * (1.0 - sigmoid_gate))
    ).astype(BF16)
    grad_up = (grad_active * gate_val * sigmoid_gate).astype(BF16)
    grad_both = jnp.concatenate([grad_gate, grad_up], axis=1)
    down_sum = scatter_chips(grad_down)
    grad_gate_up = matmul_rows(rows_two, grad_both).astype(BF16)
    gate_up_sum = scatter_chips(after(grad_gate_up, down_sum))
    normed_two_rows = return_rows(
        matmul_back(after(grad_both, grad_down), weight_gate_up), partners
    )
    grad_gates_mlp = jnp.stack(
        [jnp.sum(grad_out * mlp_branch[choice], axis=-1) for choice in range(TOP)], axis=1
    )
    grad_logits_mlp = gate_back(gates_mlp, grad_gates_mlp, mlp_routes)
    grad_normed_two = matmul(
        jnp.sum(mlp_back, axis=0), jnp.concatenate(normed_two_rows)
    ) + exact_back(grad_logits_mlp, router_f[:, EXPERTS:])
    grad_hidden_norm, grad_gain_two = norm_back(hidden, inverse_two, gains_f[1], grad_normed_two)
    grad_hidden = grad_out + grad_hidden_norm
    grad_router_two = exact_rows(normed_two.astype(F32), grad_logits_mlp)

    rows_grad_attn = send_grads(attn_pick, gates_attn, attn_hit, after(grad_hidden, down_sum))
    grad_project = matmul_rows(rows_grad_attn, attended).astype(BF16)
    grad_attended = matmul(rows_grad_attn, weight_project).astype(BF16)
    grad_gates_attn = jnp.stack(
        [jnp.sum(grad_hidden * branch[choice], axis=-1) for choice in range(TOP)], axis=1
    )
    grad_logits_attn = gate_back(gates_attn, grad_gates_attn, attn_routes)
    grad_heads = by_heads(per_sequence(pick_all, grad_attended, 1), sequences)
    grad_probs = heads_dot(grad_heads, value_heads, 3, 3)
    inner = jnp.sum(probs * grad_probs, axis=-1, keepdims=True)
    grad_scores = (probs * (grad_probs - inner)).astype(BF16)
    grad_query_heads = heads_dot(grad_scores, key_heads, 3, 2) * SCALE
    grad_key_heads = heads_dot(grad_scores, query_heads, 2, 2) * SCALE
    grad_value_heads = heads_dot(probs_low, grad_heads, 2, 2)
    back_tables = (tables[0], -tables[1])
    grad_query_pre = from_heads(rotate(grad_query_heads, *back_tables).astype(BF16))
    grad_keys = from_heads(rotate(grad_key_heads, *back_tables).astype(BF16))
    grad_values = from_heads(grad_value_heads.astype(BF16))
    grad_query = matmul_rows(normed_all, grad_query_pre).astype(BF16)
    grad_kv = sum(
        over_expert(
            regroup(
                jnp.concatenate(
                    [
                        grad_keys[:, step * sixth : (step + 1) * sixth],
                        grad_values[:, step * sixth : (step + 1) * sixth],
                    ],
                    axis=1,
                ),
                step * halves,
            ),
            step * halves,
        ).astype(F32)
        for step in range(EXPERTS)
    ).astype(BF16)
    grad_kv_weight = matmul_rows(normed_all, grad_kv).astype(BF16)
    normed_one_rows = return_rows(
        matmul_back(grad_query_pre, weight_query) + matmul_back(grad_kv, kv_weight), partners
    )
    grad_normed_one = sum(rows.astype(F32) for rows in normed_one_rows) + exact_back(
        grad_logits_attn, router_f[:, :EXPERTS]
    )
    grad_inputs_norm, grad_gain_one = norm_back(inputs_f, inverse_one, gains_f[0], grad_normed_one)
    input_grad = grad_hidden + grad_inputs_norm
    grad_small = jnp.concatenate(
        [
            exact_rows(normed_one.astype(F32), grad_logits_attn),
            grad_router_two,
            grad_gain_one[:, None],
            grad_gain_two[:, None],
        ],
        axis=1,
    ).astype(BF16)
    grad_small = jnp.pad(grad_small, ((0, 0), (0, LANES - grad_small.shape[1])))

    attn_sum = scatter_chips(
        after(
            jnp.concatenate([grad_query, grad_project, grad_kv_weight, grad_small], axis=1),
            gate_up_sum,
        )
    )
    down_mine, down_other = exchange_rows(core, down_sum)
    gate_up_mine, gate_up_other = exchange_rows(core, gate_up_sum)
    attn_mine, attn_other = exchange_rows(core, attn_sum[:, : 2 * width_attn])
    attn_mine, attn_other = arranged(attn_mine), arranged(attn_other)
    shared_sum = attn_sum[:, 2 * width_attn :]
    shared_sum = shared_sum.reshape(2, partners, local_rows, -1)
    shared_mine = jnp.where(core == 0, shared_sum[0], shared_sum[1])
    shared_theirs = core_swap(jnp.where(core == 0, shared_sum[1], shared_sum[0]))
    shared_pair = jnp.where(
        core == 0, jnp.stack([shared_mine, shared_theirs]), jnp.stack([shared_theirs, shared_mine])
    )
    received = jnp.stack(
        [
            over_expert(lax.dynamic_index_in_dim(shared_pair, expert_at ^ bits, 1, keepdims=False), bits)
            for bits in range(partners)
        ]
    )
    small_sum = jnp.sum(received[..., -LANES:].astype(F32), axis=(0, 1))
    received = jnp.stack(
        [lax.dynamic_index_in_dim(received, expert_at ^ at, 0, keepdims=False) for at in range(partners)]
    )
    reduced_kv = (
        received[..., :-LANES]
        .reshape(EXPERTS, halves, 2, local_rows, 2, sixth)
        .transpose(3, 4, 1, 2, 0, 5)
        .reshape(local_rows, -1)
        .astype(F32)
    )
    reduced_router = small_sum[:, : 2 * EXPERTS]
    reduced_gains = small_sum[:, 2 * EXPERTS : 2 * EXPERTS + 2].T
    reduced_query = in_core_order(
        core, attn_mine[:, :width_attn], attn_other[:, :width_attn], 1
    ).astype(F32)
    reduced_project = after(
        in_core_order(core, attn_mine[:, width_attn:], attn_other[:, width_attn:], 1).T
    ).astype(F32)
    reduced_down = after(in_core_order(core, down_mine, down_other, 1).T).astype(F32)
    reduced_gate_up = jnp.stack(
        [
            in_core_order(
                core,
                gate_up_mine[:, at * width_ff : (at + 1) * width_ff],
                gate_up_other[:, at * width_ff : (at + 1) * width_ff],
                1,
            )
            for at in range(2)
        ]
    ).astype(F32)
    loss_value = total_error / total_count
    return (
        outputs,
        loss_value,
        input_grad,
        *adam_step(moment_query, square_query, reduced_query),
        *adam_step(moment_project, square_project, reduced_project),
        *adam_step(moment_gate_up, square_gate_up, reduced_gate_up),
        *adam_step(moment_down, square_down, reduced_down),
        *adam_step(moment_key_value, square_key_value, reduced_kv),
        *adam_step(moment_router, square_router, reduced_router),
        *adam_step(moment_gains, square_gains, reduced_gains),
    )


def solution(mesh):
    rows = P(("dp", "expert"), None)
    flat = P(("dp", "expert"))
    columns = P(None, ("dp", "expert"))
    query, project, gate_up = P("dp", "expert"), P("expert", "dp"), P(None, "dp", "expert")
    weights = (query, project, gate_up, project, rows, rows, columns)
    return jax.shard_map(
        body,
        mesh=mesh,
        in_specs=(rows, rows, rows, rows, flat, flat)
        + tuple(spec for spec in weights for _ in range(3)),
        out_specs=(rows, P(), rows) + tuple(spec for spec in weights for _ in range(4)),
        check_vma=False,
    )
```

time: 2750 us -> 1250 us (0.45)
  waiting for transfers between devices: 1720 us -> 576 us
  blocking collectives: 486 us -> 0 us
  local copies, waits for them, and re-layouts: 71.4 us -> 202 us
  matrix products: 275 us -> 178 us
  starting transfers between devices: 26.8 us -> 79.3 us
  other arithmetic: 140 us -> 180 us
    reduce_scatter x5 -> x3, waiting for transfers between devices: 1230 us -> 69.8 us  [scatter_chips(): lax.psum_scatter(partial, 'dp', scatter_dimension=0, tiled=True, axis_ind...]
    ppermute x0 -> x57, waiting for transfers between devices: none -> 423 us  [the longest x38 404 us: over_expert(): lax.ppermute(value, 'expert', swap_perm(lax.axis_size('expert'), bits))]
    all_to_all x6 -> x0, waiting for transfers between devices: 316 us -> none  [the longest x5 291 us: give_back(): lax.all_to_all(buffer, 'expert', split_axis=0, concat_axis=0, tiled=True)]
    all_to_all x6 -> x0, blocking collectives: 251 us -> none  [the longest x5 212 us: dispatch(): lax.all_to_all(buffer, 'expert', split_axis=0, concat_axis=0, tiled=True)]
    all_gather x2 -> x0, blocking collectives: 198 us -> none  [the longest x1 129 us: body(): lax.all_gather(master_router.astype(jnp.bfloat16), ('dp', 'expert'), axis...]
    unnamed x195 -> x324, local copies, waits for them, and re-layouts: 20.2 us -> 116 us
    ppermute x0 -> x57, starting transfers between devices: none -> 78.1 us  [the longest x38 70.6 us: over_expert(): lax.ppermute(value, 'expert', swap_perm(lax.axis_size('expert'), bits))]
    unnamed x14 -> x7, waiting for transfers between devices: 75.2 us -> 0.11 us
  transfers between devices with their start and end apart: 18 -> 64, of which waited for: 14 -> 39; matrix products, arithmetic and copies ran while one was open for 12% -> 37% of each run, Pallas kernels for 0% -> 0%
where the time goes in v1:
time: 1250 us; the launch traced here: 1240 us
  waiting for transfers between devices  576 us (46%)
  local copies, waits for them, and re-layouts  202 us (16%)
  other arithmetic  180 us (14%)
  matrix products  178 us (14%)
  starting transfers between devices  79.3 us (6%)
  between operations  23.1 us (2%)
    ppermute x38, waiting for transfers between devices, over_expert(): lax.ppermute(value, 'expert', swap_perm(lax.axis_size('expert'), bits))  404 us
    unnamed x324, local copies, waits for them, and re-layouts  116 us
    all_gather x4, waiting for transfers between devices, gather_chips(): lax.all_gather(block, 'dp', axis=0, tiled=True, axis_index_groups=chip_gr...  82.9 us
    ppermute x38, starting transfers between devices, over_expert(): lax.ppermute(value, 'expert', swap_perm(lax.axis_size('expert'), bits))  70.6 us
    reduce_scatter x3, waiting for transfers between devices, scatter_chips(): lax.psum_scatter(partial, 'dp', scatter_dimension=0, tiled=True, axis_ind...  69.8 us
    dot_general x13, matrix products, matmul(): return jnp.dot(left_side, right_side, preferred_element_type=F32)  66.5 us
    dot_general x5, matrix products, matmul_back(): lax.dot_general(left_side, right_side, (((1,), (1,)), ((), ())), preferre...  51.6 us
    dot_general x5, matrix products, matmul_rows(): lax.dot_general(left_side, right_side, (((0,), (0,)), ((), ())), preferre...  47.9 us
  transfers between devices with their start and end apart: 64, of which 39 were waited for; matrix products, arithmetic and copies ran while one was open for 37% of the time, Pallas kernels for 0%

profile of v1, /device:TPU:0, one launch (start us, length us, event | category | flops | bytes accessed | tf_op | source)
XLA Modules:
  0.0 1238.2 jit_solution(11045291166668294501)
XLA Ops:
  30.1 9.1 collective-permute-done.6
  55.8 23.8 %maximum_maximum_fusion = bf16[512,5632]{1,0:T(8,128)(2,1)} fusion(bf16[256,2816]{1,0:T(8,128)(2,1)S(1)} %get-tuple-element.300, bf16[256,2816]{1,0:T(8,128)(2,1)S(1)} %get-tuple-element.431), kind=kLoop, calls=%fused_computation.20 | loop fusion | flops 23068672 | bytes 8650752 | tf_op jit(solution)/shard_map/concatenate | solution.py:112
  96.5 15.2 %collective-permute-done = bf16[128,2176]{1,0:T(8,128)(2,1)} collective-permute-done((bf16[128,2176]{1,0:T(8,128)(2,1)}, bf16[128,2176]{1,0:T(8,128)(2,1)}, u32[]{:S(2)}, u32[]{:S(2)}) %collective-permute-start) | collective-permute-done | bytes 557088 | tf_op jit(solution)/shard_map/ppermute | solution.py:85
  111.7 14.6 %collective-permute-done.1 = bf16[128,2176]{1,0:T(8,128)(2,1)} collective-permute-done((bf16[128,2176]{1,0:T(8,128)(2,1)}, bf16[128,2176]{1,0:T(8,128)(2,1)}, u32[]{:S(2)}, u32[]{:S(2)}) %collective-permute-start.1) | collective-permute-done | bytes 557088 | tf_op jit(solution)/shard_map/ppermute | solution.py:85
  153.6 10.7 collective-permute-start.10
  164.8 9.8 collective-permute-done.11
  176.4 5.5 rev.32
  184.2 57.2 %collective-permute-done.10 = bf16[1024,512]{0,1:T(8,128)(2,1)} collective-permute-done((bf16[1024,512]{0,1:T(8,128)(2,1)}, bf16[1024,512]{0,1:T(8,128)(2,1)}, u32[]{:S(2)}, u32[]{:S(2)}) %collective-permute-start.10) | collective-permute-done | bytes 1048608 | tf_op jit(solution)/shard_map/ppermute | solution.py:85
  246.6 7.6 rev.30
  263.0 8.2 fusion.26
  274.2 5.8 copy.330
  311.3 9.5 collective-permute-done.15
  320.8 22.6 %collective-permute-done.14 = bf16[96,2048]{1,0:T(8,128)(2,1)S(1)} collective-permute-done((bf16[96,2048]{1,0:T(8,128)(2,1)S(1)}, bf16[96,2048]{1,0:T(8,128)(2,1)S(1)}, u32[]{:S(2)}, u32[]{:S(2)}) %collective-permute-start.14) | collective-permute-done | bytes 393248 | tf_op jit(solution)/shard_map/ppermute | solution.py:85
  352.1 13.1 %collective-permute-done.16 = bf16[96,2048]{1,0:T(8,128)(2,1)S(1)} collective-permute-done((bf16[96,2048]{1,0:T(8,128)(2,1)S(1)}, bf16[96,2048]{1,0:T(8,128)(2,1)S(1)}, u32[]{:S(2)}, u32[]{:S(2)}) %collective-permute-start.16) | collective-permute-done | bytes 393248 | tf_op jit(solution)/shard_map/ppermute | solution.py:85
  365.2 12.4 %collective-permute-done.17 = bf16[96,2048]{1,0:T(8,128)(2,1)S(1)} collective-permute-done((bf16[96,2048]{1,0:T(8,128)(2,1)S(1)}, bf16[96,2048]{1,0:T(8,128)(2,1)S(1)}, u32[]{:S(2)}, u32[]{:S(2)}) %collective-permute-start.17) | collective-permute-done | bytes 393248 | tf_op jit(solution)/shard_map/ppermute | solution.py:85
  383.3 23.9 %fusion.178 = f32[768,5632]{1,0:T(8,128)S(1)} fusion(bf16[768,2048]{1,0:T(8,128)(2,1)} %constant_dynamic-update-slice_fusion.21, bf16[2048,5632]{1,0:T(8,128)(2,1)} %all-gather.9.cloned.1.call-done), kind=kOutput, calls=%fused_computation.483 | convolution fusion | flops 17716740096 | bytes 43515904 | tf_op jit(solution)/shard_map/dot_general | solution.py:28
  407.2 5.9 copy-done.6
  417.3 82.1 %all-gather.11.cloned.1.call-done = bf16[2048,2816]{1,0:T(8,128)(2,1)} async-done(((bf16[512,2816]{1,0:T(8,128)(2,1)}), bf16[2048,2816]{1,0:T(8,128)(2,1)}) %all-gather.11.cloned.1.call-update) | async-done | bytes 11534352 | tf_op jit(solution)/shard_map/all_gather | solution.py:94
  499.4 13.3 %fusion.179 = f32[768,2048]{1,0:T(8,128)S(1)} fusion(bf16[768,2816]{1,0:T(8,128)(2,1)} %multiply_convert_fusion.2, bf16[2048,2816]{1,0:T(8,128)(2,1)} %all-gather.11.cloned.1.call-done), kind=kOutput, calls=%fused_computation.484 | convolution fusion | flops 8858370048 | bytes 22151168 | tf_op jit(solution)/shard_map/dot_general | solution.py:32
  528.0 9.5 collective-permute-done.25
  537.5 23.5 %collective-permute-done.24 = bf16[96,2048]{1,0:T(8,128)(2,1)S(1)} collective-permute-done((bf16[96,2048]{1,0:T(8,128)(2,1)S(1)}, bf16[96,2048]{1,0:T(8,128)(2,1)S(1)}, u32[]{:S(2)}, u32[]{:S(2)}) %collective-permute-start.24) | collective-permute-done | bytes 393248 | tf_op jit(solution)/shard_map/ppermute | solution.py:85
  569.5 13.4 %collective-permute-done.31 = bf16[96,2048]{1,0:T(8,128)(2,1)S(1)} collective-permute-done((bf16[96,2048]{1,0:T(8,128)(2,1)S(1)}, bf16[96,2048]{1,0:T(8,128)(2,1)S(1)}, u32[]{:S(2)}, u32[]{:S(2)}) %collective-permute-start.31) | collective-permute-done | bytes 393248 | tf_op jit(solution)/shard_map/ppermute | solution.py:85
  582.9 12.1 collective-permute-done.32
  600.4 12.2 convolution_convert_fusion.1
  612.7 21.0 %multiply_convert_fusion.1 = (bf16[768,2816]{1,0:T(8,128)(2,1)S(1)}, bf16[768,2816]{1,0:T(8,128)(2,1)}) fusion(f32[768,5632]{1,0:T(8,128)} %copy-done.6, bf16[768,2048]{1,0:T(8,128)(2,1)} %copy-done.70, bf16[2048,2816]{1,0:T(8,128)(2,1)} %all-gather.11.cloned.1.call-done), kind=kOutput, calls=%fused_computation.12 | convolution fusion | flops 8886484992 | bytes 40632320 | tf_op jit(solution)/shard_map/dot_general | solution.py:28
  635.8 24.3 %convolution_convert_fusion = bf16[2048,5632]{1,0:T(8,128)(2,1)} fusion(bf16[768,2048]{1,0:T(8,128)(2,1)} %constant_dynamic-update-slice_fusion.21, bf16[768,2816]{1,0:T(8,128)(2,1)} %get-tuple-element.278, bf16[768,2816]{1,0:T(8,128)(2,1)S(1)} %get-tuple-element.277), kind=kOutput, calls=%fused_computation.1 | convolution fusion | flops 17745575936 | bytes 34865152 | tf_op jit(solution)/shard_map/dot_general | solution.py:38
  660.1 69.8 %reduce-scatter.4.cloned.1.call-done = bf16[512,2816]{1,0:T(8,128)(2,1)} async-done(((bf16[2048,2816]{1,0:T(8,128)(2,1)}), bf16[512,2816]{1,0:T(8,128)(2,1)}) %reduce-scatter.4.cloned.1.call-update) | async-done | bytes 2883600 | tf_op jit(solution)/shard_map/reduce_scatter | solution.py:98
  729.9 7.6 pad_maximum_fusion.1
  737.5 24.9 %fusion.180 = f32[768,2048]{1,0:T(8,128)S(1)} fusion(bf16[768,5632]{1,0:T(8,128)(2,1)} %pad_maximum_fusion.1, bf16[2048,5632]{1,0:T(8,128)(2,1)} %all-gather.9.cloned.1.call-done), kind=kOutput, calls=%fused_computation.485 | convolution fusion | flops 17716740096 | bytes 38010880 | tf_op jit(solution)/shard_map/dot_general | solution.py:32
  772.2 8.6 collective-permute-done.38
  780.8 23.5 %collective-permute-done.37 = bf16[96,2048]{1,0:T(8,128)(2,1)S(1)} collective-permute-done((bf16[96,2048]{1,0:T(8,128)(2,1)S(1)}, bf16[96,2048]{1,0:T(8,128)(2,1)S(1)}, u32[]{:S(2)}, u32[]{:S(2)}) %collective-permute-start.37) | collective-permute-done | bytes 393248 | tf_op jit(solution)/shard_map/ppermute | solution.py:85
  812.6 13.3 %collective-permute-done.39 = bf16[96,2048]{1,0:T(8,128)(2,1)S(1)} collective-permute-done((bf16[96,2048]{1,0:T(8,128)(2,1)S(1)}, bf16[96,2048]{1,0:T(8,128)(2,1)S(1)}, u32[]{:S(2)}, u32[]{:S(2)}) %collective-permute-start.39) | collective-permute-done | bytes 393248 | tf_op jit(solution)/shard_map/ppermute | solution.py:85
  825.8 12.2 collective-permute-done.40
  881.0 7.0 collective-permute-start.44
  897.1 7.6 fusion.17
  904.7 64.3 %collective-permute-done.44 = bf16[1024,512]{1,0:T(8,128)(2,1)} collective-permute-done((bf16[1024,512]{1,0:T(8,128)(2,1)}, bf16[1024,512]{1,0:T(8,128)(2,1)}, u32[]{:S(2)}, u32[]{:S(2)}) %collective-permute-start.44) | collective-permute-done | bytes 1048608 | tf_op jit(solution)/shard_map/ppermute | solution.py:85
  995.6 9.8 collective-permute-done.49
  1005.4 29.5 %collective-permute-done.48 = bf16[128,2048]{1,0:T(8,128)(2,1)S(1)} collective-permute-done((bf16[128,2048]{1,0:T(8,128)(2,1)S(1)}, bf16[128,2048]{1,0:T(8,128)(2,1)S(1)}, u32[]{:S(2)}, u32[]{:S(2)}) %collective-permute-start.48) | collective-permute-done | bytes 524320 | tf_op jit(solution)/shard_map/ppermute | solution.py:85
  1036.4 28.4 %pad_maximum_fusion = bf16[2048,2688]{0,1:T(8,128)(2,1)} fusion(bf16[2048,128]{0,1:T(8,128)(2,1)S(1)} %fusion.92, bf16[2048,512]{0,1:T(8,128)(2,1)S(1)} %convolution_convert_fusion.4, bf16[2048,1024]{0,1:T(8,128)(2,1)S(1)} %convolution_convert_fusion.2, bf16[2048,1024]{0,1:T(8,128)(2,1)S(1)} %convolution_convert_fusion.3), kind=kLoop, calls=%fused_computation.7 | loop fusion | flops 44040192 | bytes 22020096 | tf_op jit(solution)/shard_map/concatenate | solution.py:531
  1073.5 6.5 copy.347
  1079.9 6.5 copy.348
  1115.7 5.8 broadcast_select_fusion.1
  1121.4 9.9 add_divide_fusion.2
  1131.3 6.3 copy.359
  1137.6 6.6 copy.360
  1144.2 6.7 copy.361
  1159.0 20.2 %add_divide_fusion = (f32[2,256,5632]{2,1,0:T(8,128)}, f32[2,256,5632]{2,1,0:T(8,128)}, f32[2,256,5632]{2,1,0:T(8,128)}, f32[2,256,5632]{2,1,0:T(8,128)}) fusion(f32[2,256,5632]{2,1,0:T(8,128)S(1)} %bitcast.298, f32[2,256,5632]{2,1,0:T(8,128)} %param.41, bf16[1,256,5632]{2,1,0:T(8,128)(2,1)S(1)} %maximum_select_fusion.1, ...), kind=kLoop, calls=%fused_computation.4 | loop fusion | flops 37486592 | bytes 74973184 | tf_op jit(solution)/shard_map/div | solution.py:249
  1193.3 7.1 collective-permute-done.55
  (667 shorter events, 366.9 us)
Async XLA Ops:
  7.2 129.0 %all-gather.5.cloned.1.call-start = ((), (), s32[]{:S(2)}) async-start(), calls=%async_computation.3 | async-start | bytes 3276800 | tf_op jit(solution)/shard_map/all_gather | solution.py:94
  19.9 10.1 collective-permute-start.7
  25.0 14.2 %collective-permute-start.6 = (bf16[2,64,640]{2,1,0:T(8,128)(2,1)S(1)}, bf16[2,64,640]{2,1,0:T(8,128)(2,1)S(1)}, u32[]{:S(2)}, u32[]{:S(2)}) collective-permute-start(bf16[2,64,640]{2,1,0:T(8,128)(2,1)S(1)} %get-tuple-element.392), channel_id=1, source_target_pairs={{0,2},{1,3},{2,0},{3,1},{4,6},{5,7},{6,4},{7,5},{8,10},{9,11},{10,... | collective-permute-start | bytes 491528 | tf_op jit(solution)/shard_map/ppermute | solution.py:85
  25.0 14.2 %collective-permute-start.5 = (bf16[2,64,640]{2,1,0:T(8,128)(2,1)S(1)}, bf16[2,64,640]{2,1,0:T(8,128)(2,1)S(1)}, u32[]{:S(2)}, u32[]{:S(2)}) collective-permute-start(bf16[2,64,640]{2,1,0:T(8,128)(2,1)S(1)} %get-tuple-element.391), channel_id=1, source_target_pairs={{0,1},{1,0},{2,3},{3,2},{4,5},{5,4},{6,7},{7,6},{8,9},{9,8},{10,11... | collective-permute-start | bytes 491528 | tf_op jit(solution)/shard_map/ppermute | solution.py:85
  40.5 222.5 %all-gather.7.cloned.1.call-start = ((), (), s32[]{:S(2)}) async-start(), calls=%async_computation.4 | async-start | bytes 10485760 | tf_op jit(solution)/shard_map/all_gather | solution.py:94
  49.2 334.1 %all-gather.9.cloned.1.call-start = ((), (), s32[]{:S(2)}) async-start(), calls=%async_computation.5 | async-start | bytes 28835840 | tf_op jit(solution)/shard_map/all_gather | solution.py:94
  55.6 24.0 %collective-permute-start.20 = (bf16[256,5632]{1,0:T(8,128)(2,1)S(1)}, bf16[256,5632]{1,0:T(8,128)(2,1)}, u32[]{:S(2)}, u32[]{:S(2)}) collective-permute-start(bf16[256,5632]{1,0:T(8,128)(2,1)S(1)} %pad_maximum_fusion.2), channel_id=1, source_target_pairs={{0,4},{4,0},{8,12},{12,8},{16,20},{20,16},{24,28},{28,24},{1,5},{5... | collective-permute-start | bytes 8650760 | tf_op jit(solution)/shard_map/ppermute | solution.py:79
  83.2 416.1 %all-gather.11.cloned.1.call-start = ((), (), s32[]{:S(2)}) async-start(), calls=%async_computation.6 | async-start | bytes 14417920 | tf_op jit(solution)/shard_map/all_gather | solution.py:94
  85.4 26.4 %collective-permute-start = (bf16[128,2176]{1,0:T(8,128)(2,1)}, bf16[128,2176]{1,0:T(8,128)(2,1)}, u32[]{:S(2)}, u32[]{:S(2)}) collective-permute-start(bf16[128,2176]{1,0:T(8,128)(2,1)} %get-tuple-element.371), channel_id=1, source_target_pairs={{0,1},{1,0},{2,3},{3,2},{4,5},{5,4},{6,7},{7,6},{8,9},{9,8},{10,11... | collective-permute-start | bytes 1671176 | tf_op jit(solution)/shard_map/ppermute | solution.py:85
  85.4 40.9 %collective-permute-start.1 = (bf16[128,2176]{1,0:T(8,128)(2,1)}, bf16[128,2176]{1,0:T(8,128)(2,1)}, u32[]{:S(2)}, u32[]{:S(2)}) collective-permute-start(bf16[128,2176]{1,0:T(8,128)(2,1)} %get-tuple-element.371), channel_id=1, source_target_pairs={{0,2},{1,3},{2,0},{3,1},{4,6},{5,7},{6,4},{7,5},{8,10},{9,11},{10,... | collective-permute-start | bytes 1671176 | tf_op jit(solution)/shard_map/ppermute | solution.py:85
  88.6 37.7 %collective-permute-start.2 = (bf16[128,2176]{1,0:T(8,128)(2,1)}, bf16[128,2176]{1,0:T(8,128)(2,1)}, u32[]{:S(2)}, u32[]{:S(2)}) collective-permute-start(bf16[128,2176]{1,0:T(8,128)(2,1)} %get-tuple-element.371), channel_id=1, source_target_pairs={{0,3},{1,2},{2,1},{3,0},{4,7},{5,6},{6,5},{7,4},{8,11},{9,10},{10,... | collective-permute-start | bytes 1671176 | tf_op jit(solution)/shard_map/ppermute | solution.py:85
  96.0 52.7 %collective-permute-start.21 = (bf16[256,2816]{1,0:T(8,128)(2,1)}, bf16[256,2816]{1,0:T(8,128)(2,1)}, u32[]{:S(2)}, u32[]{:S(2)}) collective-permute-start(bf16[256,2816]{1,0:T(8,128)(2,1)} %get-tuple-element.295), channel_id=1, source_target_pairs={{0,4},{4,0},{8,12},{12,8},{16,20},{20,16},{24,28},{28,24},{1,5},{5... | collective-permute-start | bytes 4325384 | tf_op jit(solution)/shard_map/ppermute | solution.py:79
  146.4 28.2 %collective-permute-start.11 = (bf16[1024,512]{0,1:T(8,128)(2,1)}, bf16[1024,512]{0,1:T(8,128)(2,1)}, u32[]{:S(2)}, u32[]{:S(2)}) collective-permute-start(bf16[1024,512]{0,1:T(8,128)(2,1)} %pad_maximum_fusion.11), channel_id=1, source_target_pairs={{0,3},{1,2},{2,1},{3,0},{4,7},{5,6},{6,5},{7,4},{8,11},{9,10},{10,... | collective-permute-start | bytes 3145736 | tf_op jit(solution)/shard_map/ppermute | solution.py:85
  151.8 578.0 %reduce-scatter.4.cloned.1.call-start = ((), (), s32[]{:S(2)}) async-start(), calls=%async_computation.7 | async-start | bytes 14417920 | tf_op jit(solution)/shard_map/reduce_scatter | solution.py:98
  153.6 87.8 %collective-permute-start.10 = (bf16[1024,512]{0,1:T(8,128)(2,1)}, bf16[1024,512]{0,1:T(8,128)(2,1)}, u32[]{:S(2)}, u32[]{:S(2)}) collective-permute-start(bf16[1024,512]{0,1:T(8,128)(2,1)} %pad_maximum_fusion.11), channel_id=1, source_target_pairs={{0,2},{1,3},{2,0},{3,1},{4,6},{5,7},{6,4},{7,5},{8,10},{9,11},{10,... | collective-permute-start | bytes 3145736 | tf_op jit(solution)/shard_map/ppermute | solution.py:85
  164.3 80.4 %collective-permute-start.9 = (bf16[1024,512]{0,1:T(8,128)(2,1)}, bf16[1024,512]{0,1:T(8,128)(2,1)}, u32[]{:S(2)}, u32[]{:S(2)}) collective-permute-start(bf16[1024,512]{0,1:T(8,128)(2,1)} %pad_maximum_fusion.11), channel_id=1, source_target_pairs={{0,1},{1,0},{2,3},{3,2},{4,5},{5,4},{6,7},{7,6},{8,9},{9,8},{10,11... | collective-permute-start | bytes 3145736 | tf_op jit(solution)/shard_map/ppermute | solution.py:85
  306.8 14.0 %collective-permute-start.15 = (bf16[96,2048]{1,0:T(8,128)(2,1)S(1)}, bf16[96,2048]{1,0:T(8,128)(2,1)S(1)}, u32[]{:S(2)}, u32[]{:S(2)}) collective-permute-start(bf16[96,2048]{1,0:T(8,128)(2,1)S(1)} %get-tuple-element.338), channel_id=1, source_target_pairs={{0,3},{1,2},{2,1},{3,0},{4,7},{5,6},{6,5},{7,4},{8,11},{9,10},{10,... | collective-permute-start | bytes 1179656 | tf_op jit(solution)/shard_map/ppermute | solution.py:85
  309.9 33.5 %collective-permute-start.14 = (bf16[96,2048]{1,0:T(8,128)(2,1)S(1)}, bf16[96,2048]{1,0:T(8,128)(2,1)S(1)}, u32[]{:S(2)}, u32[]{:S(2)}) collective-permute-start(bf16[96,2048]{1,0:T(8,128)(2,1)S(1)} %get-tuple-element.339), channel_id=1, source_target_pairs={{0,2},{1,3},{2,0},{3,1},{4,6},{5,7},{6,4},{7,5},{8,10},{9,11},{10,... | collective-permute-start | bytes 1179656 | tf_op jit(solution)/shard_map/ppermute | solution.py:85
  309.9 33.5 %collective-permute-start.13 = (bf16[96,2048]{1,0:T(8,128)(2,1)S(1)}, bf16[96,2048]{1,0:T(8,128)(2,1)S(1)}, u32[]{:S(2)}, u32[]{:S(2)}) collective-permute-start(bf16[96,2048]{1,0:T(8,128)(2,1)S(1)} %get-tuple-element.340), channel_id=1, source_target_pairs={{0,1},{1,0},{2,3},{3,2},{4,5},{5,4},{6,7},{7,6},{8,9},{9,8},{10,11... | collective-permute-start | bytes 1179656 | tf_op jit(solution)/shard_map/ppermute | solution.py:85
  347.7 17.5 %collective-permute-start.16 = (bf16[96,2048]{1,0:T(8,128)(2,1)S(1)}, bf16[96,2048]{1,0:T(8,128)(2,1)S(1)}, u32[]{:S(2)}, u32[]{:S(2)}) collective-permute-start(bf16[96,2048]{1,0:T(8,128)(2,1)S(1)} %get-tuple-element.336), channel_id=1, source_target_pairs={{0,1},{1,0},{2,3},{3,2},{4,5},{5,4},{6,7},{7,6},{8,9},{9,8},{10,11... | collective-permute-start | bytes 1179656 | tf_op jit(solution)/shard_map/ppermute | solution.py:85
  347.7 29.9 %collective-permute-start.17 = (bf16[96,2048]{1,0:T(8,128)(2,1)S(1)}, bf16[96,2048]{1,0:T(8,128)(2,1)S(1)}, u32[]{:S(2)}, u32[]{:S(2)}) collective-permute-start(bf16[96,2048]{1,0:T(8,128)(2,1)S(1)} %get-tuple-element.335), channel_id=1, source_target_pairs={{0,2},{1,3},{2,0},{3,1},{4,6},{5,7},{6,4},{7,5},{8,10},{9,11},{10,... | collective-permute-start | bytes 1179656 | tf_op jit(solution)/shard_map/ppermute | solution.py:85
  349.8 27.8 %collective-permute-start.18 = (bf16[96,2048]{1,0:T(8,128)(2,1)S(1)}, bf16[96,2048]{1,0:T(8,128)(2,1)S(1)}, u32[]{:S(2)}, u32[]{:S(2)}) collective-permute-start(bf16[96,2048]{1,0:T(8,128)(2,1)S(1)} %get-tuple-element.334), channel_id=1, source_target_pairs={{0,3},{1,2},{2,1},{3,0},{4,7},{5,6},{6,5},{7,4},{8,11},{9,10},{10,... | collective-permute-start | bytes 1179656 | tf_op jit(solution)/shard_map/ppermute | solution.py:85
  523.5 14.0 %collective-permute-start.25 = (bf16[96,2048]{1,0:T(8,128)(2,1)S(1)}, bf16[96,2048]{1,0:T(8,128)(2,1)S(1)}, u32[]{:S(2)}, u32[]{:S(2)}) collective-permute-start(bf16[96,2048]{1,0:T(8,128)(2,1)S(1)} %get-tuple-element.329), channel_id=1, source_target_pairs={{0,3},{1,2},{2,1},{3,0},{4,7},{5,6},{6,5},{7,4},{8,11},{9,10},{10,... | collective-permute-start | bytes 1179656 | tf_op jit(solution)/shard_map/ppermute | solution.py:85
  526.9 34.0 %collective-permute-start.24 = (bf16[96,2048]{1,0:T(8,128)(2,1)S(1)}, bf16[96,2048]{1,0:T(8,128)(2,1)S(1)}, u32[]{:S(2)}, u32[]{:S(2)}) collective-permute-start(bf16[96,2048]{1,0:T(8,128)(2,1)S(1)} %get-tuple-element.330), channel_id=1, source_target_pairs={{0,2},{1,3},{2,0},{3,1},{4,6},{5,7},{6,4},{7,5},{8,10},{9,11},{10,... | collective-permute-start | bytes 1179656 | tf_op jit(solution)/shard_map/ppermute | solution.py:85
  526.9 34.0 %collective-permute-start.23 = (bf16[96,2048]{1,0:T(8,128)(2,1)S(1)}, bf16[96,2048]{1,0:T(8,128)(2,1)S(1)}, u32[]{:S(2)}, u32[]{:S(2)}) collective-permute-start(bf16[96,2048]{1,0:T(8,128)(2,1)S(1)} %get-tuple-element.331), channel_id=1, source_target_pairs={{0,1},{1,0},{2,3},{3,2},{4,5},{5,4},{6,7},{7,6},{8,9},{9,8},{10,11... | collective-permute-start | bytes 1179656 | tf_op jit(solution)/shard_map/ppermute | solution.py:85
  565.1 17.8 %collective-permute-start.31 = (bf16[96,2048]{1,0:T(8,128)(2,1)S(1)}, bf16[96,2048]{1,0:T(8,128)(2,1)S(1)}, u32[]{:S(2)}, u32[]{:S(2)}) collective-permute-start(bf16[96,2048]{1,0:T(8,128)(2,1)S(1)} %get-tuple-element.327), channel_id=1, source_target_pairs={{0,1},{1,0},{2,3},{3,2},{4,5},{5,4},{6,7},{7,6},{8,9},{9,8},{10,11... | collective-permute-start | bytes 1179656 | tf_op jit(solution)/shard_map/ppermute | solution.py:85
  565.1 29.9 %collective-permute-start.32 = (bf16[96,2048]{1,0:T(8,128)(2,1)S(1)}, bf16[96,2048]{1,0:T(8,128)(2,1)S(1)}, u32[]{:S(2)}, u32[]{:S(2)}) collective-permute-start(bf16[96,2048]{1,0:T(8,128)(2,1)S(1)} %get-tuple-element.326), channel_id=1, source_target_pairs={{0,2},{1,3},{2,0},{3,1},{4,6},{5,7},{6,4},{7,5},{8,10},{9,11},{10,... | collective-permute-start | bytes 1179656 | tf_op jit(solution)/shard_map/ppermute | solution.py:85
  568.1 26.9 %collective-permute-start.33 = (bf16[96,2048]{1,0:T(8,128)(2,1)S(1)}, bf16[96,2048]{1,0:T(8,128)(2,1)S(1)}, u32[]{:S(2)}, u32[]{:S(2)}) collective-permute-start(bf16[96,2048]{1,0:T(8,128)(2,1)S(1)} %get-tuple-element.325), channel_id=1, source_target_pairs={{0,3},{1,2},{2,1},{3,0},{4,7},{5,6},{6,5},{7,4},{8,11},{9,10},{10,... | collective-permute-start | bytes 1179656 | tf_op jit(solution)/shard_map/ppermute | solution.py:85
  612.6 452.2 %reduce-scatter.6.cloned.1.call-start = ((), (), s32[]{:S(2)}) async-start(), calls=%async_computation.8 | async-start | bytes 28835840 | tf_op jit(solution)/shard_map/reduce_scatter | solution.py:98
  729.8 449.4 %reduce-scatter.8.cloned.1.call-start = ((), (), s32[]{:S(2)}) async-start(), calls=%async_computation.9 | async-start | bytes 13762560 | tf_op jit(solution)/shard_map/reduce_scatter | solution.py:98
  766.8 14.0 %collective-permute-start.38 = (bf16[96,2048]{1,0:T(8,128)(2,1)S(1)}, bf16[96,2048]{1,0:T(8,128)(2,1)S(1)}, u32[]{:S(2)}, u32[]{:S(2)}) collective-permute-start(bf16[96,2048]{1,0:T(8,128)(2,1)S(1)} %get-tuple-element.321), channel_id=1, source_target_pairs={{0,3},{1,2},{2,1},{3,0},{4,7},{5,6},{6,5},{7,4},{8,11},{9,10},{10,... | collective-permute-start | bytes 1179656 | tf_op jit(solution)/shard_map/ppermute | solution.py:85
  770.2 34.0 %collective-permute-start.37 = (bf16[96,2048]{1,0:T(8,128)(2,1)S(1)}, bf16[96,2048]{1,0:T(8,128)(2,1)S(1)}, u32[]{:S(2)}, u32[]{:S(2)}) collective-permute-start(bf16[96,2048]{1,0:T(8,128)(2,1)S(1)} %get-tuple-element.322), channel_id=1, source_target_pairs={{0,2},{1,3},{2,0},{3,1},{4,6},{5,7},{6,4},{7,5},{8,10},{9,11},{10,... | collective-permute-start | bytes 1179656 | tf_op jit(solution)/shard_map/ppermute | solution.py:85
  770.2 34.0 %collective-permute-start.36 = (bf16[96,2048]{1,0:T(8,128)(2,1)S(1)}, bf16[96,2048]{1,0:T(8,128)(2,1)S(1)}, u32[]{:S(2)}, u32[]{:S(2)}) collective-permute-start(bf16[96,2048]{1,0:T(8,128)(2,1)S(1)} %get-tuple-element.323), channel_id=1, source_target_pairs={{0,1},{1,0},{2,3},{3,2},{4,5},{5,4},{6,7},{7,6},{8,9},{9,8},{10,11... | collective-permute-start | bytes 1179656 | tf_op jit(solution)/shard_map/ppermute | solution.py:85
  808.1 17.7 %collective-permute-start.39 = (bf16[96,2048]{1,0:T(8,128)(2,1)S(1)}, bf16[96,2048]{1,0:T(8,128)(2,1)S(1)}, u32[]{:S(2)}, u32[]{:S(2)}) collective-permute-start(bf16[96,2048]{1,0:T(8,128)(2,1)S(1)} %get-tuple-element.319), channel_id=1, source_target_pairs={{0,1},{1,0},{2,3},{3,2},{4,5},{5,4},{6,7},{7,6},{8,9},{9,8},{10,11... | collective-permute-start | bytes 1179656 | tf_op jit(solution)/shard_map/ppermute | solution.py:85
  808.2 29.9 %collective-permute-start.40 = (bf16[96,2048]{1,0:T(8,128)(2,1)S(1)}, bf16[96,2048]{1,0:T(8,128)(2,1)S(1)}, u32[]{:S(2)}, u32[]{:S(2)}) collective-permute-start(bf16[96,2048]{1,0:T(8,128)(2,1)S(1)} %get-tuple-element.318), channel_id=1, source_target_pairs={{0,2},{1,3},{2,0},{3,1},{4,6},{5,7},{6,4},{7,5},{8,10},{9,11},{10,... | collective-permute-start | bytes 1179656 | tf_op jit(solution)/shard_map/ppermute | solution.py:85
  810.9 27.2 %collective-permute-start.41 = (bf16[96,2048]{1,0:T(8,128)(2,1)S(1)}, bf16[96,2048]{1,0:T(8,128)(2,1)S(1)}, u32[]{:S(2)}, u32[]{:S(2)}) collective-permute-start(bf16[96,2048]{1,0:T(8,128)(2,1)S(1)} %get-tuple-element.317), channel_id=1, source_target_pairs={{0,3},{1,2},{2,1},{3,0},{4,7},{5,6},{6,5},{7,4},{8,11},{9,10},{10,... | collective-permute-start | bytes 1179656 | tf_op jit(solution)/shard_map/ppermute | solution.py:85
  874.3 30.4 %collective-permute-start.45 = (bf16[1024,512]{1,0:T(8,128)(2,1)}, bf16[1024,512]{1,0:T(8,128)(2,1)}, u32[]{:S(2)}, u32[]{:S(2)}) collective-permute-start(bf16[1024,512]{1,0:T(8,128)(2,1)} %bitcast.330), channel_id=1, source_target_pairs={{0,3},{1,2},{2,1},{3,0},{4,7},{5,6},{6,5},{7,4},{8,11},{9,10},{10,... | collective-permute-start | bytes 3145736 | tf_op jit(solution)/shard_map/ppermute | solution.py:85
  881.0 88.1 %collective-permute-start.44 = (bf16[1024,512]{1,0:T(8,128)(2,1)}, bf16[1024,512]{1,0:T(8,128)(2,1)}, u32[]{:S(2)}, u32[]{:S(2)}) collective-permute-start(bf16[1024,512]{1,0:T(8,128)(2,1)} %bitcast.331), channel_id=1, source_target_pairs={{0,2},{1,3},{2,0},{3,1},{4,6},{5,7},{6,4},{7,5},{8,10},{9,11},{10,... | collective-permute-start | bytes 3145736 | tf_op jit(solution)/shard_map/ppermute | solution.py:85
  892.6 76.5 %collective-permute-start.43 = (bf16[1024,512]{1,0:T(8,128)(2,1)}, bf16[1024,512]{1,0:T(8,128)(2,1)}, u32[]{:S(2)}, u32[]{:S(2)}) collective-permute-start(bf16[1024,512]{1,0:T(8,128)(2,1)} %bitcast.332), channel_id=1, source_target_pairs={{0,1},{1,0},{2,3},{3,2},{4,5},{5,4},{6,7},{7,6},{8,9},{9,8},{10,11... | collective-permute-start | bytes 3145736 | tf_op jit(solution)/shard_map/ppermute | solution.py:85
  974.2 11.8 collective-permute-start.46
  988.6 16.8 %collective-permute-start.49 = (bf16[128,2048]{1,0:T(8,128)(2,1)S(1)}, bf16[128,2048]{1,0:T(8,128)(2,1)S(1)}, u32[]{:S(2)}, u32[]{:S(2)}) collective-permute-start(bf16[128,2048]{1,0:T(8,128)(2,1)S(1)} %get-tuple-element.306), channel_id=1, source_target_pairs={{0,3},{1,2},{2,1},{3,0},{4,7},{5,6},{6,5},{7,4},{8,11},{9,10},{10,... | collective-permute-start | bytes 1572872 | tf_op jit(solution)/shard_map/ppermute | solution.py:85
  990.7 44.2 %collective-permute-start.48 = (bf16[128,2048]{1,0:T(8,128)(2,1)S(1)}, bf16[128,2048]{1,0:T(8,128)(2,1)S(1)}, u32[]{:S(2)}, u32[]{:S(2)}) collective-permute-start(bf16[128,2048]{1,0:T(8,128)(2,1)S(1)} %get-tuple-element.307), channel_id=1, source_target_pairs={{0,2},{1,3},{2,0},{3,1},{4,6},{5,7},{6,4},{7,5},{8,10},{9,11},{10,... | collective-permute-start | bytes 1572872 | tf_op jit(solution)/shard_map/ppermute | solution.py:85
  990.7 44.2 %collective-permute-start.47 = (bf16[128,2048]{1,0:T(8,128)(2,1)S(1)}, bf16[128,2048]{1,0:T(8,128)(2,1)S(1)}, u32[]{:S(2)}, u32[]{:S(2)}) collective-permute-start(bf16[128,2048]{1,0:T(8,128)(2,1)S(1)} %get-tuple-element.305), channel_id=1, source_target_pairs={{0,1},{1,0},{2,3},{3,2},{4,5},{5,4},{6,7},{7,6},{8,9},{9,8},{10,11... | collective-permute-start | bytes 1572872 | tf_op jit(solution)/shard_map/ppermute | solution.py:85
  1068.4 40.6 %collective-permute-start.52 = (bf16[256,2816]{1,0:T(8,128)(2,1)}, bf16[256,2816]{1,0:T(8,128)(2,1)}, u32[]{:S(2)}, u32[]{:S(2)}) collective-permute-start(bf16[256,2816]{1,0:T(8,128)(2,1)} %get-tuple-element.290), channel_id=1, source_target_pairs={{0,4},{4,0},{8,12},{12,8},{16,20},{20,16},{24,28},{28,24},{1,5},{5... | collective-permute-start | bytes 4325384 | tf_op jit(solution)/shard_map/ppermute | solution.py:79
  1121.4 32.0 %collective-permute-start.51 = (bf16[256,5632]{1,0:T(8,128)(2,1)}, bf16[256,5632]{1,0:T(8,128)(2,1)}, u32[]{:S(2)}, u32[]{:S(2)}) collective-permute-start(bf16[256,5632]{1,0:T(8,128)(2,1)} %get-tuple-element.280), channel_id=1, source_target_pairs={{0,4},{4,0},{8,12},{12,8},{16,20},{20,16},{24,28},{28,24},{1,5},{5... | collective-permute-start | bytes 8650760 | tf_op jit(solution)/shard_map/ppermute | solution.py:79
  1183.8 24.1 %collective-permute-start.50 = (bf16[256,2048]{0,1:T(8,128)(2,1)}, bf16[256,2048]{0,1:T(8,128)(2,1)}, u32[]{:S(2)}, u32[]{:S(2)}) collective-permute-start(bf16[256,2048]{0,1:T(8,128)(2,1)} %get-tuple-element.303), channel_id=1, source_target_pairs={{0,4},{4,0},{8,12},{12,8},{16,20},{20,16},{24,28},{28,24},{1,5},{5... | collective-permute-start | bytes 3145736 | tf_op jit(solution)/shard_map/ppermute | solution.py:79
  1185.2 15.2 %collective-permute-start.55 = (bf16[2,64,640]{2,1,0:T(8,128)(2,1)S(1)}, bf16[2,64,640]{2,1,0:T(8,128)(2,1)S(1)}, u32[]{:S(2)}, u32[]{:S(2)}) collective-permute-start(bf16[2,64,640]{2,1,0:T(8,128)(2,1)S(1)} %get-tuple-element.365), channel_id=1, source_target_pairs={{0,2},{1,3},{2,0},{3,1},{4,6},{5,7},{6,4},{7,5},{8,10},{9,11},{10,... | collective-permute-start | bytes 491528 | tf_op jit(solution)/shard_map/ppermute | solution.py:85
  1185.3 15.1 %collective-permute-start.54 = (bf16[2,64,640]{2,1,0:T(8,128)(2,1)S(1)}, bf16[2,64,640]{2,1,0:T(8,128)(2,1)S(1)}, u32[]{:S(2)}, u32[]{:S(2)}) collective-permute-start(bf16[2,64,640]{2,1,0:T(8,128)(2,1)S(1)} %get-tuple-element.366), channel_id=1, source_target_pairs={{0,1},{1,0},{2,3},{3,2},{4,5},{5,4},{6,7},{7,6},{8,9},{9,8},{10,11... | collective-permute-start | bytes 491528 | tf_op jit(solution)/shard_map/ppermute | solution.py:85
  (140 other events, 2162.6 us)
Sparse Core Ops, SparseCore 0:
  40.6 39.7 all-gather.4
  82.9 87.4 all-gather.6
  172.8 210.4 all-gather.8
  385.6 113.7 all-gather.10
  612.7 117.0 reduce-scatter.3
  732.8 204.7 reduce-scatter.5
  1064.9 106.1 reduce-scatter.7

commit v2 on v1

--- a/solution.py
+++ b/solution.py
@@ -1,6 +1,7 @@
 import jax
 import jax.numpy as jnp
 from jax import lax
+from jax.experimental.layout import Layout, with_layout_constraint
 from jax.sharding import PartitionSpec as P
 
 D = 2048
@@ -108,15 +109,18 @@
     )
 
 
-def stack_rows(core, mine, got):
-    both = jnp.concatenate([mine, mine], axis=0)
-    return lax.dynamic_update_slice_in_dim(both, got, (1 - core) * mine.shape[0], 0)
-
-
 def halves_of(core, whole):
     width = whole.shape[-1] // 2
-    low, high = whole[..., :width], whole[..., width:]
-    return (jnp.where(core == 0, low, high), jnp.where(core == 0, high, low))
+    return tuple(
+        lax.dynamic_slice_in_dim(whole, at * width, width, whole.ndim - 1) for at in (core, 1 - core)
+    )
+
+
+def fill(shape, parts):
+    buffer = jnp.zeros(shape, BF16)
+    for part, row, column in parts:
+        buffer = lax.dynamic_update_slice(buffer, part, (row, column))
+    return buffer
 
 
 def exchange_rows(core, summed):
@@ -167,17 +171,44 @@
     return (grad_values, grad_gain)
 
 
-def send_rows(blocks):
-    got = jnp.concatenate([over_expert(block, bits) for bits, block in enumerate(blocks)])
+def place_rows(blocks, places):
+    rows, width = blocks[0].shape
+    got = jnp.zeros((len(blocks) * rows, width), blocks[0].dtype)
+    for block, place in zip(blocks, places):
+        got = lax.dynamic_update_slice_in_dim(got, block, place * rows, 0)
     return jnp.concatenate([got, core_swap(got)])
 
 
-def return_rows(partial, partners):
+def send_rows(blocks, places=None):
+    blocks = [over_expert(block, bits) for bits, block in enumerate(blocks)]
+    return place_rows(blocks, range(len(blocks)) if places is None else places)
+
+
+def return_rows(partial, partners, places=None, between=()):
     count = partial.shape[0] // 2
     got = core_swap(partial[count:].astype(BF16))
     summed = (partial[:count] + got.astype(F32)).astype(BF16)
-    summed = summed.reshape((partners, count // partners) + summed.shape[1:])
-    return [over_expert(summed[bits], bits) for bits in range(partners)]
+    rows = count // partners
+    places = range(partners) if places is None else places
+    blocks = [lax.dynamic_slice_in_dim(summed, place * rows, rows, 0) for place in places]
+    blocks[-1] = after(blocks[-1], *between)
+    return [over_expert(block, bits) for bits, block in enumerate(blocks)]
+
+
+def over_chips(value, bits):
+    if bits == 0:
+        return value
+    return lax.ppermute(value, "dp", swap_perm(lax.axis_size("dp"), 2 * bits))
+
+
+def gather_small(chip, block):
+    count, rows = lax.axis_size("dp") // 2, block.shape[0]
+    whole = jnp.zeros((count * rows, block.shape[1]), block.dtype)
+    for bits in range(count):
+        whole = lax.dynamic_update_slice_in_dim(
+            whole, over_chips(block, bits), (chip ^ bits) * rows, 0
+        )
+    return whole
 
 
 def rotate(value, cosine, sine):
@@ -187,12 +218,13 @@
 
 
 def by_heads(rows, sequences):
-    return rows.reshape(sequences, -1, rows.shape[1] // HD, HD).transpose(0, 2, 1, 3)
+    heads = rows.shape[1] // HD
+    return rows.reshape(-1, heads, HD).transpose(1, 0, 2).reshape(heads, sequences, -1, HD)
 
 
 def from_heads(blocks):
-    sequences, heads, tokens, _ = blocks.shape
-    return blocks.transpose(0, 2, 1, 3).reshape(sequences * tokens, heads * HD)
+    heads = blocks.shape[0]
+    return blocks.reshape(heads, -1, HD).transpose(1, 0, 2).reshape(-1, heads * HD)
 
 
 def heads_dot(left_side, right_side, left_axis, right_axis):
@@ -204,25 +236,8 @@
     )
 
 
-def xor_blocks(value, axis, bits):
-    count, step = value.shape[axis], 1
-    while step < count:
-        if bits & step:
-            split = value.shape[:axis] + (count // (2 * step), 2, step) + value.shape[axis + 1 :]
-            value = jnp.flip(value.reshape(split), axis + 1).reshape(value.shape)
-        step *= 2
-    return value
-
-
-def partner_columns(expert, rows):
-    width = rows.shape[1] // EXPERTS
-    return jnp.concatenate(
-        [
-            lax.dynamic_slice_in_dim(rows, (expert ^ at) * width, width, 1)
-            for at in range(EXPERTS)
-        ],
-        axis=1,
-    )
+def turned(rows):
+    return with_layout_constraint(rows.T.astype(F32), Layout(major_to_minor=(0, 1)))
 
 
 def all_sum(value):
@@ -239,6 +254,10 @@
 
 def after(value, *others):
     return lax.optimization_barrier((value, *others))[0]
+
+
+def together(*groups):
+    return lax.optimization_barrier(groups)
 
 
 def adam_step(moment, square, gradient):
@@ -281,7 +300,7 @@
 ):
     partners = lax.axis_size("expert")
     halves = partners // EXPERTS
-    core = lax.axis_index("dp") % 2
+    core, chip = lax.axis_index("dp") % 2, lax.axis_index("dp") // 2
     expert_at = lax.axis_index("expert")
     expert, half = expert_at // halves, expert_at % halves
     names = (expert_at ^ jnp.arange(partners, dtype=jnp.int32)) // halves
@@ -293,28 +312,26 @@
     marks = jnp.concatenate([attn_routes, image_mask[:, None]], axis=1).astype(BF16)
     marks = jnp.pad(marks, ((0, 0), (0, LANES - marks.shape[1])))
     payload = jnp.concatenate([tokens, marks], axis=1)
-    everyone = send_rows([payload] * partners)
-
-    query_mine, query_theirs = halves_of(core, master_query.astype(BF16))
+    places = [expert_at ^ bits for bits in range(partners)]
+
+    map_rows = master_query.shape[0]
+    row_mine, row_got = core * map_rows, (1 - core) * map_rows
+    query_mine, query_theirs = halves_of(core, master_query)
     project_mine, project_theirs = halves_of(core, master_project.astype(BF16).T)
-    attn_got = core_swap(jnp.concatenate([query_theirs, project_theirs], axis=1))
-    attn_mine = jnp.concatenate([query_mine, project_mine], axis=1)
     width_attn = query_mine.shape[1]
-
-    def arranged(rows):
-        return jnp.concatenate(
-            [
-                partner_columns(expert, rows[:, :width_attn]),
-                partner_columns(expert, rows[:, width_attn:]),
-            ],
-            axis=1,
-        )
-
-    weight_attn = gather_chips(stack_rows(core, arranged(attn_mine), arranged(attn_got)))
+    attn_rows = fill(
+        (2 * map_rows, 2 * width_attn),
+        [
+            (query_mine.astype(BF16), row_mine, 0),
+            (project_mine, row_mine, width_attn),
+            (core_swap(query_theirs.astype(BF16)), row_got, 0),
+            (core_swap(project_theirs), row_got, width_attn),
+        ],
+    )
+    weight_attn = gather_chips(attn_rows)
     weight_query, weight_project = weight_attn[:, :width_attn], weight_attn[:, width_attn:]
 
     local_rows = master_key_value.shape[0]
-    shared_low = master_key_value.astype(BF16).reshape(local_rows, 2, halves, 2, EXPERTS, sixth)
     small = jnp.concatenate(
         [
             master_router,
@@ -324,30 +341,62 @@
         axis=1,
     ).astype(BF16)
     small = jnp.pad(small, ((0, 0), (0, LANES - small.shape[1])))
-    for_cores = [
-        jnp.concatenate([shared_low[:, :, :, at].reshape(local_rows, -1), small], axis=1)
-        for at in range(2)
-    ]
-    pair = jnp.stack(
+    half_width = EXPERTS * sixth
+
+    def for_core(at):
+        return jnp.concatenate(
+            [
+                lax.dynamic_slice_in_dim(
+                    master_key_value, side * QW + (2 * part + at) * half_width, half_width, 1
+                )
+                for side in range(2)
+                for part in range(halves)
+            ],
+            axis=1,
+        ).astype(BF16)
+
+    kv_mine = jnp.concatenate([for_core(core), small], axis=1)
+    kv_got = core_swap(jnp.concatenate([for_core(1 - core), small], axis=1))
+
+    def block_for(rows, bits):
+        other = expert_at ^ bits
+        column = ((other % halves) * EXPERTS + other // halves) * sixth
+        return jnp.concatenate(
+            [
+                lax.dynamic_slice_in_dim(rows, column, sixth, 1),
+                lax.dynamic_slice_in_dim(rows, halves * half_width + column, sixth, 1),
+                rows[:, 2 * halves * half_width :],
+            ],
+            axis=1,
+        )
+
+    kv_pair = in_core_order(core, kv_mine, kv_got, 0)
+    kv_blocks = [block_for(kv_pair, bits) for bits in range(partners)]
+
+    width_ff = master_gate_up.shape[2] // 2
+    kv_blocks = [over_expert(block, bits) for bits, block in enumerate(kv_blocks)]
+    kv_blocks, payload = together(kv_blocks, payload)
+    token_blocks = [over_expert(payload, bits) for bits in range(partners)]
+    arrived = jnp.zeros((2 * partners * local_rows, 2 * sixth + LANES), BF16)
+    for block, at in zip(kv_blocks, places):
+        arrived = lax.dynamic_update_slice_in_dim(arrived, block, at * 2 * local_rows, 0)
+    arrived = arrived.reshape(partners, 2, local_rows, -1).transpose(1, 0, 2, 3)
+    arrived = arrived.reshape(2 * partners * local_rows, -1)
+    arrived, master_gate_up, _ = together(arrived, master_gate_up, attn_rows)
+    gate_mine, gate_theirs = halves_of(core, master_gate_up[0])
+    up_mine, up_theirs = halves_of(core, master_gate_up[1])
+    gate_up_rows = fill(
+        (2 * map_rows, 2 * width_ff),
         [
-            jnp.where(core == 0, for_cores[0], for_cores[1]),
-            core_swap(jnp.where(core == 0, for_cores[1], for_cores[0])),
-        ]
-    )
-    pair_kv = pair[:, :, :-LANES].reshape(2, local_rows, 2, halves * EXPERTS, sixth)
-
-    def block_for(bits):
-        other = expert_at ^ bits
-        column = (other % halves) * EXPERTS + other // halves
-        picked = lax.dynamic_index_in_dim(pair_kv, column, 3, keepdims=False)
-        return jnp.concatenate([picked.reshape(2, local_rows, -1), pair[:, :, -LANES:]], axis=2)
-
-    arrived = jnp.stack([over_expert(block_for(bits), bits) for bits in range(partners)])
-    arrived = jnp.stack(
-        [lax.dynamic_index_in_dim(arrived, expert_at ^ at, 0, keepdims=False) for at in range(partners)]
-    )
-    arrived = jnp.where(core == 0, arrived, arrived[:, ::-1]).transpose(1, 0, 2, 3)
-    shared_whole = gather_chips(arrived.reshape(2 * partners * local_rows, -1))
+            (gate_mine.astype(BF16), row_mine, 0),
+            (up_mine.astype(BF16), row_mine, width_ff),
+            (core_swap(gate_theirs.astype(BF16)), row_got, 0),
+            (core_swap(up_theirs.astype(BF16)), row_got, width_ff),
+        ],
+    )
+    shared_whole = gather_small(chip, arrived)
+    shared_whole, token_blocks, _ = together(shared_whole, token_blocks, gate_up_rows)
+    everyone = place_rows(token_blocks, places)
     kv_weight = shared_whole[:, : 2 * sixth]
     small_whole = shared_whole[:, 2 * sixth :]
     router_low = small_whole[:, : 2 * EXPERTS]
@@ -355,22 +404,23 @@
     gains_f = small_whole[:, 2 * EXPERTS : 2 * EXPERTS + 2].astype(F32).T
     total_count = jnp.sum(small_whole[:, 2 * EXPERTS + 2].astype(F32)) / local_rows
 
-    width_ff = master_gate_up.shape[2] // 2
-    gate_mine, gate_theirs = halves_of(core, master_gate_up[0].astype(BF16))
-    up_mine, up_theirs = halves_of(core, master_gate_up[1].astype(BF16))
-    gate_up_got = core_swap(jnp.concatenate([gate_theirs, up_theirs], axis=1))
-    weight_gate_up = gather_chips(
-        stack_rows(core, jnp.concatenate([gate_mine, up_mine], axis=1), gate_up_got)
-    )
+    weight_gate_up = gather_chips(gate_up_rows)
     down_mine, down_theirs = halves_of(core, master_down.astype(BF16).T)
-    weight_down = gather_chips(stack_rows(core, down_mine, core_swap(down_theirs)))
+    down_rows = fill(
+        (2 * map_rows, width_ff),
+        [(down_mine, row_mine, 0), (core_swap(down_theirs), row_got, 0)],
+    )
+    weight_down = gather_chips(down_rows)
 
     tables = rope_tables(token_count)
     inputs_all = everyone[:, :D].astype(F32)
     inverse_all = lax.rsqrt(jnp.mean(inputs_all * inputs_all, axis=-1, keepdims=True) + NORM_EPS)
     normed_all = (inputs_all * inverse_all * gains_f[0]).astype(BF16)
     inputs_f = tokens.astype(F32)
-    inverse_one, normed_one = inverse_all[:token_count], normed_all[:token_count]
+    inverse_one, normed_one = (
+        lax.dynamic_slice_in_dim(table, expert_at * token_count, token_count, 0)
+        for table in (inverse_all, normed_all)
+    )
     marks_all = everyone[:, D:].astype(F32).reshape(sequences, token_count, LANES)
     named_all = jnp.any(marks_all[:, :, :TOP] == expert.astype(F32), axis=2)
     slot_all = slots_before(named_all[:, :, None])[:, :, 0]
@@ -382,24 +432,26 @@
         image_on[:, :, None] & image_on[:, None, :]
     )
 
-    def regroup(rows, bits):
-        blocks = rows.reshape((2, partners, token_count) + rows.shape[1:])
-        return xor_blocks(blocks, 1, bits).reshape(rows.shape)
-
-    kv_proj = matmul(normed_all, kv_weight)
-    key_own = rotate(by_heads(kv_proj[:, :sixth], sequences), *tables).astype(BF16)
-    kv_own = jnp.concatenate([from_heads(key_own), kv_proj[:, sixth:].astype(BF16)], axis=1)
-    kv_shared = [
-        regroup(over_expert(kv_own, step * halves), step * halves) for step in range(EXPERTS)
-    ]
-    key_heads = by_heads(jnp.concatenate([part[:, :sixth] for part in kv_shared], axis=1), sequences)
-    value_heads = by_heads(
-        jnp.concatenate([part[:, sixth:] for part in kv_shared], axis=1), sequences
+    kv_heads = by_heads(matmul(normed_all, kv_weight), sequences)
+    count = sixth // HD
+    kv_own = jnp.concatenate(
+        [rotate(kv_heads[:count], *tables).astype(BF16), kv_heads[count:].astype(BF16)]
     )
     query_pre = matmul(normed_all, weight_query)
     query_heads = rotate(by_heads(query_pre, sequences), *tables).astype(BF16)
+    kv_shared = [over_expert(kv_own, step * halves) for step in range(EXPERTS - 1)]
+    kv_shared.append(over_expert(after(kv_own, query_heads, down_rows), (EXPERTS - 1) * halves))
+
+    def every_head(parts):
+        whole = jnp.zeros((EXPERTS * count,) + parts[0].shape[1:], BF16)
+        for step, part in enumerate(parts):
+            whole = lax.dynamic_update_slice_in_dim(whole, part, (expert ^ step) * count, 0)
+        return whole
+
+    key_heads = every_head([part[:count] for part in kv_shared])
+    value_heads = every_head([part[count:] for part in kv_shared])
     scores = heads_dot(query_heads, key_heads, 3, 3) * SCALE
-    scores = jnp.where(allowed[:, None], scores, MASK_FILL)
+    scores = jnp.where(allowed[None], scores, MASK_FILL)
     probs = jax.nn.softmax(scores, axis=-1)
     probs_low = probs.astype(BF16)
     attended_all = from_heads(heads_dot(probs_low, value_heads, 3, 2).astype(BF16))
@@ -416,7 +468,7 @@
     attn_pick, attn_back, attn_hit = route_tables(attn_routes, names)
     gates_attn = chosen_gates(matmul(normed_one, router_low[:, :EXPERTS]), attn_routes)
     branch_rows = jnp.concatenate(
-        return_rows(matmul_back(attended, weight_project), partners)
+        return_rows(matmul_back(attended, weight_project), partners, places)
     )
     branch = [matmul(attn_back[choice], branch_rows) for choice in range(TOP)]
     hidden = inputs_f + sum(gates_attn[:, choice, None] * branch[choice] for choice in range(TOP))
@@ -439,11 +491,11 @@
     total_error = all_sum(local_error.reshape(1, 1))[0, 0]
     grad_out = 2.0 * valid_f[:, None] * deviation / total_count
 
-    def send_grads(pick, gates, hit, grad):
+    def send_grads(pick, gates, hit, grad, where=None):
         gate_of = jnp.sum(gates[:, :, None] * hit, axis=1)
         rows = (gate_of.T[:, :, None] * grad[None]).astype(BF16)
         sent = jnp.einsum("kct,ktd->kcd", pick, rows, preferred_element_type=F32).astype(BF16)
-        return send_rows(list(sent))
+        return send_rows(list(sent), where)
 
     rows_grad = send_grads(mlp_pick, gates_mlp, mlp_hit, grad_out)
     grad_down = matmul_rows(rows_grad, active).astype(BF16)
@@ -456,10 +508,10 @@
     grad_both = jnp.concatenate([grad_gate, grad_up], axis=1)
     down_sum = scatter_chips(grad_down)
     grad_gate_up = matmul_rows(rows_two, grad_both).astype(BF16)
-    gate_up_sum = scatter_chips(after(grad_gate_up, down_sum))
     normed_two_rows = return_rows(
         matmul_back(after(grad_both, grad_down), weight_gate_up), partners
     )
+    gate_up_sum = scatter_chips(after(grad_gate_up, down_sum, *normed_two_rows))
     grad_gates_mlp = jnp.stack(
         [jnp.sum(grad_out * mlp_branch[choice], axis=-1) for choice in range(TOP)], axis=1
     )
@@ -471,7 +523,7 @@
     grad_hidden = grad_out + grad_hidden_norm
     grad_router_two = exact_rows(normed_two.astype(F32), grad_logits_mlp)
 
-    rows_grad_attn = send_grads(attn_pick, gates_attn, attn_hit, after(grad_hidden, down_sum))
+    rows_grad_attn = send_grads(attn_pick, gates_attn, attn_hit, grad_hidden, places)
     grad_project = matmul_rows(rows_grad_attn, attended).astype(BF16)
     grad_attended = matmul(rows_grad_attn, weight_project).astype(BF16)
     grad_gates_attn = jnp.stack(
@@ -487,34 +539,36 @@
     grad_value_heads = heads_dot(probs_low, grad_heads, 2, 2)
     back_tables = (tables[0], -tables[1])
     grad_query_pre = from_heads(rotate(grad_query_heads, *back_tables).astype(BF16))
-    grad_keys = from_heads(rotate(grad_key_heads, *back_tables).astype(BF16))
-    grad_values = from_heads(grad_value_heads.astype(BF16))
+    grad_keys = rotate(grad_key_heads, *back_tables).astype(BF16)
+    grad_values = grad_value_heads.astype(BF16)
     grad_query = matmul_rows(normed_all, grad_query_pre).astype(BF16)
+    down_mine, down_other = exchange_rows(core, down_sum)
+    reduced_down = turned(in_core_order(core, down_mine, down_other, 1))
+    update_down = adam_step(moment_down, square_down, reduced_down)
+
+    def heads_of(step):
+        start = (expert ^ step) * count
+        return jnp.concatenate(
+            [
+                lax.dynamic_slice_in_dim(table, start, count, 0)
+                for table in (grad_keys, grad_values)
+            ]
+        )
+
+    grad_kv_parts = [heads_of(step) for step in range(EXPERTS)]
+    grad_kv_parts[-1] = after(grad_kv_parts[-1], grad_query, total_error, *update_down)
     grad_kv = sum(
-        over_expert(
-            regroup(
-                jnp.concatenate(
-                    [
-                        grad_keys[:, step * sixth : (step + 1) * sixth],
-                        grad_values[:, step * sixth : (step + 1) * sixth],
-                    ],
-                    axis=1,
-                ),
-                step * halves,
-            ),
-            step * halves,
-        ).astype(F32)
-        for step in range(EXPERTS)
+        over_expert(part, step * halves).astype(F32) for step, part in enumerate(grad_kv_parts)
     ).astype(BF16)
+    grad_kv = from_heads(grad_kv)
     grad_kv_weight = matmul_rows(normed_all, grad_kv).astype(BF16)
-    normed_one_rows = return_rows(
-        matmul_back(grad_query_pre, weight_query) + matmul_back(grad_kv, kv_weight), partners
-    )
-    grad_normed_one = sum(rows.astype(F32) for rows in normed_one_rows) + exact_back(
-        grad_logits_attn, router_f[:, :EXPERTS]
-    )
-    grad_inputs_norm, grad_gain_one = norm_back(inputs_f, inverse_one, gains_f[0], grad_normed_one)
-    input_grad = grad_hidden + grad_inputs_norm
+    normed_one_partial = matmul_back(grad_query_pre, weight_query) + matmul_back(
+        grad_kv, kv_weight
+    )
+    grad_normed_router = exact_back(grad_logits_attn, router_f[:, :EXPERTS])
+    grad_gain_one = jnp.sum(normed_one_partial * inputs_all * inverse_all, axis=0) + jnp.sum(
+        grad_normed_router * inputs_f * inverse_one, axis=0
+    )
     grad_small = jnp.concatenate(
         [
             exact_rows(normed_one.astype(F32), grad_logits_attn),
@@ -525,50 +579,17 @@
         axis=1,
     ).astype(BF16)
     grad_small = jnp.pad(grad_small, ((0, 0), (0, LANES - grad_small.shape[1])))
-
-    attn_sum = scatter_chips(
-        after(
-            jnp.concatenate([grad_query, grad_project, grad_kv_weight, grad_small], axis=1),
-            gate_up_sum,
-        )
-    )
-    down_mine, down_other = exchange_rows(core, down_sum)
+    last_rows = fill(
+        (grad_query.shape[0], 2 * width_attn + 2 * sixth + LANES),
+        [
+            (grad_project, 0, width_attn),
+            (grad_query, 0, 0),
+            (grad_kv_weight, 0, 2 * width_attn),
+            (grad_small, 0, 2 * width_attn + 2 * sixth),
+        ],
+    )
+    last_sum = scatter_chips(after(last_rows, gate_up_sum))
     gate_up_mine, gate_up_other = exchange_rows(core, gate_up_sum)
-    attn_mine, attn_other = exchange_rows(core, attn_sum[:, : 2 * width_attn])
-    attn_mine, attn_other = arranged(attn_mine), arranged(attn_other)
-    shared_sum = attn_sum[:, 2 * width_attn :]
-    shared_sum = shared_sum.reshape(2, partners, local_rows, -1)
-    shared_mine = jnp.where(core == 0, shared_sum[0], shared_sum[1])
-    shared_theirs = core_swap(jnp.where(core == 0, shared_sum[1], shared_sum[0]))
-    shared_pair = jnp.where(
-        core == 0, jnp.stack([shared_mine, shared_theirs]), jnp.stack([shared_theirs, shared_mine])
-    )
-    received = jnp.stack(
-        [
-            over_expert(lax.dynamic_index_in_dim(shared_pair, expert_at ^ bits, 1, keepdims=False), bits)
-            for bits in range(partners)
-        ]
-    )
-    small_sum = jnp.sum(received[..., -LANES:].astype(F32), axis=(0, 1))
-    received = jnp.stack(
-        [lax.dynamic_index_in_dim(received, expert_at ^ at, 0, keepdims=False) for at in range(partners)]
-    )
-    reduced_kv = (
-        received[..., :-LANES]
-        .reshape(EXPERTS, halves, 2, local_rows, 2, sixth)
-        .transpose(3, 4, 1, 2, 0, 5)
-        .reshape(local_rows, -1)
-        .astype(F32)
-    )
-    reduced_router = small_sum[:, : 2 * EXPERTS]
-    reduced_gains = small_sum[:, 2 * EXPERTS : 2 * EXPERTS + 2].T
-    reduced_query = in_core_order(
-        core, attn_mine[:, :width_attn], attn_other[:, :width_attn], 1
-    ).astype(F32)
-    reduced_project = after(
-        in_core_order(core, attn_mine[:, width_attn:], attn_other[:, width_attn:], 1).T
-    ).astype(F32)
-    reduced_down = after(in_core_order(core, down_mine, down_other, 1).T).astype(F32)
     reduced_gate_up = jnp.stack(
         [
             in_core_order(
@@ -579,7 +600,52 @@
             )
             for at in range(2)
         ]
+    )
+    reduced_gate_up = with_layout_constraint(
+        reduced_gate_up, Layout(major_to_minor=(0, 1, 2))
     ).astype(F32)
+    update_gate_up = adam_step(moment_gate_up, square_gate_up, reduced_gate_up)
+    normed_one_rows = return_rows(
+        after(normed_one_partial, last_rows), partners, places, update_gate_up
+    )
+    grad_normed_one = sum(rows.astype(F32) for rows in normed_one_rows) + grad_normed_router
+    grad_inputs_norm, _ = norm_back(inputs_f, inverse_one, gains_f[0], grad_normed_one)
+    input_grad = grad_hidden + grad_inputs_norm
+
+    last_mine, last_other = exchange_rows(core, last_sum)
+    attn_mine, attn_other = last_mine[:, : 2 * width_attn], last_other[:, : 2 * width_attn]
+    shared_mine, shared_theirs = [
+        rows[:, 2 * width_attn :].reshape(partners, local_rows, -1)
+        for rows in (last_mine, last_other)
+    ]
+    shared_pair = jnp.where(
+        core == 0, jnp.stack([shared_mine, shared_theirs]), jnp.stack([shared_theirs, shared_mine])
+    )
+    received = jnp.stack(
+        [
+            over_expert(lax.dynamic_index_in_dim(shared_pair, expert_at ^ bits, 1, keepdims=False), bits)
+            for bits in range(partners)
+        ]
+    )
+    query_mine, project_mine = attn_mine[:, :width_attn], attn_mine[:, width_attn:]
+    query_other, project_other = attn_other[:, :width_attn], attn_other[:, width_attn:]
+    small_sum = jnp.sum(received[..., -LANES:].astype(F32), axis=(0, 1))
+    received = jnp.stack(
+        [lax.dynamic_index_in_dim(received, expert_at ^ at, 0, keepdims=False) for at in range(partners)]
+    )
+    reduced_kv = (
+        received[..., :-LANES]
+        .reshape(EXPERTS, halves, 2, local_rows, 2, sixth)
+        .transpose(3, 4, 1, 2, 0, 5)
+        .reshape(local_rows, -1)
+        .astype(F32)
+    )
+    reduced_router = small_sum[:, : 2 * EXPERTS]
+    reduced_gains = small_sum[:, 2 * EXPERTS : 2 * EXPERTS + 2].T
+    reduced_query = with_layout_constraint(
+        in_core_order(core, query_mine, query_other, 1), Layout(major_to_minor=(0, 1))
+    ).astype(F32)
+    reduced_project = turned(in_core_order(core, project_mine, project_other, 1))
     loss_value = total_error / total_count
     return (
         outputs,
@@ -587,8 +653,8 @@
         input_grad,
         *adam_step(moment_query, square_query, reduced_query),
         *adam_step(moment_project, square_project, reduced_project),
-        *adam_step(moment_gate_up, square_gate_up, reduced_gate_up),
-        *adam_step(moment_down, square_down, reduced_down),
+        *update_gate_up,
+        *update_down,
         *adam_step(moment_key_value, square_key_value, reduced_kv),
         *adam_step(moment_router, square_router, reduced_router),
         *adam_step(moment_gains, square_gains, reduced_gains),

time: 1250 us -> 1080 us (0.86)
  waiting for transfers between devices: 576 us -> 423 us
  other arithmetic: 180 us -> 121 us
  matrix products: 178 us -> 216 us
  starting transfers between devices: 79.3 us -> 116 us
  local copies, waits for them, and re-layouts: 202 us -> 177 us
    ppermute x38, waiting for transfers between devices: 404 us -> 214 us  [over_expert(): lax.ppermute(value, 'expert', swap_perm(lax.axis_size('expert'), bits))]
    unnamed x324 -> x266, local copies, waits for them, and re-layouts: 116 us -> 33.5 us
    concatenate x16 -> x6, other arithmetic: 61.7 us -> 4.4 us  [the longest x3 3.18 us: heads_of(): jnp.concatenate([lax.dynamic_slice_in_dim(table, start, count, 0) for tab...]
    ppermute x0 -> x3, waiting for transfers between devices: none -> 35.5 us  [over_chips(): return lax.ppermute(value, 'dp', swap_perm(lax.axis_size('dp'), 2 * bits))]
    ppermute x38, starting transfers between devices: 70.6 us -> 103 us  [over_expert(): lax.ppermute(value, 'expert', swap_perm(lax.axis_size('expert'), bits))]
    dynamic_update_slice x3 -> x42, local copies, waits for them, and re-layouts: 5.17 us -> 36 us  [the longest x11 21.7 us: fill(): buffer = lax.dynamic_update_slice(buffer, part, (row, column))]
    rev x7 -> x0, local copies, waits for them, and re-layouts: 21.8 us -> none  [xor_blocks(): value = jnp.flip(value.reshape(split), axis + 1).reshape(value.shape)]
    convert_element_type x2 -> x9, local copies, waits for them, and re-layouts: 1.74 us -> 22.5 us  [the longest x1 6.3 us: turned(): rows.T.astype(F32)]
  transfers between devices with their start and end apart: 64 -> 67, of which waited for: 39 -> 34; matrix products, arithmetic and copies ran while one was open for 37% -> 40% of each run, Pallas kernels for 0% -> 0%
where the time goes in v2:
time: 1080 us
  waiting for transfers between devices  423 us (39%)
  matrix products  216 us (20%)
  local copies, waits for them, and re-layouts  177 us (16%)
  other arithmetic  121 us (11%)
  starting transfers between devices  116 us (11%)
  between operations  22.6 us (2%)
    ppermute x38, waiting for transfers between devices, over_expert(): lax.ppermute(value, 'expert', swap_perm(lax.axis_size('expert'), bits))  214 us
    ppermute x38, starting transfers between devices, over_expert(): lax.ppermute(value, 'expert', swap_perm(lax.axis_size('expert'), bits))  103 us
    reduce_scatter x3, waiting for transfers between devices, scatter_chips(): lax.psum_scatter(partial, 'dp', scatter_dimension=0, tiled=True, axis_ind...  87 us
    dot_general x13, matrix products, matmul(): return jnp.dot(left_side, right_side, preferred_element_type=F32)  71.1 us
    all_gather x3, waiting for transfers between devices, gather_chips(): lax.all_gather(block, 'dp', axis=0, tiled=True, axis_index_groups=chip_gr...  70.7 us
    dot_general x5, matrix products, matmul_back(): lax.dot_general(left_side, right_side, (((1,), (1,)), ((), ())), preferre...  59 us
    dot_general x5, matrix products, matmul_rows(): lax.dot_general(left_side, right_side, (((0,), (0,)), ((), ())), preferre...  54.8 us
    div x7, other arithmetic, adam_step(): direction = moment_hat / (jnp.sqrt(square_hat) + ADAM_EPS)  49.6 us
  transfers between devices with their start and end apart: 67, of which 34 were waited for; matrix products, arithmetic and copies ran while one was open for 40% of the time, Pallas kernels for 0%

profile of v2, /device:TPU:0, one launch (start us, length us, event | category | flops | bytes accessed | tf_op | source)
XLA Modules:
  0.0 1075.6 jit_solution(6014206226882021362)
XLA Ops:
  33.3 7.7 collective-permute-done.2
  41.3 5.0 fusion.149
  74.2 16.9 %collective-permute-done.6 = bf16[512,640]{1,0:T(8,128)(2,1)S(1)} collective-permute-done((bf16[512,640]{1,0:T(8,128)(2,1)S(1)}, bf16[512,640]{1,0:T(8,128)(2,1)S(1)}, u32[]{:S(2)}, u32[]{:S(2)}) %collective-permute-start.6) | collective-permute-done | bytes 655392 | tf_op jit(solution)/shard_map/ppermute | solution.py:201
  100.8 18.6 %collective-permute-done.8 = bf16[512,640]{1,0:T(8,128)(2,1)} collective-permute-done((bf16[512,640]{1,0:T(8,128)(2,1)S(1)}, bf16[512,640]{1,0:T(8,128)(2,1)}, u32[]{:S(2)}, u32[]{:S(2)}) %collective-permute-start.8) | collective-permute-done | bytes 655392 | tf_op jit(solution)/shard_map/ppermute | solution.py:201
  172.8 10.0 fusion.20
  182.8 5.5 copy.341
  188.3 5.1 fusion.152
  198.9 12.0 %collective-permute-done.15 = bf16[4,8,128,128]{3,2,1,0:T(8,128)(2,1)} collective-permute-done((bf16[4,8,128,128]{3,2,1,0:T(8,128)(2,1)}, bf16[4,8,128,128]{3,2,1,0:T(8,128)(2,1)}, u32[]{:S(2)}, u32[]{:S(2)}) %collective-permute-start.15) | collective-permute-done | bytes 1048608 | tf_op jit(solution)/shard_map/ppermute | solution.py:86
  213.3 22.8 %collective-permute-done.16 = bf16[4,8,128,128]{3,2,1,0:T(8,128)(2,1)} collective-permute-done((bf16[4,8,128,128]{3,2,1,0:T(8,128)(2,1)}, bf16[4,8,128,128]{3,2,1,0:T(8,128)(2,1)}, u32[]{:S(2)}, u32[]{:S(2)}) %collective-permute-start.16) | collective-permute-done | bytes 1048608 | tf_op jit(solution)/shard_map/ppermute | solution.py:86
  253.5 5.4 fusion.165
  259.0 4.5 convolution_convert_fusion.12
  269.6 6.0 fusion.17
  287.8 9.1 collective-permute-start.21
  297.5 25.4 %collective-permute-done.21 = bf16[96,2048]{1,0:T(8,128)(2,1)S(1)} collective-permute-done((bf16[96,2048]{1,0:T(8,128)(2,1)S(1)}, bf16[96,2048]{1,0:T(8,128)(2,1)S(1)}, u32[]{:S(2)}, u32[]{:S(2)}) %collective-permute-start.21) | collective-permute-done | bytes 393248 | tf_op jit(solution)/shard_map/ppermute | solution.py:86
  330.8 13.8 %collective-permute-done.23 = bf16[96,2048]{1,0:T(8,128)(2,1)S(1)} collective-permute-done((bf16[96,2048]{1,0:T(8,128)(2,1)S(1)}, bf16[96,2048]{1,0:T(8,128)(2,1)S(1)}, u32[]{:S(2)}, u32[]{:S(2)}) %collective-permute-start.23) | collective-permute-done | bytes 393248 | tf_op jit(solution)/shard_map/ppermute | solution.py:86
  344.6 12.3 %collective-permute-done.24 = bf16[96,2048]{1,0:T(8,128)(2,1)S(1)} collective-permute-done((bf16[96,2048]{1,0:T(8,128)(2,1)S(1)}, bf16[96,2048]{1,0:T(8,128)(2,1)S(1)}, u32[]{:S(2)}, u32[]{:S(2)}) %collective-permute-start.24) | collective-permute-done | bytes 393248 | tf_op jit(solution)/shard_map/ppermute | solution.py:86
  360.7 24.0 %fusion.37 = f32[768,5632]{1,0:T(8,128)S(1)} fusion(bf16[2048,5632]{1,0:T(8,128)(2,1)} %all-gather.6.cloned.1.call-done, bf16[384,2048]{1,0:T(8,128)(2,1)} %collective-permute-done.26, bf16[384,2048]{1,0:T(8,128)(2,1)S(1)} %constant_dynamic-update-slice_fusion.7), kind=kOutput, calls=%fused_computation.107 | convolution fusion | flops 17723031552 | bytes 43515904 | tf_op jit(solution)/shard_map/dot_general | solution.py:29
  384.6 5.9 copy-done.1
  394.6 70.7 %all-gather.8.cloned.1.call-done = bf16[2048,2816]{0,1:T(8,128)(2,1)} async-done(((bf16[512,2816]{0,1:T(8,128)(2,1)}), bf16[2048,2816]{0,1:T(8,128)(2,1)}) %all-gather.8.cloned.1.call-update) | async-done | bytes 11534352 | tf_op jit(solution)/shard_map/all_gather | solution.py:95
  465.3 13.6 %fusion.168 = f32[768,2048]{1,0:T(8,128)S(1)} fusion(bf16[768,2816]{1,0:T(8,128)(2,1)} %multiply_convert_fusion.2, bf16[2048,2816]{0,1:T(8,128)(2,1)} %all-gather.8.cloned.1.call-done), kind=kOutput, calls=%fused_computation.436 | convolution fusion | flops 8858370048 | bytes 22151168 | tf_op jit(solution)/shard_map/dot_general | solution.py:33
  493.0 9.5 collective-permute-done.30
  502.5 23.5 %collective-permute-done.29 = bf16[96,2048]{1,0:T(8,128)(2,1)S(1)} collective-permute-done((bf16[96,2048]{1,0:T(8,128)(2,1)S(1)}, bf16[96,2048]{1,0:T(8,128)(2,1)S(1)}, u32[]{:S(2)}, u32[]{:S(2)}) %collective-permute-start.29) | collective-permute-done | bytes 393248 | tf_op jit(solution)/shard_map/ppermute | solution.py:86
  533.9 13.3 %collective-permute-done.36 = bf16[96,2048]{1,0:T(8,128)(2,1)S(1)} collective-permute-done((bf16[96,2048]{1,0:T(8,128)(2,1)S(1)}, bf16[96,2048]{1,0:T(8,128)(2,1)S(1)}, u32[]{:S(2)}, u32[]{:S(2)}) %collective-permute-start.36) | collective-permute-done | bytes 393248 | tf_op jit(solution)/shard_map/ppermute | solution.py:86
  547.3 11.9 %collective-permute-done.37 = bf16[96,2048]{1,0:T(8,128)(2,1)S(1)} collective-permute-done((bf16[96,2048]{1,0:T(8,128)(2,1)S(1)}, bf16[96,2048]{1,0:T(8,128)(2,1)S(1)}, u32[]{:S(2)}, u32[]{:S(2)}) %collective-permute-start.37) | collective-permute-done | bytes 393248 | tf_op jit(solution)/shard_map/ppermute | solution.py:86
  564.0 12.2 %convolution_convert_fusion.1 = bf16[2048,2816]{1,0:T(8,128)(2,1)} fusion(bf16[768,2816]{1,0:T(8,128)(2,1)S(1)} %bitcast.217, bf16[384,2048]{1,0:T(8,128)(2,1)S(1)} %collective-permute-done.39, bf16[384,2048]{1,0:T(8,128)(2,1)S(1)} %constant_dynamic-update-slice_fusion.4), kind=kOutput, calls=%fused_computation.9 | convolution fusion | flops 8870428672 | bytes 19005440 | tf_op jit(solution)/shard_map/dot_general | solution.py:39
  576.2 20.6 %multiply_convert_fusion.1 = (bf16[768,2816]{1,0:T(8,128)(2,1)}, bf16[768,2816]{1,0:T(8,128)(2,1)}) fusion(f32[768,5632]{1,0:T(8,128)} %copy-done.1, bf16[2048,2816]{0,1:T(8,128)(2,1)} %all-gather.8.cloned.1.call-done, bf16[384,2048]{1,0:T(8,128)(2,1)} %copy-done.114, bf16[384,2048]{1,0:T(8,128)(2,1)} %copy-done.46), kind=kOutput, calls=%fused_computation.12 | convolution fusion | flops 8892776448 | bytes 40632320 | tf_op jit(solution)/shard_map/dot_general | solution.py:29
  596.8 8.0 pad_maximum_fusion
  604.8 24.2 %fusion.169 = f32[768,2048]{1,0:T(8,128)S(1)} fusion(bf16[768,5632]{1,0:T(8,128)(2,1)} %pad_maximum_fusion, bf16[2048,5632]{1,0:T(8,128)(2,1)} %all-gather.6.cloned.1.call-done), kind=kOutput, calls=%fused_computation.437 | convolution fusion | flops 17716740096 | bytes 38010880 | tf_op jit(solution)/shard_map/dot_general | solution.py:33
  636.2 7.0 collective-permute-start.42
  643.2 24.2 %convolution_convert_fusion = bf16[2048,5632]{1,0:T(8,128)(2,1)} fusion(bf16[384,2048]{1,0:T(8,128)(2,1)} %collective-permute-done.26, bf16[384,2048]{1,0:T(8,128)(2,1)} %copy-done.47, bf16[768,2816]{1,0:T(8,128)(2,1)} %get-tuple-element.179, bf16[768,2816]{1,0:T(8,128)(2,1)S(1)} %bitcast.219), kind=kOutput, calls=%fused_computation.1 | convolution fusion | flops 17751867392 | bytes 34865152 | tf_op jit(solution)/shard_map/dot_general | solution.py:39
  667.4 5.3 collective-permute-done.42
  672.7 20.7 %reduce-scatter.4.cloned.1.call-done = bf16[512,2816]{1,0:T(8,128)(2,1)} async-done(((bf16[2048,2816]{1,0:T(8,128)(2,1)}), bf16[512,2816]{1,0:T(8,128)(2,1)}) %reduce-scatter.4.cloned.1.call-update) | async-done | bytes 2883600 | tf_op jit(solution)/shard_map/reduce_scatter | solution.py:99
  704.2 13.8 %collective-permute-done.44 = bf16[96,2048]{1,0:T(8,128)(2,1)S(1)} collective-permute-done((bf16[96,2048]{1,0:T(8,128)(2,1)S(1)}, bf16[96,2048]{1,0:T(8,128)(2,1)S(1)}, u32[]{:S(2)}, u32[]{:S(2)}) %collective-permute-start.44) | collective-permute-done | bytes 393248 | tf_op jit(solution)/shard_map/ppermute | solution.py:86
  718.0 12.8 %collective-permute-done.45 = bf16[96,2048]{1,0:T(8,128)(2,1)S(1)} collective-permute-done((bf16[96,2048]{1,0:T(8,128)(2,1)S(1)}, bf16[96,2048]{1,0:T(8,128)(2,1)S(1)}, u32[]{:S(2)}, u32[]{:S(2)}) %collective-permute-start.45) | collective-permute-done | bytes 393248 | tf_op jit(solution)/shard_map/ppermute | solution.py:86
  744.1 8.9 collective-permute-start.34
  790.0 5.0 convolution_convert_fusion.10
  804.7 5.2 convolution_convert_fusion.2
  809.9 8.1 dynamic_update_slice.180
  819.1 9.5 constant_dynamic-update-slice_fusion
  828.6 4.8 convert_bitcast_fusion
  833.4 6.3 copy.368
  839.7 14.3 %add_divide_fusion.2 = (f32[5632,256]{1,0:T(8,128)}, f32[5632,256]{1,0:T(8,128)}, f32[5632,256]{1,0:T(8,128)}) fusion(f32[5632,256]{1,0:T(8,128)} %copy.368, f32[5632,256]{1,0:T(8,128)} %param.43, f32[5632,256]{1,0:T(8,128)} %param.44), kind=kLoop, calls=%fused_computation.24 | loop fusion | flops 15859712 | bytes 34603008 | tf_op jit(solution)/shard_map/div | solution.py:268
  858.4 21.2 %collective-permute-done.51 = bf16[4,8,128,128]{2,3,1,0:T(8,128)(2,1)S(1)} collective-permute-done((bf16[4,8,128,128]{2,3,1,0:T(8,128)(2,1)S(1)}, bf16[4,8,128,128]{2,3,1,0:T(8,128)(2,1)S(1)}, u32[]{:S(2)}, u32[]{:S(2)}) %collective-permute-start.51) | collective-permute-done | bytes 1048608 | tf_op jit(solution)/shard_map/ppermute | solution.py:86
  889.1 10.8 %fusion.6 = (f32[2048]{0:T(1024)S(1)}, f32[1024,2048]{1,0:T(8,128)}) fusion(bf16[1024,2048]{1,0:T(8,128)(2,1)S(1)} %copy-done.3, f32[1024]{0:T(1024)S(1)} %copy-done.74, f32[1024,2048]{1,0:T(8,128)S(1)} %fusion.38, bf16[1024,1024]{0,1:T(8,128)(2,1)S(1)} %bitcast.229, bf16[2048,2048]{0,1:T(8,128)(2,1)} %all-gather.4.cloned.1.call-done), kind=kOutput, calls=%fused_computation.20 | convolution fusion | flops 4305451008 | bytes 27275264 | tf_op jit(solution)/shard_map/dot_general | solution.py:33
  913.5 21.4 %collective-permute-start.54 = (bf16[128,2048]{1,0:T(8,128)(2,1)}, bf16[128,2048]{1,0:T(8,128)(2,1)}, u32[]{:S(2)}, u32[]{:S(2)}) collective-permute-start(bf16[128,2048]{1,0:T(8,128)(2,1)} %get-tuple-element.200), channel_id=1, source_target_pairs={{0,2},{1,3},{2,0},{3,1},{4,6},{5,7},{6,4},{7,5},{8,10},{9,11},{10,... | collective-permute-start | bytes 1572872 | tf_op jit(solution)/shard_map/ppermute | solution.py:86
  940.9 21.1 %add_divide_fusion = (f32[2,256,5632]{2,1,0:T(8,128)}, f32[2,256,5632]{2,1,0:T(8,128)}, f32[2,256,5632]{2,1,0:T(8,128)}, f32[2,256,5632]{2,1,0:T(8,128)}) fusion(f32[2,256,5632]{2,1,0:T(8,128)S(1)} %bitcast.206, f32[2,256,5632]{2,1,0:T(8,128)} %param.41, bf16[1,256,5632]{2,1,0:T(8,128)(2,1)S(1)} %get-tuple-element.313, ...), kind=kLoop, calls=%fused_computation.7 | loop fusion | flops 37486592 | bytes 74973184 | tf_op jit(solution)/shard_map/div | solution.py:268
  964.8 66.3 %reduce-scatter.8.cloned.1.call-done = bf16[512,2688]{0,1:T(8,128)(2,1)} async-done(((bf16[2048,2688]{0,1:T(8,128)(2,1)}), bf16[512,2688]{0,1:T(8,128)(2,1)}) %reduce-scatter.8.cloned.1.call-update) | async-done | bytes 2752528 | tf_op jit(solution)/shard_map/reduce_scatter | solution.py:99
  1046.6 5.7 add_divide_fusion.4
  (634 shorter events, 343.3 us)
Async XLA Ops:
  7.2 165.6 %all-gather.4.cloned.1.call-start = ((), (), s32[]{:S(2)}) async-start(), calls=%async_computation.3 | async-start | bytes 10485760 | tf_op jit(solution)/shard_map/all_gather | solution.py:95
  18.8 341.8 %all-gather.6.cloned.1.call-start = ((), (), s32[]{:S(2)}) async-start(), calls=%async_computation.4 | async-start | bytes 28835840 | tf_op jit(solution)/shard_map/all_gather | solution.py:95
  26.0 15.0 %collective-permute-start.2 = (bf16[128,640]{1,0:T(8,128)(2,1)S(1)}, bf16[128,640]{1,0:T(8,128)(2,1)S(1)}, u32[]{:S(2)}, u32[]{:S(2)}) collective-permute-start(bf16[128,640]{1,0:T(8,128)(2,1)S(1)} %get-tuple-element.277), channel_id=1, source_target_pairs={{0,2},{1,3},{2,0},{3,1},{4,6},{5,7},{6,4},{7,5},{8,10},{9,11},{10,... | collective-permute-start | bytes 491528 | tf_op jit(solution)/shard_map/ppermute | solution.py:86
  28.6 12.4 %collective-permute-start.3 = (bf16[128,640]{1,0:T(8,128)(2,1)S(1)}, bf16[128,640]{1,0:T(8,128)(2,1)S(1)}, u32[]{:S(2)}, u32[]{:S(2)}) collective-permute-start(bf16[128,640]{1,0:T(8,128)(2,1)S(1)} %get-tuple-element.275), channel_id=1, source_target_pairs={{0,3},{1,2},{2,1},{3,0},{4,7},{5,6},{6,5},{7,4},{8,11},{9,10},{10,... | collective-permute-start | bytes 491528 | tf_op jit(solution)/shard_map/ppermute | solution.py:86
  59.8 405.5 %all-gather.8.cloned.1.call-start = ((), (), s32[]{:S(2)}) async-start(), calls=%async_computation.5 | async-start | bytes 14417920 | tf_op jit(solution)/shard_map/all_gather | solution.py:95
  59.9 31.3 %collective-permute-start.6 = (bf16[512,640]{1,0:T(8,128)(2,1)S(1)}, bf16[512,640]{1,0:T(8,128)(2,1)S(1)}, u32[]{:S(2)}, u32[]{:S(2)}) collective-permute-start(bf16[512,640]{1,0:T(8,128)(2,1)S(1)} %bitcast.223), channel_id=1, source_target_pairs={{0,8},{4,12},{8,0},{12,4},{16,24},{20,28},{24,16},{28,20},{1,9},{5... | collective-permute-start | bytes 1966088 | tf_op jit(solution)/shard_map/ppermute | solution.py:201
  61.4 37.2 %collective-permute-start.7 = (bf16[512,640]{1,0:T(8,128)(2,1)S(1)}, bf16[512,640]{1,0:T(8,128)(2,1)}, u32[]{:S(2)}, u32[]{:S(2)}) collective-permute-start(bf16[512,640]{1,0:T(8,128)(2,1)S(1)} %bitcast.224), channel_id=1, source_target_pairs={{0,16},{4,20},{8,24},{12,28},{16,0},{20,4},{24,8},{28,12},{1,17},{... | collective-permute-start | bytes 1966088 | tf_op jit(solution)/shard_map/ppermute | solution.py:201
  62.9 56.4 %collective-permute-start.8 = (bf16[512,640]{1,0:T(8,128)(2,1)S(1)}, bf16[512,640]{1,0:T(8,128)(2,1)}, u32[]{:S(2)}, u32[]{:S(2)}) collective-permute-start(bf16[512,640]{1,0:T(8,128)(2,1)S(1)} %bitcast.225), channel_id=1, source_target_pairs={{0,24},{4,28},{8,16},{12,20},{16,8},{20,12},{24,0},{28,4},{1,25},{... | collective-permute-start | bytes 1966088 | tf_op jit(solution)/shard_map/ppermute | solution.py:201
  70.2 52.9 %collective-permute-start.9 = (bf16[128,2176]{1,0:T(8,128)(2,1)}, bf16[128,2176]{1,0:T(8,128)(2,1)}, u32[]{:S(2)}, u32[]{:S(2)}) collective-permute-start(bf16[128,2176]{1,0:T(8,128)(2,1)} %fusion.75), channel_id=1, source_target_pairs={{0,1},{1,0},{2,3},{3,2},{4,5},{5,4},{6,7},{7,6},{8,9},{9,8},{10,11... | collective-permute-start | bytes 1671176 | tf_op jit(solution)/shard_map/ppermute | solution.py:86
  73.2 49.9 %collective-permute-start.10 = (bf16[128,2176]{1,0:T(8,128)(2,1)}, bf16[128,2176]{1,0:T(8,128)(2,1)}, u32[]{:S(2)}, u32[]{:S(2)}) collective-permute-start(bf16[128,2176]{1,0:T(8,128)(2,1)} %fusion.75), channel_id=1, source_target_pairs={{0,2},{1,3},{2,0},{3,1},{4,6},{5,7},{6,4},{7,5},{8,10},{9,11},{10,... | collective-permute-start | bytes 1671176 | tf_op jit(solution)/shard_map/ppermute | solution.py:86
  92.0 32.6 %collective-permute-start.11 = (bf16[128,2176]{1,0:T(8,128)(2,1)}, bf16[128,2176]{1,0:T(8,128)(2,1)}, u32[]{:S(2)}, u32[]{:S(2)}) collective-permute-start(bf16[128,2176]{1,0:T(8,128)(2,1)} %fusion.75), channel_id=1, source_target_pairs={{0,3},{1,2},{2,1},{3,0},{4,7},{5,6},{6,5},{7,4},{8,11},{9,10},{10,... | collective-permute-start | bytes 1671176 | tf_op jit(solution)/shard_map/ppermute | solution.py:86
  98.6 36.8 %collective-permute-start.17 = (bf16[256,2816]{0,1:T(8,128)(2,1)}, bf16[256,2816]{0,1:T(8,128)(2,1)}, u32[]{:S(2)}, u32[]{:S(2)}) collective-permute-start(bf16[256,2816]{0,1:T(8,128)(2,1)} %dynamic-slice_bitcast_fusion), channel_id=1, source_target_pairs={{0,4},{4,0},{8,12},{12,8},{16,20},{20,16},{24,28},{28,24},{1,5},{5... | collective-permute-start | bytes 4325384 | tf_op jit(solution)/shard_map/ppermute | solution.py:80
  138.1 555.4 %reduce-scatter.4.cloned.1.call-start = ((), (), s32[]{:S(2)}) async-start(), calls=%async_computation.6 | async-start | bytes 14417920 | tf_op jit(solution)/shard_map/reduce_scatter | solution.py:99
  160.9 50.0 %collective-permute-start.15 = (bf16[4,8,128,128]{3,2,1,0:T(8,128)(2,1)}, bf16[4,8,128,128]{3,2,1,0:T(8,128)(2,1)}, u32[]{:S(2)}, u32[]{:S(2)}) collective-permute-start(bf16[4,8,128,128]{3,2,1,0:T(8,128)(2,1)} %pad_maximum_fusion.14), channel_id=1, source_target_pairs={{0,1},{1,0},{2,3},{3,2},{4,5},{5,4},{6,7},{7,6},{8,9},{9,8},{10,11... | collective-permute-start | bytes 3145736 | tf_op jit(solution)/shard_map/ppermute | solution.py:86
  164.6 71.5 %collective-permute-start.16 = (bf16[4,8,128,128]{3,2,1,0:T(8,128)(2,1)}, bf16[4,8,128,128]{3,2,1,0:T(8,128)(2,1)}, u32[]{:S(2)}, u32[]{:S(2)}) collective-permute-start(bf16[4,8,128,128]{3,2,1,0:T(8,128)(2,1)} %pad_maximum_fusion.14), channel_id=1, source_target_pairs={{0,2},{1,3},{2,0},{3,1},{4,6},{5,7},{6,4},{7,5},{8,10},{9,11},{10,... | collective-permute-start | bytes 3145736 | tf_op jit(solution)/shard_map/ppermute | solution.py:86
  194.7 53.4 %collective-permute-start.18 = (bf16[4,8,128,128]{3,2,1,0:T(8,128)(2,1)}, bf16[4,8,128,128]{3,2,1,0:T(8,128)(2,1)}, u32[]{:S(2)}, u32[]{:S(2)}) collective-permute-start(bf16[4,8,128,128]{3,2,1,0:T(8,128)(2,1)} %pad_maximum_fusion.14), channel_id=1, source_target_pairs={{0,3},{1,2},{2,1},{3,0},{4,7},{5,6},{6,5},{7,4},{8,11},{9,10},{10,... | collective-permute-start | bytes 3145736 | tf_op jit(solution)/shard_map/ppermute | solution.py:86
  284.5 13.0 %collective-permute-start.22 = (bf16[96,2048]{1,0:T(8,128)(2,1)S(1)}, bf16[96,2048]{1,0:T(8,128)(2,1)S(1)}, u32[]{:S(2)}, u32[]{:S(2)}) collective-permute-start(bf16[96,2048]{1,0:T(8,128)(2,1)S(1)} %get-tuple-element.230), channel_id=1, source_target_pairs={{0,3},{1,2},{2,1},{3,0},{4,7},{5,6},{6,5},{7,4},{8,11},{9,10},{10,... | collective-permute-start | bytes 1179656 | tf_op jit(solution)/shard_map/ppermute | solution.py:86
  287.8 35.1 %collective-permute-start.21 = (bf16[96,2048]{1,0:T(8,128)(2,1)S(1)}, bf16[96,2048]{1,0:T(8,128)(2,1)S(1)}, u32[]{:S(2)}, u32[]{:S(2)}) collective-permute-start(bf16[96,2048]{1,0:T(8,128)(2,1)S(1)} %get-tuple-element.231), channel_id=1, source_target_pairs={{0,2},{1,3},{2,0},{3,1},{4,6},{5,7},{6,4},{7,5},{8,10},{9,11},{10,... | collective-permute-start | bytes 1179656 | tf_op jit(solution)/shard_map/ppermute | solution.py:86
  296.9 26.0 %collective-permute-start.20 = (bf16[96,2048]{1,0:T(8,128)(2,1)S(1)}, bf16[96,2048]{1,0:T(8,128)(2,1)S(1)}, u32[]{:S(2)}, u32[]{:S(2)}) collective-permute-start(bf16[96,2048]{1,0:T(8,128)(2,1)S(1)} %get-tuple-element.232), channel_id=1, source_target_pairs={{0,1},{1,0},{2,3},{3,2},{4,5},{5,4},{6,7},{7,6},{8,9},{9,8},{10,11... | collective-permute-start | bytes 1179656 | tf_op jit(solution)/shard_map/ppermute | solution.py:86
  326.4 18.2 %collective-permute-start.23 = (bf16[96,2048]{1,0:T(8,128)(2,1)S(1)}, bf16[96,2048]{1,0:T(8,128)(2,1)S(1)}, u32[]{:S(2)}, u32[]{:S(2)}) collective-permute-start(bf16[96,2048]{1,0:T(8,128)(2,1)S(1)} %get-tuple-element.228), channel_id=1, source_target_pairs={{0,1},{1,0},{2,3},{3,2},{4,5},{5,4},{6,7},{7,6},{8,9},{9,8},{10,11... | collective-permute-start | bytes 1179656 | tf_op jit(solution)/shard_map/ppermute | solution.py:86
  326.7 30.2 %collective-permute-start.24 = (bf16[96,2048]{1,0:T(8,128)(2,1)S(1)}, bf16[96,2048]{1,0:T(8,128)(2,1)S(1)}, u32[]{:S(2)}, u32[]{:S(2)}) collective-permute-start(bf16[96,2048]{1,0:T(8,128)(2,1)S(1)} %get-tuple-element.227), channel_id=1, source_target_pairs={{0,2},{1,3},{2,0},{3,1},{4,6},{5,7},{6,4},{7,5},{8,10},{9,11},{10,... | collective-permute-start | bytes 1179656 | tf_op jit(solution)/shard_map/ppermute | solution.py:86
  330.1 26.9 %collective-permute-start.25 = (bf16[96,2048]{1,0:T(8,128)(2,1)S(1)}, bf16[96,2048]{1,0:T(8,128)(2,1)S(1)}, u32[]{:S(2)}, u32[]{:S(2)}) collective-permute-start(bf16[96,2048]{1,0:T(8,128)(2,1)S(1)} %get-tuple-element.226), channel_id=1, source_target_pairs={{0,3},{1,2},{2,1},{3,0},{4,7},{5,6},{6,5},{7,4},{8,11},{9,10},{10,... | collective-permute-start | bytes 1179656 | tf_op jit(solution)/shard_map/ppermute | solution.py:86
  488.5 14.0 %collective-permute-start.30 = (bf16[96,2048]{1,0:T(8,128)(2,1)S(1)}, bf16[96,2048]{1,0:T(8,128)(2,1)S(1)}, u32[]{:S(2)}, u32[]{:S(2)}) collective-permute-start(bf16[96,2048]{1,0:T(8,128)(2,1)S(1)} %get-tuple-element.223), channel_id=1, source_target_pairs={{0,3},{1,2},{2,1},{3,0},{4,7},{5,6},{6,5},{7,4},{8,11},{9,10},{10,... | collective-permute-start | bytes 1179656 | tf_op jit(solution)/shard_map/ppermute | solution.py:86
  491.9 34.1 %collective-permute-start.29 = (bf16[96,2048]{1,0:T(8,128)(2,1)S(1)}, bf16[96,2048]{1,0:T(8,128)(2,1)S(1)}, u32[]{:S(2)}, u32[]{:S(2)}) collective-permute-start(bf16[96,2048]{1,0:T(8,128)(2,1)S(1)} %get-tuple-element.224), channel_id=1, source_target_pairs={{0,2},{1,3},{2,0},{3,1},{4,6},{5,7},{6,4},{7,5},{8,10},{9,11},{10,... | collective-permute-start | bytes 1179656 | tf_op jit(solution)/shard_map/ppermute | solution.py:86
  491.9 34.1 %collective-permute-start.28 = (bf16[96,2048]{1,0:T(8,128)(2,1)S(1)}, bf16[96,2048]{1,0:T(8,128)(2,1)S(1)}, u32[]{:S(2)}, u32[]{:S(2)}) collective-permute-start(bf16[96,2048]{1,0:T(8,128)(2,1)S(1)} %get-tuple-element.225), channel_id=1, source_target_pairs={{0,1},{1,0},{2,3},{3,2},{4,5},{5,4},{6,7},{7,6},{8,9},{9,8},{10,11... | collective-permute-start | bytes 1179656 | tf_op jit(solution)/shard_map/ppermute | solution.py:86
  529.3 18.0 %collective-permute-start.36 = (bf16[96,2048]{1,0:T(8,128)(2,1)S(1)}, bf16[96,2048]{1,0:T(8,128)(2,1)S(1)}, u32[]{:S(2)}, u32[]{:S(2)}) collective-permute-start(bf16[96,2048]{1,0:T(8,128)(2,1)S(1)} %get-tuple-element.220), channel_id=1, source_target_pairs={{0,1},{1,0},{2,3},{3,2},{4,5},{5,4},{6,7},{7,6},{8,9},{9,8},{10,11... | collective-permute-start | bytes 1179656 | tf_op jit(solution)/shard_map/ppermute | solution.py:86
  529.4 29.9 %collective-permute-start.37 = (bf16[96,2048]{1,0:T(8,128)(2,1)S(1)}, bf16[96,2048]{1,0:T(8,128)(2,1)S(1)}, u32[]{:S(2)}, u32[]{:S(2)}) collective-permute-start(bf16[96,2048]{1,0:T(8,128)(2,1)S(1)} %get-tuple-element.219), channel_id=1, source_target_pairs={{0,2},{1,3},{2,0},{3,1},{4,6},{5,7},{6,4},{7,5},{8,10},{9,11},{10,... | collective-permute-start | bytes 1179656 | tf_op jit(solution)/shard_map/ppermute | solution.py:86
  532.3 27.0 %collective-permute-start.38 = (bf16[96,2048]{1,0:T(8,128)(2,1)S(1)}, bf16[96,2048]{1,0:T(8,128)(2,1)S(1)}, u32[]{:S(2)}, u32[]{:S(2)}) collective-permute-start(bf16[96,2048]{1,0:T(8,128)(2,1)S(1)} %get-tuple-element.218), channel_id=1, source_target_pairs={{0,3},{1,2},{2,1},{3,0},{4,7},{5,6},{6,5},{7,4},{8,11},{9,10},{10,... | collective-permute-start | bytes 1179656 | tf_op jit(solution)/shard_map/ppermute | solution.py:86
  576.2 328.4 %reduce-scatter.6.cloned.1.call-start = ((), (), s32[]{:S(2)}) async-start(), calls=%async_computation.7 | async-start | bytes 28835840 | tf_op jit(solution)/shard_map/reduce_scatter | solution.py:99
  634.2 33.3 %collective-permute-start.43 = (bf16[96,2048]{1,0:T(8,128)(2,1)}, bf16[96,2048]{1,0:T(8,128)(2,1)}, u32[]{:S(2)}, u32[]{:S(2)}) collective-permute-start(bf16[96,2048]{1,0:T(8,128)(2,1)} %get-tuple-element.215), channel_id=1, source_target_pairs={{0,3},{1,2},{2,1},{3,0},{4,7},{5,6},{6,5},{7,4},{8,11},{9,10},{10,... | collective-permute-start | bytes 1179656 | tf_op jit(solution)/shard_map/ppermute | solution.py:86
  636.2 36.5 %collective-permute-start.42 = (bf16[96,2048]{1,0:T(8,128)(2,1)S(1)}, bf16[96,2048]{1,0:T(8,128)(2,1)}, u32[]{:S(2)}, u32[]{:S(2)}) collective-permute-start(bf16[96,2048]{1,0:T(8,128)(2,1)S(1)} %get-tuple-element.216), channel_id=1, source_target_pairs={{0,2},{1,3},{2,0},{3,1},{4,6},{5,7},{6,4},{7,5},{8,10},{9,11},{10,... | collective-permute-start | bytes 1179656 | tf_op jit(solution)/shard_map/ppermute | solution.py:86
  643.2 29.6 %collective-permute-start.41 = (bf16[96,2048]{1,0:T(8,128)(2,1)S(1)}, bf16[96,2048]{1,0:T(8,128)(2,1)}, u32[]{:S(2)}, u32[]{:S(2)}) collective-permute-start(bf16[96,2048]{1,0:T(8,128)(2,1)S(1)} %get-tuple-element.217), channel_id=1, source_target_pairs={{0,1},{1,0},{2,3},{3,2},{4,5},{5,4},{6,7},{7,6},{8,9},{9,8},{10,11... | collective-permute-start | bytes 1179656 | tf_op jit(solution)/shard_map/ppermute | solution.py:86
  693.4 337.7 %reduce-scatter.8.cloned.1.call-start = ((), (), s32[]{:S(2)}) async-start(), calls=%async_computation.8 | async-start | bytes 13762560 | tf_op jit(solution)/shard_map/reduce_scatter | solution.py:99
  699.4 18.5 %collective-permute-start.44 = (bf16[96,2048]{1,0:T(8,128)(2,1)S(1)}, bf16[96,2048]{1,0:T(8,128)(2,1)S(1)}, u32[]{:S(2)}, u32[]{:S(2)}) collective-permute-start(bf16[96,2048]{1,0:T(8,128)(2,1)S(1)} %get-tuple-element.213), channel_id=1, source_target_pairs={{0,1},{1,0},{2,3},{3,2},{4,5},{5,4},{6,7},{7,6},{8,9},{9,8},{10,11... | collective-permute-start | bytes 1179656 | tf_op jit(solution)/shard_map/ppermute | solution.py:86
  700.9 29.8 %collective-permute-start.45 = (bf16[96,2048]{1,0:T(8,128)(2,1)S(1)}, bf16[96,2048]{1,0:T(8,128)(2,1)S(1)}, u32[]{:S(2)}, u32[]{:S(2)}) collective-permute-start(bf16[96,2048]{1,0:T(8,128)(2,1)S(1)} %get-tuple-element.212), channel_id=1, source_target_pairs={{0,2},{1,3},{2,0},{3,1},{4,6},{5,7},{6,4},{7,5},{8,10},{9,11},{10,... | collective-permute-start | bytes 1179656 | tf_op jit(solution)/shard_map/ppermute | solution.py:86
  703.6 27.2 %collective-permute-start.46 = (bf16[96,2048]{1,0:T(8,128)(2,1)S(1)}, bf16[96,2048]{1,0:T(8,128)(2,1)S(1)}, u32[]{:S(2)}, u32[]{:S(2)}) collective-permute-start(bf16[96,2048]{1,0:T(8,128)(2,1)S(1)} %get-tuple-element.211), channel_id=1, source_target_pairs={{0,3},{1,2},{2,1},{3,0},{4,7},{5,6},{6,5},{7,4},{8,11},{9,10},{10,... | collective-permute-start | bytes 1179656 | tf_op jit(solution)/shard_map/ppermute | solution.py:86
  730.8 28.1 %collective-permute-start.47 = (bf16[384,2048]{1,0:T(8,128)(2,1)S(1)}, bf16[384,2048]{1,0:T(8,128)(2,1)S(1)}, u32[]{:S(2)}, u32[]{:S(2)}) collective-permute-start(bf16[384,2048]{1,0:T(8,128)(2,1)S(1)} %constant_dynamic-update-slice_fusion.1), channel_id=1, source_target_pairs={{0,4},{4,0},{8,12},{12,8},{16,20},{20,16},{24,28},{28,24},{1,5},{5... | collective-permute-start | bytes 4718600 | tf_op jit(solution)/shard_map/ppermute | solution.py:80
  797.2 61.2 %collective-permute-start.49 = (bf16[4,8,128,128]{2,3,1,0:T(8,128)(2,1)}, bf16[4,8,128,128]{2,3,1,0:T(8,128)(2,1)}, u32[]{:S(2)}, u32[]{:S(2)}) collective-permute-start(bf16[4,8,128,128]{2,3,1,0:T(8,128)(2,1)} %pad_maximum_fusion.16), channel_id=1, source_target_pairs={{0,2},{1,3},{2,0},{3,1},{4,6},{5,7},{6,4},{7,5},{8,10},{9,11},{10,... | collective-permute-start | bytes 3145736 | tf_op jit(solution)/shard_map/ppermute | solution.py:86
  801.1 57.3 %collective-permute-start.48 = (bf16[4,8,128,128]{2,3,1,0:T(8,128)(2,1)}, bf16[4,8,128,128]{2,3,1,0:T(8,128)(2,1)}, u32[]{:S(2)}, u32[]{:S(2)}) collective-permute-start(bf16[4,8,128,128]{2,3,1,0:T(8,128)(2,1)} %pad_maximum_fusion.15), channel_id=1, source_target_pairs={{0,1},{1,0},{2,3},{3,2},{4,5},{5,4},{6,7},{7,6},{8,9},{9,8},{10,11... | collective-permute-start | bytes 3145736 | tf_op jit(solution)/shard_map/ppermute | solution.py:86
  802.8 25.7 %collective-permute-start.50 = (bf16[256,2816]{1,0:T(8,128)(2,1)}, bf16[256,2816]{1,0:T(8,128)(2,1)}, u32[]{:S(2)}, u32[]{:S(2)}) collective-permute-start(bf16[256,2816]{1,0:T(8,128)(2,1)} %get-tuple-element.195), channel_id=1, source_target_pairs={{0,4},{4,0},{8,12},{12,8},{16,20},{20,16},{24,28},{28,24},{1,5},{5... | collective-permute-start | bytes 4325384 | tf_op jit(solution)/shard_map/ppermute | solution.py:80
  854.0 25.7 %collective-permute-start.51 = (bf16[4,8,128,128]{2,3,1,0:T(8,128)(2,1)S(1)}, bf16[4,8,128,128]{2,3,1,0:T(8,128)(2,1)S(1)}, u32[]{:S(2)}, u32[]{:S(2)}) collective-permute-start(bf16[4,8,128,128]{2,3,1,0:T(8,128)(2,1)S(1)} %copy-done.49), channel_id=1, source_target_pairs={{0,3},{1,2},{2,1},{3,0},{4,7},{5,6},{6,5},{7,4},{8,11},{9,10},{10,... | collective-permute-start | bytes 3145736 | tf_op jit(solution)/shard_map/ppermute | solution.py:86
  910.6 25.8 %collective-permute-start.55 = (bf16[256,5632]{1,0:T(8,128)(2,1)S(1)}, bf16[256,5632]{1,0:T(8,128)(2,1)S(1)}, u32[]{:S(2)}, u32[]{:S(2)}) collective-permute-start(bf16[256,5632]{1,0:T(8,128)(2,1)S(1)} %get-tuple-element.183), channel_id=1, source_target_pairs={{0,4},{4,0},{8,12},{12,8},{16,20},{20,16},{24,28},{28,24},{1,5},{5... | collective-permute-start | bytes 8650760 | tf_op jit(solution)/shard_map/ppermute | solution.py:80
  913.5 120.7 %collective-permute-start.54 = (bf16[128,2048]{1,0:T(8,128)(2,1)}, bf16[128,2048]{1,0:T(8,128)(2,1)}, u32[]{:S(2)}, u32[]{:S(2)}) collective-permute-start(bf16[128,2048]{1,0:T(8,128)(2,1)} %get-tuple-element.200), channel_id=1, source_target_pairs={{0,2},{1,3},{2,0},{3,1},{4,6},{5,7},{6,4},{7,5},{8,10},{9,11},{10,... | collective-permute-start | bytes 1572872 | tf_op jit(solution)/shard_map/ppermute | solution.py:86
  934.9 99.3 %collective-permute-start.53 = (bf16[128,2048]{1,0:T(8,128)(2,1)}, bf16[128,2048]{1,0:T(8,128)(2,1)}, u32[]{:S(2)}, u32[]{:S(2)}) collective-permute-start(bf16[128,2048]{1,0:T(8,128)(2,1)} %get-tuple-element.198), channel_id=1, source_target_pairs={{0,1},{1,0},{2,3},{3,2},{4,5},{5,4},{6,7},{7,6},{8,9},{9,8},{10,11... | collective-permute-start | bytes 1572872 | tf_op jit(solution)/shard_map/ppermute | solution.py:86
  962.0 72.2 %collective-permute-start.56 = (bf16[128,2048]{1,0:T(8,128)(2,1)S(1)}, bf16[128,2048]{1,0:T(8,128)(2,1)}, u32[]{:S(2)}, u32[]{:S(2)}) collective-permute-start(bf16[128,2048]{1,0:T(8,128)(2,1)S(1)} %get-tuple-element.67), channel_id=1, source_target_pairs={{0,3},{1,2},{2,1},{3,0},{4,7},{5,6},{6,5},{7,4},{8,11},{9,10},{10,... | collective-permute-start | bytes 1572872 | tf_op jit(solution)/shard_map/ppermute | solution.py:86
  1042.1 14.1 %collective-permute-start.60 = (bf16[2,64,640]{2,1,0:T(8,128)(2,1)S(1)}, bf16[2,64,640]{2,1,0:T(8,128)(2,1)S(1)}, u32[]{:S(2)}, u32[]{:S(2)}) collective-permute-start(bf16[2,64,640]{2,1,0:T(8,128)(2,1)S(1)} %get-tuple-element.254), channel_id=1, source_target_pairs={{0,3},{1,2},{2,1},{3,0},{4,7},{5,6},{6,5},{7,4},{8,11},{9,10},{10,... | collective-permute-start | bytes 491528 | tf_op jit(solution)/shard_map/ppermute | solution.py:86
  1045.5 14.8 %collective-permute-start.59 = (bf16[2,64,640]{2,1,0:T(8,128)(2,1)S(1)}, bf16[2,64,640]{2,1,0:T(8,128)(2,1)S(1)}, u32[]{:S(2)}, u32[]{:S(2)}) collective-permute-start(bf16[2,64,640]{2,1,0:T(8,128)(2,1)S(1)} %get-tuple-element.255), channel_id=1, source_target_pairs={{0,2},{1,3},{2,0},{3,1},{4,6},{5,7},{6,4},{7,5},{8,10},{9,11},{10,... | collective-permute-start | bytes 491528 | tf_op jit(solution)/shard_map/ppermute | solution.py:86
  1045.5 14.7 %collective-permute-start.58 = (bf16[2,64,640]{2,1,0:T(8,128)(2,1)S(1)}, bf16[2,64,640]{2,1,0:T(8,128)(2,1)S(1)}, u32[]{:S(2)}, u32[]{:S(2)}) collective-permute-start(bf16[2,64,640]{2,1,0:T(8,128)(2,1)S(1)} %get-tuple-element.256), channel_id=1, source_target_pairs={{0,1},{1,0},{2,3},{3,2},{4,5},{5,4},{6,7},{7,6},{8,9},{9,8},{10,11... | collective-permute-start | bytes 491528 | tf_op jit(solution)/shard_map/ppermute | solution.py:86
  (150 other events, 1716.2 us)
Sparse Core Ops, SparseCore 0:
  18.9 118.0 all-gather.3
  139.5 209.7 all-gather.5
  351.6 113.6 all-gather.7
  576.3 117.0 reduce-scatter.3
  696.4 204.8 reduce-scatter.5
  904.7 126.3 reduce-scatter.7

commit v3 on v2

--- a/solution.py
+++ b/solution.py
@@ -125,9 +125,10 @@
 
 def exchange_rows(core, summed):
     rows = summed.shape[0] // 2
-    low, high = summed[:rows], summed[rows:]
-    mine = jnp.where(core == 0, low, high)
-    return (mine, core_swap(jnp.where(core == 0, high, low)))
+    mine, theirs = [
+        lax.dynamic_slice_in_dim(summed, at * rows, rows, 0) for at in (core, 1 - core)
+    ]
+    return (mine, core_swap(theirs))
 
 
 def slots_before(hits):
@@ -488,7 +489,6 @@
 
     deviation = outputs - teacher.astype(F32)
     local_error = jnp.sum(valid_f[:, None] * deviation * deviation)
-    total_error = all_sum(local_error.reshape(1, 1))[0, 0]
     grad_out = 2.0 * valid_f[:, None] * deviation / total_count
 
     def send_grads(pick, gates, hit, grad, where=None):
@@ -542,10 +542,6 @@
     grad_keys = rotate(grad_key_heads, *back_tables).astype(BF16)
     grad_values = grad_value_heads.astype(BF16)
     grad_query = matmul_rows(normed_all, grad_query_pre).astype(BF16)
-    down_mine, down_other = exchange_rows(core, down_sum)
-    reduced_down = turned(in_core_order(core, down_mine, down_other, 1))
-    update_down = adam_step(moment_down, square_down, reduced_down)
-
     def heads_of(step):
         start = (expert ^ step) * count
         return jnp.concatenate(
@@ -556,7 +552,7 @@
         )
 
     grad_kv_parts = [heads_of(step) for step in range(EXPERTS)]
-    grad_kv_parts[-1] = after(grad_kv_parts[-1], grad_query, total_error, *update_down)
+    grad_kv_parts[-1] = after(grad_kv_parts[-1], grad_query)
     grad_kv = sum(
         over_expert(part, step * halves).astype(F32) for step, part in enumerate(grad_kv_parts)
     ).astype(BF16)
@@ -612,7 +608,13 @@
     grad_inputs_norm, _ = norm_back(inputs_f, inverse_one, gains_f[0], grad_normed_one)
     input_grad = grad_hidden + grad_inputs_norm
 
-    last_mine, last_other = exchange_rows(core, last_sum)
+    down_sum, local_error, _ = together(down_sum, local_error, normed_one_rows)
+    down_mine, down_other = exchange_rows(core, down_sum)
+    reduced_down = turned(in_core_order(core, down_mine, down_other, 1))
+    update_down = adam_step(moment_down, square_down, reduced_down)
+    total_error = all_sum(local_error.reshape(1, 1))[0, 0]
+
+    last_mine, last_other = exchange_rows(core, after(last_sum, total_error, *update_down))
     attn_mine, attn_other = last_mine[:, : 2 * width_attn], last_other[:, : 2 * width_attn]
     shared_mine, shared_theirs = [
         rows[:, 2 * width_attn :].reshape(partners, local_rows, -1)

time: 1080 us -> 1070 us (level)
  starting transfers between devices: 116 us -> 99.2 us
  other arithmetic: 121 us -> 108 us
    reduce_scatter x3, waiting for transfers between devices: 87 us -> 50.9 us  [scatter_chips(): lax.psum_scatter(partial, 'dp', scatter_dimension=0, tiled=True, axis_ind...]
    ppermute x38, waiting for transfers between devices: 214 us -> 245 us  [over_expert(): lax.ppermute(value, 'expert', swap_perm(lax.axis_size('expert'), bits))]
    ppermute x38, starting transfers between devices: 103 us -> 86.5 us  [over_expert(): lax.ppermute(value, 'expert', swap_perm(lax.axis_size('expert'), bits))]
    unnamed x266 -> x246, local copies, waits for them, and re-layouts: 33.5 us -> 29.2 us
  transfers between devices with their start and end apart: 67 -> 67, of which waited for: 34 -> 40; matrix products, arithmetic and copies ran while one was open for 40% -> 41% of each run, Pallas kernels for 0% -> 0%
where the time goes in v3:
time: 1070 us; the launch traced here: 1060 us
  waiting for transfers between devices  428 us (40%)
  matrix products  216 us (20%)
  local copies, waits for them, and re-layouts  183 us (17%)
  other arithmetic  108 us (10%)
  starting transfers between devices  99.2 us (9%)
  between operations  22.4 us (2%)
    ppermute x38, waiting for transfers between devices, over_expert(): lax.ppermute(value, 'expert', swap_perm(lax.axis_size('expert'), bits))  245 us
    ppermute x38, starting transfers between devices, over_expert(): lax.ppermute(value, 'expert', swap_perm(lax.axis_size('expert'), bits))  86.5 us
    all_gather x3, waiting for transfers between devices, gather_chips(): lax.all_gather(block, 'dp', axis=0, tiled=True, axis_index_groups=chip_gr...  72.2 us
    dot_general x13, matrix products, matmul(): return jnp.dot(left_side, right_side, preferred_element_type=F32)  72 us
    dot_general x5, matrix products, matmul_back(): lax.dot_general(left_side, right_side, (((1,), (1,)), ((), ())), preferre...  58.5 us
    dot_general x5, matrix products, matmul_rows(): lax.dot_general(left_side, right_side, (((0,), (0,)), ((), ())), preferre...  54.8 us
    reduce_scatter x3, waiting for transfers between devices, scatter_chips(): lax.psum_scatter(partial, 'dp', scatter_dimension=0, tiled=True, axis_ind...  50.9 us
    div x7, other arithmetic, adam_step(): direction = moment_hat / (jnp.sqrt(square_hat) + ADAM_EPS)  47.3 us
  transfers between devices with their start and end apart: 67, of which 40 were waited for; matrix products, arithmetic and copies ran while one was open for 41% of the time, Pallas kernels for 0%

profile of v3, /device:TPU:0, one launch (start us, length us, event | category | flops | bytes accessed | tf_op | source)
XLA Modules:
  0.0 1055.9 jit_solution(2127266171603945834)
XLA Ops:
  23.0 5.0 collective-permute-start.3
  37.2 5.1 collective-permute-done.2
  73.8 19.2 %collective-permute-done.8 = bf16[512,640]{1,0:T(8,128)(2,1)S(1)} collective-permute-done((bf16[512,640]{1,0:T(8,128)(2,1)S(1)}, bf16[512,640]{1,0:T(8,128)(2,1)S(1)}, u32[]{:S(2)}, u32[]{:S(2)}) %collective-permute-start.8) | collective-permute-done | bytes 655392 | tf_op jit(solution)/shard_map/ppermute | solution.py:202
  99.0 8.8 collective-permute-done.7
  110.0 11.4 %collective-permute-done.6 = bf16[512,640]{1,0:T(8,128)(2,1)} collective-permute-done((bf16[512,640]{1,0:T(8,128)(2,1)S(1)}, bf16[512,640]{1,0:T(8,128)(2,1)}, u32[]{:S(2)}, u32[]{:S(2)}) %collective-permute-start.6) | collective-permute-done | bytes 655392 | tf_op jit(solution)/shard_map/ppermute | solution.py:202
  171.5 10.0 fusion.20
  181.6 5.7 copy.341
  187.3 5.1 fusion.152
  198.0 15.3 %collective-permute-done.16 = bf16[4,8,128,128]{3,2,1,0:T(8,128)(2,1)} collective-permute-done((bf16[4,8,128,128]{3,2,1,0:T(8,128)(2,1)}, bf16[4,8,128,128]{3,2,1,0:T(8,128)(2,1)}, u32[]{:S(2)}, u32[]{:S(2)}) %collective-permute-start.16) | collective-permute-done | bytes 1048608 | tf_op jit(solution)/shard_map/ppermute | solution.py:86
  217.0 18.7 %collective-permute-done.15 = bf16[4,8,128,128]{3,2,1,0:T(8,128)(2,1)} collective-permute-done((bf16[4,8,128,128]{3,2,1,0:T(8,128)(2,1)}, bf16[4,8,128,128]{3,2,1,0:T(8,128)(2,1)}, u32[]{:S(2)}, u32[]{:S(2)}) %collective-permute-start.15) | collective-permute-done | bytes 1048608 | tf_op jit(solution)/shard_map/ppermute | solution.py:86
  252.9 5.4 fusion.165
  268.9 6.0 fusion.17
  285.6 10.7 %collective-permute-start.21 = (bf16[96,2048]{1,0:T(8,128)(2,1)S(1)}, bf16[96,2048]{1,0:T(8,128)(2,1)S(1)}, u32[]{:S(2)}, u32[]{:S(2)}) collective-permute-start(bf16[96,2048]{1,0:T(8,128)(2,1)S(1)} %get-tuple-element.238), channel_id=1, source_target_pairs={{0,2},{1,3},{2,0},{3,1},{4,6},{5,7},{6,4},{7,5},{8,10},{9,11},{10,... | collective-permute-start | bytes 1179656 | tf_op jit(solution)/shard_map/ppermute | solution.py:86
  296.8 25.5 %collective-permute-done.21 = bf16[96,2048]{1,0:T(8,128)(2,1)S(1)} collective-permute-done((bf16[96,2048]{1,0:T(8,128)(2,1)S(1)}, bf16[96,2048]{1,0:T(8,128)(2,1)S(1)}, u32[]{:S(2)}, u32[]{:S(2)}) %collective-permute-start.21) | collective-permute-done | bytes 393248 | tf_op jit(solution)/shard_map/ppermute | solution.py:86
  330.2 13.1 %collective-permute-done.23 = bf16[96,2048]{1,0:T(8,128)(2,1)S(1)} collective-permute-done((bf16[96,2048]{1,0:T(8,128)(2,1)S(1)}, bf16[96,2048]{1,0:T(8,128)(2,1)S(1)}, u32[]{:S(2)}, u32[]{:S(2)}) %collective-permute-start.23) | collective-permute-done | bytes 393248 | tf_op jit(solution)/shard_map/ppermute | solution.py:86
  343.3 12.4 %collective-permute-done.24 = bf16[96,2048]{1,0:T(8,128)(2,1)S(1)} collective-permute-done((bf16[96,2048]{1,0:T(8,128)(2,1)S(1)}, bf16[96,2048]{1,0:T(8,128)(2,1)S(1)}, u32[]{:S(2)}, u32[]{:S(2)}) %collective-permute-start.24) | collective-permute-done | bytes 393248 | tf_op jit(solution)/shard_map/ppermute | solution.py:86
  359.4 24.6 %fusion.37 = f32[768,5632]{1,0:T(8,128)S(1)} fusion(bf16[2048,5632]{1,0:T(8,128)(2,1)} %all-gather.6.cloned.1.call-done, bf16[384,2048]{1,0:T(8,128)(2,1)} %collective-permute-done.26, bf16[384,2048]{1,0:T(8,128)(2,1)S(1)} %constant_dynamic-update-slice_fusion.7), kind=kOutput, calls=%fused_computation.105 | convolution fusion | flops 17723031552 | bytes 43515904 | tf_op jit(solution)/shard_map/dot_general | solution.py:29
  384.0 5.9 copy-done.1
  394.0 72.2 %all-gather.8.cloned.1.call-done = bf16[2048,2816]{0,1:T(8,128)(2,1)} async-done(((bf16[512,2816]{0,1:T(8,128)(2,1)}), bf16[2048,2816]{0,1:T(8,128)(2,1)}) %all-gather.8.cloned.1.call-update) | async-done | bytes 11534352 | tf_op jit(solution)/shard_map/all_gather | solution.py:95
  466.2 13.4 %fusion.168 = f32[768,2048]{1,0:T(8,128)S(1)} fusion(bf16[768,2816]{1,0:T(8,128)(2,1)} %multiply_convert_fusion.2, bf16[2048,2816]{0,1:T(8,128)(2,1)} %all-gather.8.cloned.1.call-done), kind=kOutput, calls=%fused_computation.436 | convolution fusion | flops 8858370048 | bytes 22151168 | tf_op jit(solution)/shard_map/dot_general | solution.py:33
  493.7 9.5 collective-permute-done.30
  503.2 23.5 %collective-permute-done.29 = bf16[96,2048]{1,0:T(8,128)(2,1)S(1)} collective-permute-done((bf16[96,2048]{1,0:T(8,128)(2,1)S(1)}, bf16[96,2048]{1,0:T(8,128)(2,1)S(1)}, u32[]{:S(2)}, u32[]{:S(2)}) %collective-permute-start.29) | collective-permute-done | bytes 393248 | tf_op jit(solution)/shard_map/ppermute | solution.py:86
  535.0 13.2 %collective-permute-done.31 = bf16[96,2048]{1,0:T(8,128)(2,1)S(1)} collective-permute-done((bf16[96,2048]{1,0:T(8,128)(2,1)S(1)}, bf16[96,2048]{1,0:T(8,128)(2,1)S(1)}, u32[]{:S(2)}, u32[]{:S(2)}) %collective-permute-start.31) | collective-permute-done | bytes 393248 | tf_op jit(solution)/shard_map/ppermute | solution.py:86
  548.3 12.1 %collective-permute-done.32 = bf16[96,2048]{1,0:T(8,128)(2,1)S(1)} collective-permute-done((bf16[96,2048]{1,0:T(8,128)(2,1)S(1)}, bf16[96,2048]{1,0:T(8,128)(2,1)S(1)}, u32[]{:S(2)}, u32[]{:S(2)}) %collective-permute-start.32) | collective-permute-done | bytes 393248 | tf_op jit(solution)/shard_map/ppermute | solution.py:86
  565.0 12.2 %convolution_convert_fusion.1 = bf16[2048,2816]{0,1:T(8,128)(2,1)} fusion(bf16[768,2816]{1,0:T(8,128)(2,1)S(1)} %bitcast.216, bf16[384,2048]{1,0:T(8,128)(2,1)S(1)} %collective-permute-done.34, bf16[384,2048]{1,0:T(8,128)(2,1)S(1)} %constant_dynamic-update-slice_fusion.4), kind=kOutput, calls=%fused_computation.9 | convolution fusion | flops 8870428672 | bytes 19005440 | tf_op jit(solution)/shard_map/dot_general | solution.py:39
  577.3 20.8 %multiply_convert_fusion.1 = (bf16[768,2816]{1,0:T(8,128)(2,1)}, bf16[768,2816]{1,0:T(8,128)(2,1)}) fusion(f32[768,5632]{1,0:T(8,128)} %copy-done.1, bf16[2048,2816]{0,1:T(8,128)(2,1)} %all-gather.8.cloned.1.call-done, bf16[384,2048]{1,0:T(8,128)(2,1)} %copy-done.107, bf16[384,2048]{1,0:T(8,128)(2,1)} %copy-done.42), kind=kOutput, calls=%fused_computation.12 | convolution fusion | flops 8892776448 | bytes 40632320 | tf_op jit(solution)/shard_map/dot_general | solution.py:29
  598.1 8.0 pad_maximum_fusion
  606.1 24.2 %fusion.169 = f32[768,2048]{1,0:T(8,128)S(1)} fusion(bf16[768,5632]{1,0:T(8,128)(2,1)} %pad_maximum_fusion, bf16[2048,5632]{1,0:T(8,128)(2,1)} %all-gather.6.cloned.1.call-done), kind=kOutput, calls=%fused_computation.437 | convolution fusion | flops 17716740096 | bytes 38010880 | tf_op jit(solution)/shard_map/dot_general | solution.py:33
  637.6 6.8 collective-permute-start.37
  644.4 24.2 %convolution_convert_fusion = bf16[2048,5632]{1,0:T(8,128)(2,1)} fusion(bf16[384,2048]{1,0:T(8,128)(2,1)} %collective-permute-done.26, bf16[384,2048]{1,0:T(8,128)(2,1)} %copy-done.43, bf16[768,2816]{1,0:T(8,128)(2,1)} %get-tuple-element.188, bf16[768,2816]{1,0:T(8,128)(2,1)S(1)} %bitcast.218), kind=kOutput, calls=%fused_computation.1 | convolution fusion | flops 17751867392 | bytes 34865152 | tf_op jit(solution)/shard_map/dot_general | solution.py:39
  668.6 5.4 collective-permute-done.37
  674.1 20.4 %reduce-scatter.4.cloned.1.call-done = bf16[512,2816]{0,1:T(8,128)(2,1)} async-done(((bf16[2048,2816]{0,1:T(8,128)(2,1)}), bf16[512,2816]{0,1:T(8,128)(2,1)}) %reduce-scatter.4.cloned.1.call-update) | async-done | bytes 2883600 | tf_op jit(solution)/shard_map/reduce_scatter | solution.py:99
  705.4 15.7 %collective-permute-done.39 = bf16[96,2048]{1,0:T(8,128)(2,1)S(1)} collective-permute-done((bf16[96,2048]{1,0:T(8,128)(2,1)S(1)}, bf16[96,2048]{1,0:T(8,128)(2,1)S(1)}, u32[]{:S(2)}, u32[]{:S(2)}) %collective-permute-start.39) | collective-permute-done | bytes 393248 | tf_op jit(solution)/shard_map/ppermute | solution.py:86
  721.2 9.2 collective-permute-done.40
  772.3 7.9 collective-permute-start.43
  782.9 5.2 convolution_convert_fusion.2
  788.1 8.1 dynamic_update_slice.180
  796.4 9.5 constant_dynamic-update-slice_fusion
  811.4 14.6 %collective-permute-done.43 = bf16[4,8,128,128]{2,3,1,0:T(8,128)(2,1)} collective-permute-done((bf16[4,8,128,128]{2,3,1,0:T(8,128)(2,1)}, bf16[4,8,128,128]{2,3,1,0:T(8,128)(2,1)}, u32[]{:S(2)}, u32[]{:S(2)}) %collective-permute-start.43) | collective-permute-done | bytes 1048608 | tf_op jit(solution)/shard_map/ppermute | solution.py:86
  826.0 26.5 %collective-permute-done.44 = bf16[4,8,128,128]{2,3,1,0:T(8,128)(2,1)} collective-permute-done((bf16[4,8,128,128]{2,3,1,0:T(8,128)(2,1)}, bf16[4,8,128,128]{2,3,1,0:T(8,128)(2,1)}, u32[]{:S(2)}, u32[]{:S(2)}) %collective-permute-start.44) | collective-permute-done | bytes 1048608 | tf_op jit(solution)/shard_map/ppermute | solution.py:86
  862.2 10.8 %fusion.6 = (f32[2048]{0:T(1024)S(1)}, f32[1024,2048]{1,0:T(8,128)}) fusion(bf16[1024,2048]{1,0:T(8,128)(2,1)S(1)} %copy-done.3, f32[1024]{0:T(1024)S(1)} %copy-done.68, f32[1024,2048]{1,0:T(8,128)S(1)} %fusion.38, bf16[1024,1024]{0,1:T(8,128)(2,1)S(1)} %bitcast.228, bf16[2048,2048]{0,1:T(8,128)(2,1)} %all-gather.4.cloned.1.call-done), kind=kOutput, calls=%fused_computation.20 | convolution fusion | flops 4305451008 | bytes 27275264 | tf_op jit(solution)/shard_map/dot_general | solution.py:33
  877.5 24.7 %reduce-scatter.6.cloned.1.call-done = bf16[512,5632]{1,0:T(8,128)(2,1)} async-done(((bf16[2048,5632]{1,0:T(8,128)(2,1)}), bf16[512,5632]{1,0:T(8,128)(2,1)}) %reduce-scatter.6.cloned.1.call-update) | async-done | bytes 5767184 | tf_op jit(solution)/shard_map/reduce_scatter | solution.py:99
  927.0 21.2 %add_divide_fusion = (f32[2,256,5632]{2,1,0:T(8,128)}, f32[2,256,5632]{2,1,0:T(8,128)}, f32[2,256,5632]{2,1,0:T(8,128)}, f32[2,256,5632]{2,1,0:T(8,128)}) fusion(f32[2,256,5632]{2,1,0:T(8,128)S(1)} %bitcast.207, f32[2,256,5632]{2,1,0:T(8,128)} %param.41, bf16[1,256,5632]{2,1,0:T(8,128)(2,1)S(1)} %get-tuple-element.319, ...), kind=kLoop, calls=%fused_computation.7 | loop fusion | flops 37486592 | bytes 74973184 | tf_op jit(solution)/shard_map/div | solution.py:269
  948.8 14.8 %collective-permute-done.50 = bf16[128,2048]{1,0:T(8,128)(2,1)S(1)} collective-permute-done((bf16[128,2048]{1,0:T(8,128)(2,1)S(1)}, bf16[128,2048]{1,0:T(8,128)(2,1)S(1)}, u32[]{:S(2)}, u32[]{:S(2)}) %collective-permute-start.50) | collective-permute-done | bytes 524320 | tf_op jit(solution)/shard_map/ppermute | solution.py:86
  978.7 11.6 %collective-permute-start.54 = (f32[1,1]{1,0:T(1,128)}, f32[1,1]{1,0:T(1,128)}, u32[]{:S(2)}, u32[]{:S(2)}) collective-permute-start(f32[1,1]{1,0:T(1,128)} %add.520), channel_id=1, source_target_pairs={{0,1},{1,0},{2,3},{3,2},{4,5},{5,4},{6,7},{7,6},{8,9},{9,8},{10,11... | collective-permute-start | bytes 20 | tf_op jit(solution)/shard_map/ppermute | solution.py:86
  996.2 11.3 %add_divide_fusion.2 = (f32[5632,256]{1,0:T(8,128)}, f32[5632,256]{1,0:T(8,128)}, f32[5632,256]{1,0:T(8,128)}, f32[5632,256]{1,0:T(8,128)}) fusion(f32[5632,256]{1,0:T(8,128)} %param.43, f32[5632,256]{1,0:T(8,128)} %param.44, bf16[256,2816]{0,1:T(8,128)(2,1)S(1)} %get-tuple-element.200, bf16[256,2816]{0,1:T(8,128)(2,1)S(1)} %collective-permute-done.56, ...), kind=kLoop, calls=%fused_computation.24 | loop fusion | flops 30277632 | bytes 37486592 | tf_op jit(solution)/shard_map/div | solution.py:269
  1007.5 5.8 reduce-scatter.8.cloned.1.call-done
  1028.3 6.4 add_divide_fusion.4
  (612 shorter events, 356.5 us)
Async XLA Ops:
  7.2 164.3 %all-gather.4.cloned.1.call-start = ((), (), s32[]{:S(2)}) async-start(), calls=%async_computation.3 | async-start | bytes 10485760 | tf_op jit(solution)/shard_map/all_gather | solution.py:95
  18.8 340.6 %all-gather.6.cloned.1.call-start = ((), (), s32[]{:S(2)}) async-start(), calls=%async_computation.4 | async-start | bytes 28835840 | tf_op jit(solution)/shard_map/all_gather | solution.py:95
  23.0 10.1 collective-permute-start.3
  28.1 14.2 %collective-permute-start.2 = (bf16[128,640]{1,0:T(8,128)(2,1)S(1)}, bf16[128,640]{1,0:T(8,128)(2,1)S(1)}, u32[]{:S(2)}, u32[]{:S(2)}) collective-permute-start(bf16[128,640]{1,0:T(8,128)(2,1)S(1)} %get-tuple-element.282), channel_id=1, source_target_pairs={{0,2},{1,3},{2,0},{3,1},{4,6},{5,7},{6,4},{7,5},{8,10},{9,11},{10,... | collective-permute-start | bytes 491528 | tf_op jit(solution)/shard_map/ppermute | solution.py:86
  61.0 405.2 %all-gather.8.cloned.1.call-start = ((), (), s32[]{:S(2)}) async-start(), calls=%async_computation.5 | async-start | bytes 14417920 | tf_op jit(solution)/shard_map/all_gather | solution.py:95
  61.0 32.0 %collective-permute-start.8 = (bf16[512,640]{1,0:T(8,128)(2,1)S(1)}, bf16[512,640]{1,0:T(8,128)(2,1)S(1)}, u32[]{:S(2)}, u32[]{:S(2)}) collective-permute-start(bf16[512,640]{1,0:T(8,128)(2,1)S(1)} %bitcast.222), channel_id=1, source_target_pairs={{0,24},{4,28},{8,16},{12,20},{16,8},{20,12},{24,0},{28,4},{1,25},{... | collective-permute-start | bytes 1966088 | tf_op jit(solution)/shard_map/ppermute | solution.py:202
  63.6 44.2 %collective-permute-start.7 = (bf16[512,640]{1,0:T(8,128)(2,1)S(1)}, bf16[512,640]{1,0:T(8,128)(2,1)}, u32[]{:S(2)}, u32[]{:S(2)}) collective-permute-start(bf16[512,640]{1,0:T(8,128)(2,1)S(1)} %bitcast.223), channel_id=1, source_target_pairs={{0,16},{4,20},{8,24},{12,28},{16,0},{20,4},{24,8},{28,12},{1,17},{... | collective-permute-start | bytes 1966088 | tf_op jit(solution)/shard_map/ppermute | solution.py:202
  64.1 57.3 %collective-permute-start.6 = (bf16[512,640]{1,0:T(8,128)(2,1)S(1)}, bf16[512,640]{1,0:T(8,128)(2,1)}, u32[]{:S(2)}, u32[]{:S(2)}) collective-permute-start(bf16[512,640]{1,0:T(8,128)(2,1)S(1)} %bitcast.224), channel_id=1, source_target_pairs={{0,8},{4,12},{8,0},{12,4},{16,24},{20,28},{24,16},{28,20},{1,9},{5... | collective-permute-start | bytes 1966088 | tf_op jit(solution)/shard_map/ppermute | solution.py:202
  71.4 54.7 %collective-permute-start.11 = (bf16[128,2176]{1,0:T(8,128)(2,1)}, bf16[128,2176]{1,0:T(8,128)(2,1)}, u32[]{:S(2)}, u32[]{:S(2)}) collective-permute-start(bf16[128,2176]{1,0:T(8,128)(2,1)} %fusion.75), channel_id=1, source_target_pairs={{0,3},{1,2},{2,1},{3,0},{4,7},{5,6},{6,5},{7,4},{8,11},{9,10},{10,... | collective-permute-start | bytes 1671176 | tf_op jit(solution)/shard_map/ppermute | solution.py:86
  73.8 52.3 %collective-permute-start.10 = (bf16[128,2176]{1,0:T(8,128)(2,1)}, bf16[128,2176]{1,0:T(8,128)(2,1)}, u32[]{:S(2)}, u32[]{:S(2)}) collective-permute-start(bf16[128,2176]{1,0:T(8,128)(2,1)} %fusion.75), channel_id=1, source_target_pairs={{0,2},{1,3},{2,0},{3,1},{4,6},{5,7},{6,4},{7,5},{8,10},{9,11},{10,... | collective-permute-start | bytes 1671176 | tf_op jit(solution)/shard_map/ppermute | solution.py:86
  93.9 33.7 %collective-permute-start.9 = (bf16[128,2176]{1,0:T(8,128)(2,1)}, bf16[128,2176]{1,0:T(8,128)(2,1)}, u32[]{:S(2)}, u32[]{:S(2)}) collective-permute-start(bf16[128,2176]{1,0:T(8,128)(2,1)} %fusion.75), channel_id=1, source_target_pairs={{0,1},{1,0},{2,3},{3,2},{4,5},{5,4},{6,7},{7,6},{8,9},{9,8},{10,11... | collective-permute-start | bytes 1671176 | tf_op jit(solution)/shard_map/ppermute | solution.py:86
  107.8 29.5 %collective-permute-start.17 = (bf16[256,2816]{0,1:T(8,128)(2,1)}, bf16[256,2816]{0,1:T(8,128)(2,1)}, u32[]{:S(2)}, u32[]{:S(2)}) collective-permute-start(bf16[256,2816]{0,1:T(8,128)(2,1)} %dynamic-slice_bitcast_fusion.2), channel_id=1, source_target_pairs={{0,4},{4,0},{8,12},{12,8},{16,20},{20,16},{24,28},{28,24},{1,5},{5... | collective-permute-start | bytes 4325384 | tf_op jit(solution)/shard_map/ppermute | solution.py:80
  139.9 554.5 %reduce-scatter.4.cloned.1.call-start = ((), (), s32[]{:S(2)}) async-start(), calls=%async_computation.6 | async-start | bytes 14417920 | tf_op jit(solution)/shard_map/reduce_scatter | solution.py:99
  164.1 49.2 %collective-permute-start.16 = (bf16[4,8,128,128]{3,2,1,0:T(8,128)(2,1)}, bf16[4,8,128,128]{3,2,1,0:T(8,128)(2,1)}, u32[]{:S(2)}, u32[]{:S(2)}) collective-permute-start(bf16[4,8,128,128]{3,2,1,0:T(8,128)(2,1)} %pad_maximum_fusion.14), channel_id=1, source_target_pairs={{0,2},{1,3},{2,0},{3,1},{4,6},{5,7},{6,4},{7,5},{8,10},{9,11},{10,... | collective-permute-start | bytes 3145736 | tf_op jit(solution)/shard_map/ppermute | solution.py:86
  164.2 71.5 %collective-permute-start.15 = (bf16[4,8,128,128]{3,2,1,0:T(8,128)(2,1)}, bf16[4,8,128,128]{3,2,1,0:T(8,128)(2,1)}, u32[]{:S(2)}, u32[]{:S(2)}) collective-permute-start(bf16[4,8,128,128]{3,2,1,0:T(8,128)(2,1)} %pad_maximum_fusion.14), channel_id=1, source_target_pairs={{0,1},{1,0},{2,3},{3,2},{4,5},{5,4},{6,7},{7,6},{8,9},{9,8},{10,11... | collective-permute-start | bytes 3145736 | tf_op jit(solution)/shard_map/ppermute | solution.py:86
  193.7 53.8 %collective-permute-start.18 = (bf16[4,8,128,128]{3,2,1,0:T(8,128)(2,1)}, bf16[4,8,128,128]{3,2,1,0:T(8,128)(2,1)}, u32[]{:S(2)}, u32[]{:S(2)}) collective-permute-start(bf16[4,8,128,128]{3,2,1,0:T(8,128)(2,1)} %pad_maximum_fusion.14), channel_id=1, source_target_pairs={{0,3},{1,2},{2,1},{3,0},{4,7},{5,6},{6,5},{7,4},{8,11},{9,10},{10,... | collective-permute-start | bytes 3145736 | tf_op jit(solution)/shard_map/ppermute | solution.py:86
  283.8 13.0 %collective-permute-start.22 = (bf16[96,2048]{1,0:T(8,128)(2,1)S(1)}, bf16[96,2048]{1,0:T(8,128)(2,1)S(1)}, u32[]{:S(2)}, u32[]{:S(2)}) collective-permute-start(bf16[96,2048]{1,0:T(8,128)(2,1)S(1)} %get-tuple-element.237), channel_id=1, source_target_pairs={{0,3},{1,2},{2,1},{3,0},{4,7},{5,6},{6,5},{7,4},{8,11},{9,10},{10,... | collective-permute-start | bytes 1179656 | tf_op jit(solution)/shard_map/ppermute | solution.py:86
  285.6 36.7 %collective-permute-start.21 = (bf16[96,2048]{1,0:T(8,128)(2,1)S(1)}, bf16[96,2048]{1,0:T(8,128)(2,1)S(1)}, u32[]{:S(2)}, u32[]{:S(2)}) collective-permute-start(bf16[96,2048]{1,0:T(8,128)(2,1)S(1)} %get-tuple-element.238), channel_id=1, source_target_pairs={{0,2},{1,3},{2,0},{3,1},{4,6},{5,7},{6,4},{7,5},{8,10},{9,11},{10,... | collective-permute-start | bytes 1179656 | tf_op jit(solution)/shard_map/ppermute | solution.py:86
  296.3 26.0 %collective-permute-start.20 = (bf16[96,2048]{1,0:T(8,128)(2,1)S(1)}, bf16[96,2048]{1,0:T(8,128)(2,1)S(1)}, u32[]{:S(2)}, u32[]{:S(2)}) collective-permute-start(bf16[96,2048]{1,0:T(8,128)(2,1)S(1)} %get-tuple-element.239), channel_id=1, source_target_pairs={{0,1},{1,0},{2,3},{3,2},{4,5},{5,4},{6,7},{7,6},{8,9},{9,8},{10,11... | collective-permute-start | bytes 1179656 | tf_op jit(solution)/shard_map/ppermute | solution.py:86
  325.7 17.5 %collective-permute-start.23 = (bf16[96,2048]{1,0:T(8,128)(2,1)S(1)}, bf16[96,2048]{1,0:T(8,128)(2,1)S(1)}, u32[]{:S(2)}, u32[]{:S(2)}) collective-permute-start(bf16[96,2048]{1,0:T(8,128)(2,1)S(1)} %get-tuple-element.235), channel_id=1, source_target_pairs={{0,1},{1,0},{2,3},{3,2},{4,5},{5,4},{6,7},{7,6},{8,9},{9,8},{10,11... | collective-permute-start | bytes 1179656 | tf_op jit(solution)/shard_map/ppermute | solution.py:86
  325.8 29.9 %collective-permute-start.24 = (bf16[96,2048]{1,0:T(8,128)(2,1)S(1)}, bf16[96,2048]{1,0:T(8,128)(2,1)S(1)}, u32[]{:S(2)}, u32[]{:S(2)}) collective-permute-start(bf16[96,2048]{1,0:T(8,128)(2,1)S(1)} %get-tuple-element.234), channel_id=1, source_target_pairs={{0,2},{1,3},{2,0},{3,1},{4,6},{5,7},{6,4},{7,5},{8,10},{9,11},{10,... | collective-permute-start | bytes 1179656 | tf_op jit(solution)/shard_map/ppermute | solution.py:86
  328.1 27.6 %collective-permute-start.25 = (bf16[96,2048]{1,0:T(8,128)(2,1)S(1)}, bf16[96,2048]{1,0:T(8,128)(2,1)S(1)}, u32[]{:S(2)}, u32[]{:S(2)}) collective-permute-start(bf16[96,2048]{1,0:T(8,128)(2,1)S(1)} %get-tuple-element.233), channel_id=1, source_target_pairs={{0,3},{1,2},{2,1},{3,0},{4,7},{5,6},{6,5},{7,4},{8,11},{9,10},{10,... | collective-permute-start | bytes 1179656 | tf_op jit(solution)/shard_map/ppermute | solution.py:86
  489.3 14.0 %collective-permute-start.30 = (bf16[96,2048]{1,0:T(8,128)(2,1)S(1)}, bf16[96,2048]{1,0:T(8,128)(2,1)S(1)}, u32[]{:S(2)}, u32[]{:S(2)}) collective-permute-start(bf16[96,2048]{1,0:T(8,128)(2,1)S(1)} %get-tuple-element.230), channel_id=1, source_target_pairs={{0,3},{1,2},{2,1},{3,0},{4,7},{5,6},{6,5},{7,4},{8,11},{9,10},{10,... | collective-permute-start | bytes 1179656 | tf_op jit(solution)/shard_map/ppermute | solution.py:86
  492.7 34.0 %collective-permute-start.29 = (bf16[96,2048]{1,0:T(8,128)(2,1)S(1)}, bf16[96,2048]{1,0:T(8,128)(2,1)S(1)}, u32[]{:S(2)}, u32[]{:S(2)}) collective-permute-start(bf16[96,2048]{1,0:T(8,128)(2,1)S(1)} %get-tuple-element.231), channel_id=1, source_target_pairs={{0,2},{1,3},{2,0},{3,1},{4,6},{5,7},{6,4},{7,5},{8,10},{9,11},{10,... | collective-permute-start | bytes 1179656 | tf_op jit(solution)/shard_map/ppermute | solution.py:86
  492.7 34.0 %collective-permute-start.28 = (bf16[96,2048]{1,0:T(8,128)(2,1)S(1)}, bf16[96,2048]{1,0:T(8,128)(2,1)S(1)}, u32[]{:S(2)}, u32[]{:S(2)}) collective-permute-start(bf16[96,2048]{1,0:T(8,128)(2,1)S(1)} %get-tuple-element.232), channel_id=1, source_target_pairs={{0,1},{1,0},{2,3},{3,2},{4,5},{5,4},{6,7},{7,6},{8,9},{9,8},{10,11... | collective-permute-start | bytes 1179656 | tf_op jit(solution)/shard_map/ppermute | solution.py:86
  530.4 17.9 %collective-permute-start.31 = (bf16[96,2048]{1,0:T(8,128)(2,1)S(1)}, bf16[96,2048]{1,0:T(8,128)(2,1)S(1)}, u32[]{:S(2)}, u32[]{:S(2)}) collective-permute-start(bf16[96,2048]{1,0:T(8,128)(2,1)S(1)} %get-tuple-element.227), channel_id=1, source_target_pairs={{0,1},{1,0},{2,3},{3,2},{4,5},{5,4},{6,7},{7,6},{8,9},{9,8},{10,11... | collective-permute-start | bytes 1179656 | tf_op jit(solution)/shard_map/ppermute | solution.py:86
  530.5 29.9 %collective-permute-start.32 = (bf16[96,2048]{1,0:T(8,128)(2,1)S(1)}, bf16[96,2048]{1,0:T(8,128)(2,1)S(1)}, u32[]{:S(2)}, u32[]{:S(2)}) collective-permute-start(bf16[96,2048]{1,0:T(8,128)(2,1)S(1)} %get-tuple-element.226), channel_id=1, source_target_pairs={{0,2},{1,3},{2,0},{3,1},{4,6},{5,7},{6,4},{7,5},{8,10},{9,11},{10,... | collective-permute-start | bytes 1179656 | tf_op jit(solution)/shard_map/ppermute | solution.py:86
  533.4 27.0 %collective-permute-start.33 = (bf16[96,2048]{1,0:T(8,128)(2,1)S(1)}, bf16[96,2048]{1,0:T(8,128)(2,1)S(1)}, u32[]{:S(2)}, u32[]{:S(2)}) collective-permute-start(bf16[96,2048]{1,0:T(8,128)(2,1)S(1)} %get-tuple-element.225), channel_id=1, source_target_pairs={{0,3},{1,2},{2,1},{3,0},{4,7},{5,6},{6,5},{7,4},{8,11},{9,10},{10,... | collective-permute-start | bytes 1179656 | tf_op jit(solution)/shard_map/ppermute | solution.py:86
  577.2 325.0 %reduce-scatter.6.cloned.1.call-start = ((), (), s32[]{:S(2)}) async-start(), calls=%async_computation.7 | async-start | bytes 28835840 | tf_op jit(solution)/shard_map/reduce_scatter | solution.py:99
  635.5 33.2 %collective-permute-start.38 = (bf16[96,2048]{1,0:T(8,128)(2,1)}, bf16[96,2048]{1,0:T(8,128)(2,1)}, u32[]{:S(2)}, u32[]{:S(2)}) collective-permute-start(bf16[96,2048]{1,0:T(8,128)(2,1)} %get-tuple-element.222), channel_id=1, source_target_pairs={{0,3},{1,2},{2,1},{3,0},{4,7},{5,6},{6,5},{7,4},{8,11},{9,10},{10,... | collective-permute-start | bytes 1179656 | tf_op jit(solution)/shard_map/ppermute | solution.py:86
  637.6 36.4 %collective-permute-start.37 = (bf16[96,2048]{1,0:T(8,128)(2,1)S(1)}, bf16[96,2048]{1,0:T(8,128)(2,1)}, u32[]{:S(2)}, u32[]{:S(2)}) collective-permute-start(bf16[96,2048]{1,0:T(8,128)(2,1)S(1)} %get-tuple-element.223), channel_id=1, source_target_pairs={{0,2},{1,3},{2,0},{3,1},{4,6},{5,7},{6,4},{7,5},{8,10},{9,11},{10,... | collective-permute-start | bytes 1179656 | tf_op jit(solution)/shard_map/ppermute | solution.py:86
  644.4 29.7 %collective-permute-start.36 = (bf16[96,2048]{1,0:T(8,128)(2,1)S(1)}, bf16[96,2048]{1,0:T(8,128)(2,1)}, u32[]{:S(2)}, u32[]{:S(2)}) collective-permute-start(bf16[96,2048]{1,0:T(8,128)(2,1)S(1)} %get-tuple-element.224), channel_id=1, source_target_pairs={{0,1},{1,0},{2,3},{3,2},{4,5},{5,4},{6,7},{7,6},{8,9},{9,8},{10,11... | collective-permute-start | bytes 1179656 | tf_op jit(solution)/shard_map/ppermute | solution.py:86
  694.5 318.9 %reduce-scatter.8.cloned.1.call-start = ((), (), s32[]{:S(2)}) async-start(), calls=%async_computation.8 | async-start | bytes 13762560 | tf_op jit(solution)/shard_map/reduce_scatter | solution.py:99
  700.7 29.7 %collective-permute-start.40 = (bf16[96,2048]{1,0:T(8,128)(2,1)S(1)}, bf16[96,2048]{1,0:T(8,128)(2,1)S(1)}, u32[]{:S(2)}, u32[]{:S(2)}) collective-permute-start(bf16[96,2048]{1,0:T(8,128)(2,1)S(1)} %get-tuple-element.219), channel_id=1, source_target_pairs={{0,2},{1,3},{2,0},{3,1},{4,6},{5,7},{6,4},{7,5},{8,10},{9,11},{10,... | collective-permute-start | bytes 1179656 | tf_op jit(solution)/shard_map/ppermute | solution.py:86
  703.2 18.0 %collective-permute-start.39 = (bf16[96,2048]{1,0:T(8,128)(2,1)S(1)}, bf16[96,2048]{1,0:T(8,128)(2,1)S(1)}, u32[]{:S(2)}, u32[]{:S(2)}) collective-permute-start(bf16[96,2048]{1,0:T(8,128)(2,1)S(1)} %get-tuple-element.220), channel_id=1, source_target_pairs={{0,1},{1,0},{2,3},{3,2},{4,5},{5,4},{6,7},{7,6},{8,9},{9,8},{10,11... | collective-permute-start | bytes 1179656 | tf_op jit(solution)/shard_map/ppermute | solution.py:86
  704.9 25.6 %collective-permute-start.41 = (bf16[96,2048]{1,0:T(8,128)(2,1)S(1)}, bf16[96,2048]{1,0:T(8,128)(2,1)S(1)}, u32[]{:S(2)}, u32[]{:S(2)}) collective-permute-start(bf16[96,2048]{1,0:T(8,128)(2,1)S(1)} %get-tuple-element.218), channel_id=1, source_target_pairs={{0,3},{1,2},{2,1},{3,0},{4,7},{5,6},{6,5},{7,4},{8,11},{9,10},{10,... | collective-permute-start | bytes 1179656 | tf_op jit(solution)/shard_map/ppermute | solution.py:86
  772.3 53.7 %collective-permute-start.43 = (bf16[4,8,128,128]{2,3,1,0:T(8,128)(2,1)}, bf16[4,8,128,128]{2,3,1,0:T(8,128)(2,1)}, u32[]{:S(2)}, u32[]{:S(2)}) collective-permute-start(bf16[4,8,128,128]{2,3,1,0:T(8,128)(2,1)} %pad_maximum_fusion.15), channel_id=1, source_target_pairs={{0,1},{1,0},{2,3},{3,2},{4,5},{5,4},{6,7},{7,6},{8,9},{9,8},{10,11... | collective-permute-start | bytes 3145736 | tf_op jit(solution)/shard_map/ppermute | solution.py:86
  781.2 71.3 %collective-permute-start.44 = (bf16[4,8,128,128]{2,3,1,0:T(8,128)(2,1)}, bf16[4,8,128,128]{2,3,1,0:T(8,128)(2,1)}, u32[]{:S(2)}, u32[]{:S(2)}) collective-permute-start(bf16[4,8,128,128]{2,3,1,0:T(8,128)(2,1)} %pad_maximum_fusion.16), channel_id=1, source_target_pairs={{0,2},{1,3},{2,0},{3,1},{4,6},{5,7},{6,4},{7,5},{8,10},{9,11},{10,... | collective-permute-start | bytes 3145736 | tf_op jit(solution)/shard_map/ppermute | solution.py:86
  805.9 46.6 %collective-permute-start.45 = (bf16[4,8,128,128]{2,3,1,0:T(8,128)(2,1)S(1)}, bf16[4,8,128,128]{2,3,1,0:T(8,128)(2,1)S(1)}, u32[]{:S(2)}, u32[]{:S(2)}) collective-permute-start(bf16[4,8,128,128]{2,3,1,0:T(8,128)(2,1)S(1)} %pad_maximum_fusion.17), channel_id=1, source_target_pairs={{0,3},{1,2},{2,1},{3,0},{4,7},{5,6},{6,5},{7,4},{8,11},{9,10},{10,... | collective-permute-start | bytes 3145736 | tf_op jit(solution)/shard_map/ppermute | solution.py:86
  909.6 12.7 %collective-permute-start.49 = (bf16[256,5632]{1,0:T(8,128)(2,1)}, bf16[256,5632]{1,0:T(8,128)(2,1)}, u32[]{:S(2)}, u32[]{:S(2)}) collective-permute-start(bf16[256,5632]{1,0:T(8,128)(2,1)} %constant_dynamic-slice_fusion.7), channel_id=1, source_target_pairs={{0,4},{4,0},{8,12},{12,8},{16,20},{20,16},{24,28},{28,24},{1,5},{5... | collective-permute-start | bytes 8650760 | tf_op jit(solution)/shard_map/ppermute | solution.py:80
  916.3 32.5 %collective-permute-start.47 = (bf16[128,2048]{1,0:T(8,128)(2,1)}, bf16[128,2048]{1,0:T(8,128)(2,1)}, u32[]{:S(2)}, u32[]{:S(2)}) collective-permute-start(bf16[128,2048]{1,0:T(8,128)(2,1)} %get-tuple-element.205), channel_id=1, source_target_pairs={{0,1},{1,0},{2,3},{3,2},{4,5},{5,4},{6,7},{7,6},{8,9},{9,8},{10,11... | collective-permute-start | bytes 1572872 | tf_op jit(solution)/shard_map/ppermute | solution.py:86
  917.7 31.1 %collective-permute-start.48 = (bf16[128,2048]{1,0:T(8,128)(2,1)}, bf16[128,2048]{1,0:T(8,128)(2,1)}, u32[]{:S(2)}, u32[]{:S(2)}) collective-permute-start(bf16[128,2048]{1,0:T(8,128)(2,1)} %get-tuple-element.207), channel_id=1, source_target_pairs={{0,2},{1,3},{2,0},{3,1},{4,6},{5,7},{6,4},{7,5},{8,10},{9,11},{10,... | collective-permute-start | bytes 1572872 | tf_op jit(solution)/shard_map/ppermute | solution.py:86
  948.2 15.4 %collective-permute-start.50 = (bf16[128,2048]{1,0:T(8,128)(2,1)S(1)}, bf16[128,2048]{1,0:T(8,128)(2,1)S(1)}, u32[]{:S(2)}, u32[]{:S(2)}) collective-permute-start(bf16[128,2048]{1,0:T(8,128)(2,1)S(1)} %get-tuple-element.70), channel_id=1, source_target_pairs={{0,3},{1,2},{2,1},{3,0},{4,7},{5,6},{6,5},{7,4},{8,11},{9,10},{10,... | collective-permute-start | bytes 1572872 | tf_op jit(solution)/shard_map/ppermute | solution.py:86
  966.0 30.2 %collective-permute-start.56 = (bf16[256,2816]{0,1:T(8,128)(2,1)S(1)}, bf16[256,2816]{0,1:T(8,128)(2,1)S(1)}, u32[]{:S(2)}, u32[]{:S(2)}) collective-permute-start(bf16[256,2816]{0,1:T(8,128)(2,1)S(1)} %get-tuple-element.199), channel_id=1, source_target_pairs={{0,4},{4,0},{8,12},{12,8},{16,20},{20,16},{24,28},{28,24},{1,5},{5... | collective-permute-start | bytes 4325384 | tf_op jit(solution)/shard_map/ppermute | solution.py:80
  978.7 11.8 %collective-permute-start.54 = (f32[1,1]{1,0:T(1,128)}, f32[1,1]{1,0:T(1,128)}, u32[]{:S(2)}, u32[]{:S(2)}) collective-permute-start(f32[1,1]{1,0:T(1,128)} %add.520), channel_id=1, source_target_pairs={{0,1},{1,0},{2,3},{3,2},{4,5},{5,4},{6,7},{7,6},{8,9},{9,8},{10,11... | collective-permute-start | bytes 20 | tf_op jit(solution)/shard_map/ppermute | solution.py:86
  1021.5 17.1 %collective-permute-start.60 = (bf16[2,64,640]{2,1,0:T(8,128)(2,1)}, bf16[2,64,640]{2,1,0:T(8,128)(2,1)}, u32[]{:S(2)}, u32[]{:S(2)}) collective-permute-start(bf16[2,64,640]{2,1,0:T(8,128)(2,1)} %get-tuple-element.259), channel_id=1, source_target_pairs={{0,3},{1,2},{2,1},{3,0},{4,7},{5,6},{6,5},{7,4},{8,11},{9,10},{10,... | collective-permute-start | bytes 491528 | tf_op jit(solution)/shard_map/ppermute | solution.py:86
  1024.8 14.7 %collective-permute-start.59 = (bf16[2,64,640]{2,1,0:T(8,128)(2,1)}, bf16[2,64,640]{2,1,0:T(8,128)(2,1)}, u32[]{:S(2)}, u32[]{:S(2)}) collective-permute-start(bf16[2,64,640]{2,1,0:T(8,128)(2,1)} %get-tuple-element.260), channel_id=1, source_target_pairs={{0,2},{1,3},{2,0},{3,1},{4,6},{5,7},{6,4},{7,5},{8,10},{9,11},{10,... | collective-permute-start | bytes 491528 | tf_op jit(solution)/shard_map/ppermute | solution.py:86
  1024.8 14.7 %collective-permute-start.58 = (bf16[2,64,640]{2,1,0:T(8,128)(2,1)S(1)}, bf16[2,64,640]{2,1,0:T(8,128)(2,1)}, u32[]{:S(2)}, u32[]{:S(2)}) collective-permute-start(bf16[2,64,640]{2,1,0:T(8,128)(2,1)S(1)} %get-tuple-element.261), channel_id=1, source_target_pairs={{0,1},{1,0},{2,3},{3,2},{4,5},{5,4},{6,7},{7,6},{8,9},{9,8},{10,11... | collective-permute-start | bytes 491528 | tf_op jit(solution)/shard_map/ppermute | solution.py:86
  (141 other events, 1842.4 us)
Sparse Core Ops, SparseCore 0:
  18.9 118.2 all-gather.3
  139.6 210.3 all-gather.5
  352.5 113.6 all-gather.7
  577.4 117.0 reduce-scatter.3
  697.4 204.7 reduce-scatter.5
  905.5 107.8 reduce-scatter.7

commit v4 on v3

--- a/solution.py
+++ b/solution.py
@@ -188,7 +188,7 @@
 def return_rows(partial, partners, places=None, between=()):
     count = partial.shape[0] // 2
     got = core_swap(partial[count:].astype(BF16))
-    summed = (partial[:count] + got.astype(F32)).astype(BF16)
+    summed = (partial[:count].astype(F32) + got.astype(F32)).astype(BF16)
     rows = count // partners
     places = range(partners) if places is None else places
     blocks = [lax.dynamic_slice_in_dim(summed, place * rows, rows, 0) for place in places]
@@ -209,6 +209,25 @@
         whole = lax.dynamic_update_slice_in_dim(
             whole, over_chips(block, bits), (chip ^ bits) * rows, 0
         )
+    return whole
+
+
+def gather_split(chip, block):
+    if lax.axis_size("dp") != 8:
+        return gather_small(chip, block)
+    rows = block.shape[0]
+    middle = rows // 2
+    across, along = over_chips(block, 1), over_chips(block, 2)
+    pieces = [
+        (block, chip, 0),
+        (across, chip ^ 1, 0),
+        (along, chip ^ 2, 0),
+        (over_chips(across[:middle], 2), chip ^ 3, 0),
+        (over_chips(along[middle:], 1), chip ^ 3, middle),
+    ]
+    whole = jnp.zeros((4 * rows, block.shape[1]), block.dtype)
+    for piece, place, start in pieces:
+        whole = lax.dynamic_update_slice_in_dim(whole, piece, place * rows + start, 0)
     return whole
 
 
@@ -395,7 +414,7 @@
             (core_swap(up_theirs.astype(BF16)), row_got, width_ff),
         ],
     )
-    shared_whole = gather_small(chip, arrived)
+    shared_whole = gather_split(chip, arrived)
     shared_whole, token_blocks, _ = together(shared_whole, token_blocks, gate_up_rows)
     everyone = place_rows(token_blocks, places)
     kv_weight = shared_whole[:, : 2 * sixth]
@@ -483,7 +502,7 @@
     gate_up_val = matmul(rows_two, weight_gate_up)
     gate_val, up_val = gate_up_val[:, :width_ff], gate_up_val[:, width_ff:]
     active = (jax.nn.silu(gate_val) * up_val).astype(BF16)
-    mlp_rows = jnp.concatenate(return_rows(matmul_back(active, weight_down), partners))
+    mlp_rows = jnp.concatenate(return_rows(matmul_back(active, weight_down).astype(BF16), partners))
     mlp_branch = [matmul(mlp_back[choice], mlp_rows) for choice in range(TOP)]
     outputs = hidden + sum(gates_mlp[:, choice, None] * mlp_branch[choice] for choice in range(TOP))
 

time: 1070 us -> 1060 us (level)
  waiting for transfers between devices: 428 us -> 417 us
    ppermute x3 -> x4, waiting for transfers between devices: 39.4 us -> 29.6 us  [over_chips(): return lax.ppermute(value, 'dp', swap_perm(lax.axis_size('dp'), 2 * bits))]
    unnamed x246 -> x242, local copies, waits for them, and re-layouts: 29.2 us -> 25.1 us
  transfers between devices with their start and end apart: 67 -> 68, of which waited for: 40 -> 40; matrix products, arithmetic and copies ran while one was open for 41% -> 41% of each run, Pallas kernels for 0% -> 0%
where the time goes in v4:
time: 1060 us; the launch traced here: 1050 us
  waiting for transfers between devices  417 us (39%)
  matrix products  216 us (20%)
  local copies, waits for them, and re-layouts  180 us (17%)
  other arithmetic  107 us (10%)
  starting transfers between devices  104 us (10%)
  between operations  22.9 us (2%)
    ppermute x38, waiting for transfers between devices, over_expert(): lax.ppermute(value, 'expert', swap_perm(lax.axis_size('expert'), bits))  245 us
    ppermute x38, starting transfers between devices, over_expert(): lax.ppermute(value, 'expert', swap_perm(lax.axis_size('expert'), bits))  88.3 us
    all_gather x3, waiting for transfers between devices, gather_chips(): lax.all_gather(block, 'dp', axis=0, tiled=True, axis_index_groups=chip_gr...  72.1 us
    dot_general x13, matrix products, matmul(): return jnp.dot(left_side, right_side, preferred_element_type=F32)  72 us
    dot_general x5, matrix products, matmul_back(): lax.dot_general(left_side, right_side, (((1,), (1,)), ((), ())), preferre...  58.5 us
    dot_general x5, matrix products, matmul_rows(): lax.dot_general(left_side, right_side, (((0,), (0,)), ((), ())), preferre...  54.8 us
    reduce_scatter x3, waiting for transfers between devices, scatter_chips(): lax.psum_scatter(partial, 'dp', scatter_dimension=0, tiled=True, axis_ind...  50.1 us
    div x7, other arithmetic, adam_step(): direction = moment_hat / (jnp.sqrt(square_hat) + ADAM_EPS)  47.5 us
  transfers between devices with their start and end apart: 68, of which 40 were waited for; matrix products, arithmetic and copies ran while one was open for 41% of the time, Pallas kernels for 0%

profile of v4, /device:TPU:0, one launch (start us, length us, event | category | flops | bytes accessed | tf_op | source)
XLA Modules:
  0.0 1047.2 jit_solution(3979220638337229505)
XLA Ops:
  23.0 5.0 collective-permute-start.3
  37.2 5.1 collective-permute-done.2
  42.5 5.0 fusion.148
  75.5 20.3 %collective-permute-done.7 = bf16[512,640]{1,0:T(8,128)(2,1)} collective-permute-done((bf16[512,640]{1,0:T(8,128)(2,1)S(1)}, bf16[512,640]{1,0:T(8,128)(2,1)}, u32[]{:S(2)}, u32[]{:S(2)}) %collective-permute-start.7) | collective-permute-done | bytes 655392 | tf_op jit(solution)/shard_map/ppermute | solution.py:202
  107.4 7.4 collective-permute-done.9
  164.6 10.0 fusion.20
  174.6 5.7 copy.346
  180.3 5.1 fusion.151
  191.1 15.3 %collective-permute-done.17 = bf16[4,8,128,128]{3,2,1,0:T(8,128)(2,1)} collective-permute-done((bf16[4,8,128,128]{3,2,1,0:T(8,128)(2,1)}, bf16[4,8,128,128]{3,2,1,0:T(8,128)(2,1)}, u32[]{:S(2)}, u32[]{:S(2)}) %collective-permute-start.17) | collective-permute-done | bytes 1048608 | tf_op jit(solution)/shard_map/ppermute | solution.py:86
  210.1 18.7 %collective-permute-done.16 = bf16[4,8,128,128]{3,2,1,0:T(8,128)(2,1)} collective-permute-done((bf16[4,8,128,128]{3,2,1,0:T(8,128)(2,1)}, bf16[4,8,128,128]{3,2,1,0:T(8,128)(2,1)}, u32[]{:S(2)}, u32[]{:S(2)}) %collective-permute-start.16) | collective-permute-done | bytes 1048608 | tf_op jit(solution)/shard_map/ppermute | solution.py:86
  245.9 5.4 fusion.164
  262.0 6.0 fusion.17
  278.6 10.7 %collective-permute-start.22 = (bf16[96,2048]{1,0:T(8,128)(2,1)S(1)}, bf16[96,2048]{1,0:T(8,128)(2,1)S(1)}, u32[]{:S(2)}, u32[]{:S(2)}) collective-permute-start(bf16[96,2048]{1,0:T(8,128)(2,1)S(1)} %get-tuple-element.238), channel_id=1, source_target_pairs={{0,2},{1,3},{2,0},{3,1},{4,6},{5,7},{6,4},{7,5},{8,10},{9,11},{10,... | collective-permute-start | bytes 1179656 | tf_op jit(solution)/shard_map/ppermute | solution.py:86
  289.9 25.5 %collective-permute-done.22 = bf16[96,2048]{1,0:T(8,128)(2,1)S(1)} collective-permute-done((bf16[96,2048]{1,0:T(8,128)(2,1)S(1)}, bf16[96,2048]{1,0:T(8,128)(2,1)S(1)}, u32[]{:S(2)}, u32[]{:S(2)}) %collective-permute-start.22) | collective-permute-done | bytes 393248 | tf_op jit(solution)/shard_map/ppermute | solution.py:86
  323.3 13.1 %collective-permute-done.24 = bf16[96,2048]{1,0:T(8,128)(2,1)S(1)} collective-permute-done((bf16[96,2048]{1,0:T(8,128)(2,1)S(1)}, bf16[96,2048]{1,0:T(8,128)(2,1)S(1)}, u32[]{:S(2)}, u32[]{:S(2)}) %collective-permute-start.24) | collective-permute-done | bytes 393248 | tf_op jit(solution)/shard_map/ppermute | solution.py:86
  336.4 12.4 %collective-permute-done.25 = bf16[96,2048]{1,0:T(8,128)(2,1)S(1)} collective-permute-done((bf16[96,2048]{1,0:T(8,128)(2,1)S(1)}, bf16[96,2048]{1,0:T(8,128)(2,1)S(1)}, u32[]{:S(2)}, u32[]{:S(2)}) %collective-permute-start.25) | collective-permute-done | bytes 393248 | tf_op jit(solution)/shard_map/ppermute | solution.py:86
  352.5 24.6 %fusion.36 = f32[768,5632]{1,0:T(8,128)S(1)} fusion(bf16[2048,5632]{1,0:T(8,128)(2,1)} %all-gather.6.cloned.1.call-done, bf16[384,2048]{1,0:T(8,128)(2,1)} %collective-permute-done.27, bf16[384,2048]{1,0:T(8,128)(2,1)S(1)} %constant_dynamic-update-slice_fusion.7), kind=kOutput, calls=%fused_computation.104 | convolution fusion | flops 17723031552 | bytes 43515904 | tf_op jit(solution)/shard_map/dot_general | solution.py:29
  377.1 5.9 copy-done.1
  387.1 72.1 %all-gather.8.cloned.1.call-done = bf16[2048,2816]{0,1:T(8,128)(2,1)} async-done(((bf16[512,2816]{0,1:T(8,128)(2,1)}), bf16[2048,2816]{0,1:T(8,128)(2,1)}) %all-gather.8.cloned.1.call-update) | async-done | bytes 11534352 | tf_op jit(solution)/shard_map/all_gather | solution.py:95
  459.2 13.4 %convolution_convert_fusion.4 = bf16[768,2048]{1,0:T(8,128)(2,1)S(1)} fusion(bf16[768,2816]{1,0:T(8,128)(2,1)} %multiply_convert_fusion.2, bf16[2048,2816]{0,1:T(8,128)(2,1)} %all-gather.8.cloned.1.call-done), kind=kOutput, calls=%fused_computation.56 | convolution fusion | flops 8859942912 | bytes 19005440 | tf_op jit(solution)/shard_map/dot_general | solution.py:33
  485.3 9.5 collective-permute-done.31
  494.8 23.3 %collective-permute-done.30 = bf16[96,2048]{1,0:T(8,128)(2,1)S(1)} collective-permute-done((bf16[96,2048]{1,0:T(8,128)(2,1)S(1)}, bf16[96,2048]{1,0:T(8,128)(2,1)S(1)}, u32[]{:S(2)}, u32[]{:S(2)}) %collective-permute-start.30) | collective-permute-done | bytes 393248 | tf_op jit(solution)/shard_map/ppermute | solution.py:86
  526.4 13.0 %collective-permute-done.32 = bf16[96,2048]{1,0:T(8,128)(2,1)S(1)} collective-permute-done((bf16[96,2048]{1,0:T(8,128)(2,1)S(1)}, bf16[96,2048]{1,0:T(8,128)(2,1)S(1)}, u32[]{:S(2)}, u32[]{:S(2)}) %collective-permute-start.32) | collective-permute-done | bytes 393248 | tf_op jit(solution)/shard_map/ppermute | solution.py:86
  539.5 12.3 %collective-permute-done.33 = bf16[96,2048]{1,0:T(8,128)(2,1)S(1)} collective-permute-done((bf16[96,2048]{1,0:T(8,128)(2,1)S(1)}, bf16[96,2048]{1,0:T(8,128)(2,1)S(1)}, u32[]{:S(2)}, u32[]{:S(2)}) %collective-permute-start.33) | collective-permute-done | bytes 393248 | tf_op jit(solution)/shard_map/ppermute | solution.py:86
  556.5 12.2 %convolution_convert_fusion.1 = bf16[2048,2816]{0,1:T(8,128)(2,1)} fusion(bf16[768,2816]{1,0:T(8,128)(2,1)S(1)} %bitcast.216, bf16[384,2048]{1,0:T(8,128)(2,1)S(1)} %collective-permute-done.35, bf16[384,2048]{1,0:T(8,128)(2,1)S(1)} %constant_dynamic-update-slice_fusion.4), kind=kOutput, calls=%fused_computation.9 | convolution fusion | flops 8870428672 | bytes 19005440 | tf_op jit(solution)/shard_map/dot_general | solution.py:39
  568.7 20.8 %multiply_convert_fusion.1 = (bf16[768,2816]{1,0:T(8,128)(2,1)}, bf16[768,2816]{1,0:T(8,128)(2,1)}) fusion(f32[768,5632]{1,0:T(8,128)} %copy-done.1, bf16[2048,2816]{0,1:T(8,128)(2,1)} %all-gather.8.cloned.1.call-done, bf16[384,2048]{1,0:T(8,128)(2,1)} %copy-done.105, bf16[384,2048]{1,0:T(8,128)(2,1)} %copy-done.41), kind=kOutput, calls=%fused_computation.12 | convolution fusion | flops 8892776448 | bytes 40632320 | tf_op jit(solution)/shard_map/dot_general | solution.py:29
  589.5 8.0 pad_maximum_fusion
  597.5 24.2 %fusion.167 = f32[768,2048]{1,0:T(8,128)S(1)} fusion(bf16[768,5632]{1,0:T(8,128)(2,1)} %pad_maximum_fusion, bf16[2048,5632]{1,0:T(8,128)(2,1)} %all-gather.6.cloned.1.call-done), kind=kOutput, calls=%fused_computation.436 | convolution fusion | flops 17716740096 | bytes 38010880 | tf_op jit(solution)/shard_map/dot_general | solution.py:33
  629.1 6.6 collective-permute-start.38
  635.7 24.3 %convolution_convert_fusion = bf16[2048,5632]{1,0:T(8,128)(2,1)} fusion(bf16[384,2048]{1,0:T(8,128)(2,1)} %collective-permute-done.27, bf16[384,2048]{1,0:T(8,128)(2,1)} %copy-done.42, bf16[768,2816]{1,0:T(8,128)(2,1)} %get-tuple-element.188, bf16[768,2816]{1,0:T(8,128)(2,1)S(1)} %bitcast.218), kind=kOutput, calls=%fused_computation.1 | convolution fusion | flops 17751867392 | bytes 34865152 | tf_op jit(solution)/shard_map/dot_general | solution.py:39
  660.0 5.6 collective-permute-done.38
  665.5 20.2 %reduce-scatter.4.cloned.1.call-done = bf16[512,2816]{0,1:T(8,128)(2,1)} async-done(((bf16[2048,2816]{0,1:T(8,128)(2,1)}), bf16[512,2816]{0,1:T(8,128)(2,1)}) %reduce-scatter.4.cloned.1.call-update) | async-done | bytes 2883600 | tf_op jit(solution)/shard_map/reduce_scatter | solution.py:99
  696.8 15.7 %collective-permute-done.40 = bf16[96,2048]{1,0:T(8,128)(2,1)S(1)} collective-permute-done((bf16[96,2048]{1,0:T(8,128)(2,1)S(1)}, bf16[96,2048]{1,0:T(8,128)(2,1)S(1)}, u32[]{:S(2)}, u32[]{:S(2)}) %collective-permute-start.40) | collective-permute-done | bytes 393248 | tf_op jit(solution)/shard_map/ppermute | solution.py:86
  712.5 9.2 collective-permute-done.41
  763.6 7.9 collective-permute-start.44
  774.2 5.2 convolution_convert_fusion.2
  779.4 8.1 dynamic_update_slice.184
  787.7 9.5 constant_dynamic-update-slice_fusion
  802.7 14.6 %collective-permute-done.44 = bf16[4,8,128,128]{2,3,1,0:T(8,128)(2,1)} collective-permute-done((bf16[4,8,128,128]{2,3,1,0:T(8,128)(2,1)}, bf16[4,8,128,128]{2,3,1,0:T(8,128)(2,1)}, u32[]{:S(2)}, u32[]{:S(2)}) %collective-permute-start.44) | collective-permute-done | bytes 1048608 | tf_op jit(solution)/shard_map/ppermute | solution.py:86
  817.3 26.5 %collective-permute-done.45 = bf16[4,8,128,128]{2,3,1,0:T(8,128)(2,1)} collective-permute-done((bf16[4,8,128,128]{2,3,1,0:T(8,128)(2,1)}, bf16[4,8,128,128]{2,3,1,0:T(8,128)(2,1)}, u32[]{:S(2)}, u32[]{:S(2)}) %collective-permute-start.45) | collective-permute-done | bytes 1048608 | tf_op jit(solution)/shard_map/ppermute | solution.py:86
  853.5 10.8 %fusion.6 = (f32[2048]{0:T(1024)S(1)}, f32[1024,2048]{1,0:T(8,128)}) fusion(bf16[1024,2048]{1,0:T(8,128)(2,1)S(1)} %copy-done.3, f32[1024]{0:T(1024)S(1)} %copy-done.66, f32[1024,2048]{1,0:T(8,128)S(1)} %fusion.37, bf16[1024,1024]{0,1:T(8,128)(2,1)S(1)} %bitcast.227, bf16[2048,2048]{0,1:T(8,128)(2,1)} %all-gather.4.cloned.1.call-done), kind=kOutput, calls=%fused_computation.20 | convolution fusion | flops 4305451008 | bytes 27275264 | tf_op jit(solution)/shard_map/dot_general | solution.py:33
  868.9 24.6 %reduce-scatter.6.cloned.1.call-done = bf16[512,5632]{1,0:T(8,128)(2,1)} async-done(((bf16[2048,5632]{1,0:T(8,128)(2,1)}), bf16[512,5632]{1,0:T(8,128)(2,1)}) %reduce-scatter.6.cloned.1.call-update) | async-done | bytes 5767184 | tf_op jit(solution)/shard_map/reduce_scatter | solution.py:99
  918.3 21.2 %add_divide_fusion = (f32[2,256,5632]{2,1,0:T(8,128)}, f32[2,256,5632]{2,1,0:T(8,128)}, f32[2,256,5632]{2,1,0:T(8,128)}, f32[2,256,5632]{2,1,0:T(8,128)}) fusion(f32[2,256,5632]{2,1,0:T(8,128)S(1)} %bitcast.207, f32[2,256,5632]{2,1,0:T(8,128)} %param.41, bf16[1,256,5632]{2,1,0:T(8,128)(2,1)S(1)} %get-tuple-element.319, ...), kind=kLoop, calls=%fused_computation.7 | loop fusion | flops 37486592 | bytes 74973184 | tf_op jit(solution)/shard_map/div | solution.py:288
  940.1 14.8 %collective-permute-done.51 = bf16[128,2048]{1,0:T(8,128)(2,1)S(1)} collective-permute-done((bf16[128,2048]{1,0:T(8,128)(2,1)S(1)}, bf16[128,2048]{1,0:T(8,128)(2,1)S(1)}, u32[]{:S(2)}, u32[]{:S(2)}) %collective-permute-start.51) | collective-permute-done | bytes 524320 | tf_op jit(solution)/shard_map/ppermute | solution.py:86
  970.2 11.6 %collective-permute-start.55 = (f32[1,1]{1,0:T(1,128)}, f32[1,1]{1,0:T(1,128)}, u32[]{:S(2)}, u32[]{:S(2)}) collective-permute-start(f32[1,1]{1,0:T(1,128)} %add.530), channel_id=1, source_target_pairs={{0,1},{1,0},{2,3},{3,2},{4,5},{5,4},{6,7},{7,6},{8,9},{9,8},{10,11... | collective-permute-start | bytes 20 | tf_op jit(solution)/shard_map/ppermute | solution.py:86
  987.9 11.5 %add_divide_fusion.2 = (f32[5632,256]{1,0:T(8,128)}, f32[5632,256]{1,0:T(8,128)}, f32[5632,256]{1,0:T(8,128)}, f32[5632,256]{1,0:T(8,128)}) fusion(f32[5632,256]{1,0:T(8,128)} %param.43, f32[5632,256]{1,0:T(8,128)} %param.44, bf16[256,2816]{0,1:T(8,128)(2,1)S(1)} %get-tuple-element.200, bf16[256,2816]{0,1:T(8,128)(2,1)S(1)} %collective-permute-done.57, ...), kind=kLoop, calls=%fused_computation.24 | loop fusion | flops 30277632 | bytes 37486592 | tf_op jit(solution)/shard_map/div | solution.py:288
  999.4 5.3 reduce-scatter.8.cloned.1.call-done
  1019.6 6.4 add_divide_fusion.4
  (614 shorter events, 354.7 us)
Async XLA Ops:
  7.2 157.4 %all-gather.4.cloned.1.call-start = ((), (), s32[]{:S(2)}) async-start(), calls=%async_computation.3 | async-start | bytes 10485760 | tf_op jit(solution)/shard_map/all_gather | solution.py:95
  18.8 333.7 %all-gather.6.cloned.1.call-start = ((), (), s32[]{:S(2)}) async-start(), calls=%async_computation.4 | async-start | bytes 28835840 | tf_op jit(solution)/shard_map/all_gather | solution.py:95
  28.1 14.2 %collective-permute-start.2 = (bf16[128,640]{1,0:T(8,128)(2,1)S(1)}, bf16[128,640]{1,0:T(8,128)(2,1)S(1)}, u32[]{:S(2)}, u32[]{:S(2)}) collective-permute-start(bf16[128,640]{1,0:T(8,128)(2,1)S(1)} %get-tuple-element.282), channel_id=1, source_target_pairs={{0,2},{1,3},{2,0},{3,1},{4,6},{5,7},{6,4},{7,5},{8,10},{9,11},{10,... | collective-permute-start | bytes 491528 | tf_op jit(solution)/shard_map/ppermute | solution.py:86
  61.0 398.2 %all-gather.8.cloned.1.call-start = ((), (), s32[]{:S(2)}) async-start(), calls=%async_computation.5 | async-start | bytes 14417920 | tf_op jit(solution)/shard_map/all_gather | solution.py:95
  64.3 31.5 %collective-permute-start.7 = (bf16[512,640]{1,0:T(8,128)(2,1)S(1)}, bf16[512,640]{1,0:T(8,128)(2,1)}, u32[]{:S(2)}, u32[]{:S(2)}) collective-permute-start(bf16[512,640]{1,0:T(8,128)(2,1)S(1)} %bitcast.222), channel_id=1, source_target_pairs={{0,16},{4,20},{8,24},{12,28},{16,0},{20,4},{24,8},{28,12},{1,17},{... | collective-permute-start | bytes 1966088 | tf_op jit(solution)/shard_map/ppermute | solution.py:202
  65.8 33.1 %collective-permute-start.6 = (bf16[512,640]{1,0:T(8,128)(2,1)S(1)}, bf16[512,640]{1,0:T(8,128)(2,1)}, u32[]{:S(2)}, u32[]{:S(2)}) collective-permute-start(bf16[512,640]{1,0:T(8,128)(2,1)S(1)} %bitcast.223), channel_id=1, source_target_pairs={{0,8},{4,12},{8,0},{12,4},{16,24},{20,28},{24,16},{28,20},{1,9},{5... | collective-permute-start | bytes 1966088 | tf_op jit(solution)/shard_map/ppermute | solution.py:202
  70.0 49.1 %collective-permute-start.12 = (bf16[128,2176]{1,0:T(8,128)(2,1)}, bf16[128,2176]{1,0:T(8,128)(2,1)}, u32[]{:S(2)}, u32[]{:S(2)}) collective-permute-start(bf16[128,2176]{1,0:T(8,128)(2,1)} %fusion.74), channel_id=1, source_target_pairs={{0,3},{1,2},{2,1},{3,0},{4,7},{5,6},{6,5},{7,4},{8,11},{9,10},{10,... | collective-permute-start | bytes 1671176 | tf_op jit(solution)/shard_map/ppermute | solution.py:86
  72.4 46.8 %collective-permute-start.11 = (bf16[128,2176]{1,0:T(8,128)(2,1)}, bf16[128,2176]{1,0:T(8,128)(2,1)}, u32[]{:S(2)}, u32[]{:S(2)}) collective-permute-start(bf16[128,2176]{1,0:T(8,128)(2,1)} %fusion.74), channel_id=1, source_target_pairs={{0,2},{1,3},{2,0},{3,1},{4,6},{5,7},{6,4},{7,5},{8,10},{9,11},{10,... | collective-permute-start | bytes 1671176 | tf_op jit(solution)/shard_map/ppermute | solution.py:86
  72.4 48.2 %collective-permute-start.10 = (bf16[128,2176]{1,0:T(8,128)(2,1)}, bf16[128,2176]{1,0:T(8,128)(2,1)}, u32[]{:S(2)}, u32[]{:S(2)}) collective-permute-start(bf16[128,2176]{1,0:T(8,128)(2,1)} %fusion.74), channel_id=1, source_target_pairs={{0,1},{1,0},{2,3},{3,2},{4,5},{5,4},{6,7},{7,6},{8,9},{9,8},{10,11... | collective-permute-start | bytes 1671176 | tf_op jit(solution)/shard_map/ppermute | solution.py:86
  97.5 17.3 %collective-permute-start.9 = (bf16[256,640]{1,0:T(8,128)(2,1)}, bf16[256,640]{1,0:T(8,128)(2,1)}, u32[]{:S(2)}, u32[]{:S(2)}) collective-permute-start(bf16[256,640]{1,0:T(8,128)(2,1)} %slice.304), channel_id=1, source_target_pairs={{0,8},{4,12},{8,0},{12,4},{16,24},{20,28},{24,16},{28,20},{1,9},{5... | collective-permute-start | bytes 983048 | tf_op jit(solution)/shard_map/ppermute | solution.py:202
  100.7 17.2 %collective-permute-start.8 = (bf16[256,640]{1,0:T(8,128)(2,1)}, bf16[256,640]{1,0:T(8,128)(2,1)}, u32[]{:S(2)}, u32[]{:S(2)}) collective-permute-start(bf16[256,640]{1,0:T(8,128)(2,1)} %slice.303), channel_id=1, source_target_pairs={{0,16},{4,20},{8,24},{12,28},{16,0},{20,4},{24,8},{28,12},{1,17},{... | collective-permute-start | bytes 983048 | tf_op jit(solution)/shard_map/ppermute | solution.py:202
  114.8 15.6 %collective-permute-start.18 = (bf16[256,2816]{0,1:T(8,128)(2,1)}, bf16[256,2816]{0,1:T(8,128)(2,1)}, u32[]{:S(2)}, u32[]{:S(2)}) collective-permute-start(bf16[256,2816]{0,1:T(8,128)(2,1)} %dynamic-slice_bitcast_fusion.2), channel_id=1, source_target_pairs={{0,4},{4,0},{8,12},{12,8},{16,20},{20,16},{24,28},{28,24},{1,5},{5... | collective-permute-start | bytes 4325384 | tf_op jit(solution)/shard_map/ppermute | solution.py:80
  132.9 552.8 %reduce-scatter.4.cloned.1.call-start = ((), (), s32[]{:S(2)}) async-start(), calls=%async_computation.6 | async-start | bytes 14417920 | tf_op jit(solution)/shard_map/reduce_scatter | solution.py:99
  157.1 49.2 %collective-permute-start.17 = (bf16[4,8,128,128]{3,2,1,0:T(8,128)(2,1)}, bf16[4,8,128,128]{3,2,1,0:T(8,128)(2,1)}, u32[]{:S(2)}, u32[]{:S(2)}) collective-permute-start(bf16[4,8,128,128]{3,2,1,0:T(8,128)(2,1)} %pad_maximum_fusion.14), channel_id=1, source_target_pairs={{0,2},{1,3},{2,0},{3,1},{4,6},{5,7},{6,4},{7,5},{8,10},{9,11},{10,... | collective-permute-start | bytes 3145736 | tf_op jit(solution)/shard_map/ppermute | solution.py:86
  157.2 71.6 %collective-permute-start.16 = (bf16[4,8,128,128]{3,2,1,0:T(8,128)(2,1)}, bf16[4,8,128,128]{3,2,1,0:T(8,128)(2,1)}, u32[]{:S(2)}, u32[]{:S(2)}) collective-permute-start(bf16[4,8,128,128]{3,2,1,0:T(8,128)(2,1)} %pad_maximum_fusion.14), channel_id=1, source_target_pairs={{0,1},{1,0},{2,3},{3,2},{4,5},{5,4},{6,7},{7,6},{8,9},{9,8},{10,11... | collective-permute-start | bytes 3145736 | tf_op jit(solution)/shard_map/ppermute | solution.py:86
  186.7 53.8 %collective-permute-start.19 = (bf16[4,8,128,128]{3,2,1,0:T(8,128)(2,1)}, bf16[4,8,128,128]{3,2,1,0:T(8,128)(2,1)}, u32[]{:S(2)}, u32[]{:S(2)}) collective-permute-start(bf16[4,8,128,128]{3,2,1,0:T(8,128)(2,1)} %pad_maximum_fusion.14), channel_id=1, source_target_pairs={{0,3},{1,2},{2,1},{3,0},{4,7},{5,6},{6,5},{7,4},{8,11},{9,10},{10,... | collective-permute-start | bytes 3145736 | tf_op jit(solution)/shard_map/ppermute | solution.py:86
  276.9 13.0 %collective-permute-start.23 = (bf16[96,2048]{1,0:T(8,128)(2,1)S(1)}, bf16[96,2048]{1,0:T(8,128)(2,1)S(1)}, u32[]{:S(2)}, u32[]{:S(2)}) collective-permute-start(bf16[96,2048]{1,0:T(8,128)(2,1)S(1)} %get-tuple-element.237), channel_id=1, source_target_pairs={{0,3},{1,2},{2,1},{3,0},{4,7},{5,6},{6,5},{7,4},{8,11},{9,10},{10,... | collective-permute-start | bytes 1179656 | tf_op jit(solution)/shard_map/ppermute | solution.py:86
  278.6 36.7 %collective-permute-start.22 = (bf16[96,2048]{1,0:T(8,128)(2,1)S(1)}, bf16[96,2048]{1,0:T(8,128)(2,1)S(1)}, u32[]{:S(2)}, u32[]{:S(2)}) collective-permute-start(bf16[96,2048]{1,0:T(8,128)(2,1)S(1)} %get-tuple-element.238), channel_id=1, source_target_pairs={{0,2},{1,3},{2,0},{3,1},{4,6},{5,7},{6,4},{7,5},{8,10},{9,11},{10,... | collective-permute-start | bytes 1179656 | tf_op jit(solution)/shard_map/ppermute | solution.py:86
  289.4 26.0 %collective-permute-start.21 = (bf16[96,2048]{1,0:T(8,128)(2,1)S(1)}, bf16[96,2048]{1,0:T(8,128)(2,1)S(1)}, u32[]{:S(2)}, u32[]{:S(2)}) collective-permute-start(bf16[96,2048]{1,0:T(8,128)(2,1)S(1)} %get-tuple-element.239), channel_id=1, source_target_pairs={{0,1},{1,0},{2,3},{3,2},{4,5},{5,4},{6,7},{7,6},{8,9},{9,8},{10,11... | collective-permute-start | bytes 1179656 | tf_op jit(solution)/shard_map/ppermute | solution.py:86
  318.8 17.5 %collective-permute-start.24 = (bf16[96,2048]{1,0:T(8,128)(2,1)S(1)}, bf16[96,2048]{1,0:T(8,128)(2,1)S(1)}, u32[]{:S(2)}, u32[]{:S(2)}) collective-permute-start(bf16[96,2048]{1,0:T(8,128)(2,1)S(1)} %get-tuple-element.235), channel_id=1, source_target_pairs={{0,1},{1,0},{2,3},{3,2},{4,5},{5,4},{6,7},{7,6},{8,9},{9,8},{10,11... | collective-permute-start | bytes 1179656 | tf_op jit(solution)/shard_map/ppermute | solution.py:86
  318.9 29.9 %collective-permute-start.25 = (bf16[96,2048]{1,0:T(8,128)(2,1)S(1)}, bf16[96,2048]{1,0:T(8,128)(2,1)S(1)}, u32[]{:S(2)}, u32[]{:S(2)}) collective-permute-start(bf16[96,2048]{1,0:T(8,128)(2,1)S(1)} %get-tuple-element.234), channel_id=1, source_target_pairs={{0,2},{1,3},{2,0},{3,1},{4,6},{5,7},{6,4},{7,5},{8,10},{9,11},{10,... | collective-permute-start | bytes 1179656 | tf_op jit(solution)/shard_map/ppermute | solution.py:86
  321.2 27.7 %collective-permute-start.26 = (bf16[96,2048]{1,0:T(8,128)(2,1)S(1)}, bf16[96,2048]{1,0:T(8,128)(2,1)S(1)}, u32[]{:S(2)}, u32[]{:S(2)}) collective-permute-start(bf16[96,2048]{1,0:T(8,128)(2,1)S(1)} %get-tuple-element.233), channel_id=1, source_target_pairs={{0,3},{1,2},{2,1},{3,0},{4,7},{5,6},{6,5},{7,4},{8,11},{9,10},{10,... | collective-permute-start | bytes 1179656 | tf_op jit(solution)/shard_map/ppermute | solution.py:86
  480.8 14.0 %collective-permute-start.31 = (bf16[96,2048]{1,0:T(8,128)(2,1)S(1)}, bf16[96,2048]{1,0:T(8,128)(2,1)S(1)}, u32[]{:S(2)}, u32[]{:S(2)}) collective-permute-start(bf16[96,2048]{1,0:T(8,128)(2,1)S(1)} %get-tuple-element.230), channel_id=1, source_target_pairs={{0,3},{1,2},{2,1},{3,0},{4,7},{5,6},{6,5},{7,4},{8,11},{9,10},{10,... | collective-permute-start | bytes 1179656 | tf_op jit(solution)/shard_map/ppermute | solution.py:86
  484.2 33.9 %collective-permute-start.30 = (bf16[96,2048]{1,0:T(8,128)(2,1)S(1)}, bf16[96,2048]{1,0:T(8,128)(2,1)S(1)}, u32[]{:S(2)}, u32[]{:S(2)}) collective-permute-start(bf16[96,2048]{1,0:T(8,128)(2,1)S(1)} %get-tuple-element.231), channel_id=1, source_target_pairs={{0,2},{1,3},{2,0},{3,1},{4,6},{5,7},{6,4},{7,5},{8,10},{9,11},{10,... | collective-permute-start | bytes 1179656 | tf_op jit(solution)/shard_map/ppermute | solution.py:86
  484.2 33.9 %collective-permute-start.29 = (bf16[96,2048]{1,0:T(8,128)(2,1)S(1)}, bf16[96,2048]{1,0:T(8,128)(2,1)S(1)}, u32[]{:S(2)}, u32[]{:S(2)}) collective-permute-start(bf16[96,2048]{1,0:T(8,128)(2,1)S(1)} %get-tuple-element.232), channel_id=1, source_target_pairs={{0,1},{1,0},{2,3},{3,2},{4,5},{5,4},{6,7},{7,6},{8,9},{9,8},{10,11... | collective-permute-start | bytes 1179656 | tf_op jit(solution)/shard_map/ppermute | solution.py:86
  521.8 17.7 %collective-permute-start.32 = (bf16[96,2048]{1,0:T(8,128)(2,1)S(1)}, bf16[96,2048]{1,0:T(8,128)(2,1)S(1)}, u32[]{:S(2)}, u32[]{:S(2)}) collective-permute-start(bf16[96,2048]{1,0:T(8,128)(2,1)S(1)} %get-tuple-element.227), channel_id=1, source_target_pairs={{0,1},{1,0},{2,3},{3,2},{4,5},{5,4},{6,7},{7,6},{8,9},{9,8},{10,11... | collective-permute-start | bytes 1179656 | tf_op jit(solution)/shard_map/ppermute | solution.py:86
  521.9 29.9 %collective-permute-start.33 = (bf16[96,2048]{1,0:T(8,128)(2,1)S(1)}, bf16[96,2048]{1,0:T(8,128)(2,1)S(1)}, u32[]{:S(2)}, u32[]{:S(2)}) collective-permute-start(bf16[96,2048]{1,0:T(8,128)(2,1)S(1)} %get-tuple-element.226), channel_id=1, source_target_pairs={{0,2},{1,3},{2,0},{3,1},{4,6},{5,7},{6,4},{7,5},{8,10},{9,11},{10,... | collective-permute-start | bytes 1179656 | tf_op jit(solution)/shard_map/ppermute | solution.py:86
  524.8 27.0 %collective-permute-start.34 = (bf16[96,2048]{1,0:T(8,128)(2,1)S(1)}, bf16[96,2048]{1,0:T(8,128)(2,1)S(1)}, u32[]{:S(2)}, u32[]{:S(2)}) collective-permute-start(bf16[96,2048]{1,0:T(8,128)(2,1)S(1)} %get-tuple-element.225), channel_id=1, source_target_pairs={{0,3},{1,2},{2,1},{3,0},{4,7},{5,6},{6,5},{7,4},{8,11},{9,10},{10,... | collective-permute-start | bytes 1179656 | tf_op jit(solution)/shard_map/ppermute | solution.py:86
  568.7 324.8 %reduce-scatter.6.cloned.1.call-start = ((), (), s32[]{:S(2)}) async-start(), calls=%async_computation.7 | async-start | bytes 28835840 | tf_op jit(solution)/shard_map/reduce_scatter | solution.py:99
  626.9 33.0 %collective-permute-start.39 = (bf16[96,2048]{1,0:T(8,128)(2,1)}, bf16[96,2048]{1,0:T(8,128)(2,1)}, u32[]{:S(2)}, u32[]{:S(2)}) collective-permute-start(bf16[96,2048]{1,0:T(8,128)(2,1)} %get-tuple-element.222), channel_id=1, source_target_pairs={{0,3},{1,2},{2,1},{3,0},{4,7},{5,6},{6,5},{7,4},{8,11},{9,10},{10,... | collective-permute-start | bytes 1179656 | tf_op jit(solution)/shard_map/ppermute | solution.py:86
  629.1 36.5 %collective-permute-start.38 = (bf16[96,2048]{1,0:T(8,128)(2,1)S(1)}, bf16[96,2048]{1,0:T(8,128)(2,1)}, u32[]{:S(2)}, u32[]{:S(2)}) collective-permute-start(bf16[96,2048]{1,0:T(8,128)(2,1)S(1)} %get-tuple-element.223), channel_id=1, source_target_pairs={{0,2},{1,3},{2,0},{3,1},{4,6},{5,7},{6,4},{7,5},{8,10},{9,11},{10,... | collective-permute-start | bytes 1179656 | tf_op jit(solution)/shard_map/ppermute | solution.py:86
  635.7 29.9 %collective-permute-start.37 = (bf16[96,2048]{1,0:T(8,128)(2,1)S(1)}, bf16[96,2048]{1,0:T(8,128)(2,1)}, u32[]{:S(2)}, u32[]{:S(2)}) collective-permute-start(bf16[96,2048]{1,0:T(8,128)(2,1)S(1)} %get-tuple-element.224), channel_id=1, source_target_pairs={{0,1},{1,0},{2,3},{3,2},{4,5},{5,4},{6,7},{7,6},{8,9},{9,8},{10,11... | collective-permute-start | bytes 1179656 | tf_op jit(solution)/shard_map/ppermute | solution.py:86
  685.8 318.9 %reduce-scatter.8.cloned.1.call-start = ((), (), s32[]{:S(2)}) async-start(), calls=%async_computation.8 | async-start | bytes 13762560 | tf_op jit(solution)/shard_map/reduce_scatter | solution.py:99
  692.0 29.8 %collective-permute-start.41 = (bf16[96,2048]{1,0:T(8,128)(2,1)S(1)}, bf16[96,2048]{1,0:T(8,128)(2,1)S(1)}, u32[]{:S(2)}, u32[]{:S(2)}) collective-permute-start(bf16[96,2048]{1,0:T(8,128)(2,1)S(1)} %get-tuple-element.219), channel_id=1, source_target_pairs={{0,2},{1,3},{2,0},{3,1},{4,6},{5,7},{6,4},{7,5},{8,10},{9,11},{10,... | collective-permute-start | bytes 1179656 | tf_op jit(solution)/shard_map/ppermute | solution.py:86
  694.5 18.0 %collective-permute-start.40 = (bf16[96,2048]{1,0:T(8,128)(2,1)S(1)}, bf16[96,2048]{1,0:T(8,128)(2,1)S(1)}, u32[]{:S(2)}, u32[]{:S(2)}) collective-permute-start(bf16[96,2048]{1,0:T(8,128)(2,1)S(1)} %get-tuple-element.220), channel_id=1, source_target_pairs={{0,1},{1,0},{2,3},{3,2},{4,5},{5,4},{6,7},{7,6},{8,9},{9,8},{10,11... | collective-permute-start | bytes 1179656 | tf_op jit(solution)/shard_map/ppermute | solution.py:86
  696.2 25.6 %collective-permute-start.42 = (bf16[96,2048]{1,0:T(8,128)(2,1)S(1)}, bf16[96,2048]{1,0:T(8,128)(2,1)S(1)}, u32[]{:S(2)}, u32[]{:S(2)}) collective-permute-start(bf16[96,2048]{1,0:T(8,128)(2,1)S(1)} %get-tuple-element.218), channel_id=1, source_target_pairs={{0,3},{1,2},{2,1},{3,0},{4,7},{5,6},{6,5},{7,4},{8,11},{9,10},{10,... | collective-permute-start | bytes 1179656 | tf_op jit(solution)/shard_map/ppermute | solution.py:86
  763.6 53.7 %collective-permute-start.44 = (bf16[4,8,128,128]{2,3,1,0:T(8,128)(2,1)}, bf16[4,8,128,128]{2,3,1,0:T(8,128)(2,1)}, u32[]{:S(2)}, u32[]{:S(2)}) collective-permute-start(bf16[4,8,128,128]{2,3,1,0:T(8,128)(2,1)} %pad_maximum_fusion.15), channel_id=1, source_target_pairs={{0,1},{1,0},{2,3},{3,2},{4,5},{5,4},{6,7},{7,6},{8,9},{9,8},{10,11... | collective-permute-start | bytes 3145736 | tf_op jit(solution)/shard_map/ppermute | solution.py:86
  772.5 71.3 %collective-permute-start.45 = (bf16[4,8,128,128]{2,3,1,0:T(8,128)(2,1)}, bf16[4,8,128,128]{2,3,1,0:T(8,128)(2,1)}, u32[]{:S(2)}, u32[]{:S(2)}) collective-permute-start(bf16[4,8,128,128]{2,3,1,0:T(8,128)(2,1)} %pad_maximum_fusion.16), channel_id=1, source_target_pairs={{0,2},{1,3},{2,0},{3,1},{4,6},{5,7},{6,4},{7,5},{8,10},{9,11},{10,... | collective-permute-start | bytes 3145736 | tf_op jit(solution)/shard_map/ppermute | solution.py:86
  797.2 46.7 %collective-permute-start.46 = (bf16[4,8,128,128]{2,3,1,0:T(8,128)(2,1)S(1)}, bf16[4,8,128,128]{2,3,1,0:T(8,128)(2,1)S(1)}, u32[]{:S(2)}, u32[]{:S(2)}) collective-permute-start(bf16[4,8,128,128]{2,3,1,0:T(8,128)(2,1)S(1)} %pad_maximum_fusion.17), channel_id=1, source_target_pairs={{0,3},{1,2},{2,1},{3,0},{4,7},{5,6},{6,5},{7,4},{8,11},{9,10},{10,... | collective-permute-start | bytes 3145736 | tf_op jit(solution)/shard_map/ppermute | solution.py:86
  900.9 12.7 %collective-permute-start.50 = (bf16[256,5632]{1,0:T(8,128)(2,1)}, bf16[256,5632]{1,0:T(8,128)(2,1)}, u32[]{:S(2)}, u32[]{:S(2)}) collective-permute-start(bf16[256,5632]{1,0:T(8,128)(2,1)} %constant_dynamic-slice_fusion.7), channel_id=1, source_target_pairs={{0,4},{4,0},{8,12},{12,8},{16,20},{20,16},{24,28},{28,24},{1,5},{5... | collective-permute-start | bytes 8650760 | tf_op jit(solution)/shard_map/ppermute | solution.py:80
  907.6 32.5 %collective-permute-start.48 = (bf16[128,2048]{1,0:T(8,128)(2,1)}, bf16[128,2048]{1,0:T(8,128)(2,1)}, u32[]{:S(2)}, u32[]{:S(2)}) collective-permute-start(bf16[128,2048]{1,0:T(8,128)(2,1)} %get-tuple-element.205), channel_id=1, source_target_pairs={{0,1},{1,0},{2,3},{3,2},{4,5},{5,4},{6,7},{7,6},{8,9},{9,8},{10,11... | collective-permute-start | bytes 1572872 | tf_op jit(solution)/shard_map/ppermute | solution.py:86
  909.1 31.1 %collective-permute-start.49 = (bf16[128,2048]{1,0:T(8,128)(2,1)}, bf16[128,2048]{1,0:T(8,128)(2,1)}, u32[]{:S(2)}, u32[]{:S(2)}) collective-permute-start(bf16[128,2048]{1,0:T(8,128)(2,1)} %get-tuple-element.207), channel_id=1, source_target_pairs={{0,2},{1,3},{2,0},{3,1},{4,6},{5,7},{6,4},{7,5},{8,10},{9,11},{10,... | collective-permute-start | bytes 1572872 | tf_op jit(solution)/shard_map/ppermute | solution.py:86
  939.5 15.4 %collective-permute-start.51 = (bf16[128,2048]{1,0:T(8,128)(2,1)S(1)}, bf16[128,2048]{1,0:T(8,128)(2,1)S(1)}, u32[]{:S(2)}, u32[]{:S(2)}) collective-permute-start(bf16[128,2048]{1,0:T(8,128)(2,1)S(1)} %get-tuple-element.70), channel_id=1, source_target_pairs={{0,3},{1,2},{2,1},{3,0},{4,7},{5,6},{6,5},{7,4},{8,11},{9,10},{10,... | collective-permute-start | bytes 1572872 | tf_op jit(solution)/shard_map/ppermute | solution.py:86
  957.3 30.6 %collective-permute-start.57 = (bf16[256,2816]{0,1:T(8,128)(2,1)S(1)}, bf16[256,2816]{0,1:T(8,128)(2,1)S(1)}, u32[]{:S(2)}, u32[]{:S(2)}) collective-permute-start(bf16[256,2816]{0,1:T(8,128)(2,1)S(1)} %get-tuple-element.199), channel_id=1, source_target_pairs={{0,4},{4,0},{8,12},{12,8},{16,20},{20,16},{24,28},{28,24},{1,5},{5... | collective-permute-start | bytes 4325384 | tf_op jit(solution)/shard_map/ppermute | solution.py:80
  970.2 11.8 %collective-permute-start.55 = (f32[1,1]{1,0:T(1,128)}, f32[1,1]{1,0:T(1,128)}, u32[]{:S(2)}, u32[]{:S(2)}) collective-permute-start(f32[1,1]{1,0:T(1,128)} %add.530), channel_id=1, source_target_pairs={{0,1},{1,0},{2,3},{3,2},{4,5},{5,4},{6,7},{7,6},{8,9},{9,8},{10,11... | collective-permute-start | bytes 20 | tf_op jit(solution)/shard_map/ppermute | solution.py:86
  1012.8 17.1 %collective-permute-start.61 = (bf16[2,64,640]{2,1,0:T(8,128)(2,1)}, bf16[2,64,640]{2,1,0:T(8,128)(2,1)}, u32[]{:S(2)}, u32[]{:S(2)}) collective-permute-start(bf16[2,64,640]{2,1,0:T(8,128)(2,1)} %get-tuple-element.259), channel_id=1, source_target_pairs={{0,3},{1,2},{2,1},{3,0},{4,7},{5,6},{6,5},{7,4},{8,11},{9,10},{10,... | collective-permute-start | bytes 491528 | tf_op jit(solution)/shard_map/ppermute | solution.py:86
  1016.1 14.7 %collective-permute-start.60 = (bf16[2,64,640]{2,1,0:T(8,128)(2,1)}, bf16[2,64,640]{2,1,0:T(8,128)(2,1)}, u32[]{:S(2)}, u32[]{:S(2)}) collective-permute-start(bf16[2,64,640]{2,1,0:T(8,128)(2,1)} %get-tuple-element.260), channel_id=1, source_target_pairs={{0,2},{1,3},{2,0},{3,1},{4,6},{5,7},{6,4},{7,5},{8,10},{9,11},{10,... | collective-permute-start | bytes 491528 | tf_op jit(solution)/shard_map/ppermute | solution.py:86
  1016.1 14.7 %collective-permute-start.59 = (bf16[2,64,640]{2,1,0:T(8,128)(2,1)S(1)}, bf16[2,64,640]{2,1,0:T(8,128)(2,1)}, u32[]{:S(2)}, u32[]{:S(2)}) collective-permute-start(bf16[2,64,640]{2,1,0:T(8,128)(2,1)S(1)} %get-tuple-element.261), channel_id=1, source_target_pairs={{0,1},{1,0},{2,3},{3,2},{4,5},{5,4},{6,7},{7,6},{8,9},{9,8},{10,11... | collective-permute-start | bytes 491528 | tf_op jit(solution)/shard_map/ppermute | solution.py:86
  (140 other events, 1905.6 us)
Sparse Core Ops, SparseCore 0:
  18.9 111.2 all-gather.3
  132.6 210.4 all-gather.5
  345.5 113.6 all-gather.7
  568.8 116.8 reduce-scatter.3
  688.7 204.7 reduce-scatter.5
  896.8 107.8 reduce-scatter.7

commit v5 on v4

--- a/solution.py
+++ b/solution.py
@@ -180,8 +180,10 @@
     return jnp.concatenate([got, core_swap(got)])
 
 
-def send_rows(blocks, places=None):
+def send_rows(blocks, places=None, by_block=False):
     blocks = [over_expert(block, bits) for bits, block in enumerate(blocks)]
+    if by_block:
+        return jnp.concatenate(blocks + [core_swap(block) for block in blocks])
     return place_rows(blocks, range(len(blocks)) if places is None else places)
 
 
@@ -414,8 +416,8 @@
             (core_swap(up_theirs.astype(BF16)), row_got, width_ff),
         ],
     )
-    shared_whole = gather_split(chip, arrived)
-    shared_whole, token_blocks, _ = together(shared_whole, token_blocks, gate_up_rows)
+    shared_whole = gather_split(chip, after(arrived, gate_up_rows, weight_attn))
+    token_blocks, shared_whole = together(token_blocks, shared_whole)
     everyone = place_rows(token_blocks, places)
     kv_weight = shared_whole[:, : 2 * sixth]
     small_whole = shared_whole[:, 2 * sixth :]
@@ -510,13 +512,13 @@
     local_error = jnp.sum(valid_f[:, None] * deviation * deviation)
     grad_out = 2.0 * valid_f[:, None] * deviation / total_count
 
-    def send_grads(pick, gates, hit, grad, where=None):
+    def send_grads(pick, gates, hit, grad, where=None, by_block=False):
         gate_of = jnp.sum(gates[:, :, None] * hit, axis=1)
         rows = (gate_of.T[:, :, None] * grad[None]).astype(BF16)
         sent = jnp.einsum("kct,ktd->kcd", pick, rows, preferred_element_type=F32).astype(BF16)
-        return send_rows(list(sent), where)
-
-    rows_grad = send_grads(mlp_pick, gates_mlp, mlp_hit, grad_out)
+        return send_rows(list(sent), where, by_block)
+
+    rows_grad = send_grads(mlp_pick, gates_mlp, mlp_hit, grad_out, by_block=True)
     grad_down = matmul_rows(rows_grad, active).astype(BF16)
     grad_active = matmul(rows_grad, weight_down)
     sigmoid_gate = jax.nn.sigmoid(gate_val)
@@ -571,7 +573,8 @@
         )
 
     grad_kv_parts = [heads_of(step) for step in range(EXPERTS)]
-    grad_kv_parts[-1] = after(grad_kv_parts[-1], grad_query)
+    total_error = all_sum(after(local_error, grad_query).reshape(1, 1))[0, 0]
+    grad_kv_parts[-1] = after(grad_kv_parts[-1], grad_query, total_error)
     grad_kv = sum(
         over_expert(part, step * halves).astype(F32) for step, part in enumerate(grad_kv_parts)
     ).astype(BF16)
@@ -627,13 +630,12 @@
     grad_inputs_norm, _ = norm_back(inputs_f, inverse_one, gains_f[0], grad_normed_one)
     input_grad = grad_hidden + grad_inputs_norm
 
-    down_sum, local_error, _ = together(down_sum, local_error, normed_one_rows)
+    down_sum, _ = together(down_sum, normed_one_rows)
     down_mine, down_other = exchange_rows(core, down_sum)
     reduced_down = turned(in_core_order(core, down_mine, down_other, 1))
     update_down = adam_step(moment_down, square_down, reduced_down)
-    total_error = all_sum(local_error.reshape(1, 1))[0, 0]
-
-    last_mine, last_other = exchange_rows(core, after(last_sum, total_error, *update_down))
+
+    last_mine, last_other = exchange_rows(core, after(last_sum, *update_down))
     attn_mine, attn_other = last_mine[:, : 2 * width_attn], last_other[:, : 2 * width_attn]
     shared_mine, shared_theirs = [
         rows[:, 2 * width_attn :].reshape(partners, local_rows, -1)

time: 1060 us -> 1040 us (0.981)
    reduce_scatter x3, waiting for transfers between devices: 50.1 us -> 76.3 us  [scatter_chips(): lax.psum_scatter(partial, 'dp', scatter_dimension=0, tiled=True, axis_ind...]
    all_gather x3, waiting for transfers between devices: 72.1 us -> 53.3 us  [gather_chips(): lax.all_gather(block, 'dp', axis=0, tiled=True, axis_index_groups=chip_gr...]
    ppermute x4, waiting for transfers between devices: 29.6 us -> 16.6 us  [over_chips(): return lax.ppermute(value, 'dp', swap_perm(lax.axis_size('dp'), 2 * bits))]
    unnamed x242 -> x249, local copies, waits for them, and re-layouts: 25.1 us -> 22.4 us
  transfers between devices with their start and end apart: 68 -> 71, of which waited for: 40 -> 41; matrix products, arithmetic and copies ran while one was open for 41% -> 42% of each run, Pallas kernels for 0% -> 0%
where the time goes in v5:
time: 1040 us; the launch traced here: 1030 us
  waiting for transfers between devices  412 us (40%)
  matrix products  220 us (21%)
  local copies, waits for them, and re-layouts  176 us (17%)
  other arithmetic  108 us (10%)
  starting transfers between devices  94.2 us (9%)
  between operations  22.3 us (2%)
    ppermute x38, waiting for transfers between devices, over_expert(): lax.ppermute(value, 'expert', swap_perm(lax.axis_size('expert'), bits))  246 us
    ppermute x38, starting transfers between devices, over_expert(): lax.ppermute(value, 'expert', swap_perm(lax.axis_size('expert'), bits))  80.5 us
    reduce_scatter x3, waiting for transfers between devices, scatter_chips(): lax.psum_scatter(partial, 'dp', scatter_dimension=0, tiled=True, axis_ind...  76.3 us
    dot_general x13, matrix products, matmul(): return jnp.dot(left_side, right_side, preferred_element_type=F32)  75.6 us
    dot_general x5, matrix products, matmul_back(): lax.dot_general(left_side, right_side, (((1,), (1,)), ((), ())), preferre...  58.8 us
    dot_general x5, matrix products, matmul_rows(): lax.dot_general(left_side, right_side, (((0,), (0,)), ((), ())), preferre...  57.6 us
    all_gather x3, waiting for transfers between devices, gather_chips(): lax.all_gather(block, 'dp', axis=0, tiled=True, axis_index_groups=chip_gr...  53.3 us
    div x7, other arithmetic, adam_step(): direction = moment_hat / (jnp.sqrt(square_hat) + ADAM_EPS)  47.7 us
  transfers between devices with their start and end apart: 71, of which 41 were waited for; matrix products, arithmetic and copies ran while one was open for 42% of the time, Pallas kernels for 0%

profile of v5, /device:TPU:0, one launch (start us, length us, event | category | flops | bytes accessed | tf_op | source)
XLA Modules:
  0.0 1031.5 jit_solution(13827801539017359046)
XLA Ops:
  23.0 5.0 collective-permute-start.3
  37.2 5.1 collective-permute-done.2
  42.5 5.0 fusion.145
  64.3 44.8 %all-gather.4.cloned.1.call-done = bf16[2048,2048]{0,1:T(8,128)(2,1)} async-done(((bf16[512,2048]{0,1:T(8,128)(2,1)}), bf16[2048,2048]{0,1:T(8,128)(2,1)}) %all-gather.4.cloned.1.call-update) | async-done | bytes 8388624 | tf_op jit(solution)/shard_map/all_gather | solution.py:95
  119.3 6.4 collective-permute-done.12
  136.5 8.1 collective-permute-done.14
  149.1 15.5 %collective-permute-done.5 = bf16[128,2176]{1,0:T(8,128)(2,1)} collective-permute-done((bf16[128,2176]{1,0:T(8,128)(2,1)}, bf16[128,2176]{1,0:T(8,128)(2,1)}, u32[]{:S(2)}, u32[]{:S(2)}) %collective-permute-start.5) | collective-permute-done | bytes 557088 | tf_op jit(solution)/shard_map/ppermute | solution.py:86
  204.3 12.5 %fusion.20 = f32[1024,1024]{0,1:T(8,128)} fusion(bf16[1024,2048]{1,0:T(8,128)(2,1)} %copy-done.17, bf16[2048,2048]{0,1:T(8,128)(2,1)} %all-gather.4.cloned.1.call-done), kind=kOutput, calls=%fused_computation.54 | convolution fusion | flops 4294967296 | bytes 12582912 | tf_op jit(solution)/shard_map/dot_general | solution.py:29
  216.7 5.5 copy.346
  222.2 5.1 fusion.148
  233.6 15.7 %collective-permute-done.17 = bf16[4,8,128,128]{3,2,1,0:T(8,128)(2,1)} collective-permute-done((bf16[4,8,128,128]{3,2,1,0:T(8,128)(2,1)}, bf16[4,8,128,128]{3,2,1,0:T(8,128)(2,1)}, u32[]{:S(2)}, u32[]{:S(2)}) %collective-permute-start.17) | collective-permute-done | bytes 1048608 | tf_op jit(solution)/shard_map/ppermute | solution.py:86
  252.9 18.8 %collective-permute-done.16 = bf16[4,8,128,128]{3,2,1,0:T(8,128)(2,1)} collective-permute-done((bf16[4,8,128,128]{3,2,1,0:T(8,128)(2,1)}, bf16[4,8,128,128]{3,2,1,0:T(8,128)(2,1)}, u32[]{:S(2)}, u32[]{:S(2)}) %collective-permute-start.16) | collective-permute-done | bytes 1048608 | tf_op jit(solution)/shard_map/ppermute | solution.py:86
  291.6 5.4 fusion.161
  297.0 4.5 convolution_convert_fusion.13
  307.6 5.8 fusion.17
  323.9 16.4 %collective-permute-start.22 = (bf16[96,2048]{1,0:T(8,128)(2,1)S(1)}, bf16[96,2048]{1,0:T(8,128)(2,1)S(1)}, u32[]{:S(2)}, u32[]{:S(2)}) collective-permute-start(bf16[96,2048]{1,0:T(8,128)(2,1)S(1)} %get-tuple-element.239), channel_id=1, source_target_pairs={{0,2},{1,3},{2,0},{3,1},{4,6},{5,7},{6,4},{7,5},{8,10},{9,11},{10,... | collective-permute-start | bytes 1179656 | tf_op jit(solution)/shard_map/ppermute | solution.py:86
  340.4 25.9 %collective-permute-done.22 = bf16[96,2048]{1,0:T(8,128)(2,1)S(1)} collective-permute-done((bf16[96,2048]{1,0:T(8,128)(2,1)S(1)}, bf16[96,2048]{1,0:T(8,128)(2,1)S(1)}, u32[]{:S(2)}, u32[]{:S(2)}) %collective-permute-start.22) | collective-permute-done | bytes 393248 | tf_op jit(solution)/shard_map/ppermute | solution.py:86
  374.2 13.1 %collective-permute-done.24 = bf16[96,2048]{1,0:T(8,128)(2,1)S(1)} collective-permute-done((bf16[96,2048]{1,0:T(8,128)(2,1)S(1)}, bf16[96,2048]{1,0:T(8,128)(2,1)S(1)}, u32[]{:S(2)}, u32[]{:S(2)}) %collective-permute-start.24) | collective-permute-done | bytes 393248 | tf_op jit(solution)/shard_map/ppermute | solution.py:86
  387.3 12.4 %collective-permute-done.25 = bf16[96,2048]{1,0:T(8,128)(2,1)S(1)} collective-permute-done((bf16[96,2048]{1,0:T(8,128)(2,1)S(1)}, bf16[96,2048]{1,0:T(8,128)(2,1)S(1)}, u32[]{:S(2)}, u32[]{:S(2)}) %collective-permute-start.25) | collective-permute-done | bytes 393248 | tf_op jit(solution)/shard_map/ppermute | solution.py:86
  403.4 23.3 %fusion.35 = f32[768,5632]{1,0:T(8,128)S(1)} fusion(bf16[2048,5632]{1,0:T(8,128)(2,1)} %all-gather.6.cloned.1.call-done, bf16[384,2048]{1,0:T(8,128)(2,1)} %collective-permute-done.27, bf16[384,2048]{1,0:T(8,128)(2,1)S(1)} %constant_dynamic-update-slice_fusion.4), kind=kOutput, calls=%fused_computation.102 | convolution fusion | flops 17723031552 | bytes 43515904 | tf_op jit(solution)/shard_map/dot_general | solution.py:29
  426.7 5.9 copy-done.1
  436.7 8.5 all-gather.8.cloned.1.call-done
  445.2 13.6 %convolution_convert_fusion.4 = bf16[768,2048]{1,0:T(8,128)(2,1)S(1)} fusion(bf16[768,2816]{1,0:T(8,128)(2,1)} %multiply_convert_fusion.2, bf16[2048,2816]{0,1:T(8,128)(2,1)} %all-gather.8.cloned.1.call-done), kind=kOutput, calls=%fused_computation.56 | convolution fusion | flops 8859942912 | bytes 19005440 | tf_op jit(solution)/shard_map/dot_general | solution.py:33
  471.4 9.5 collective-permute-done.31
  480.9 23.4 %collective-permute-done.30 = bf16[96,2048]{1,0:T(8,128)(2,1)S(1)} collective-permute-done((bf16[96,2048]{1,0:T(8,128)(2,1)S(1)}, bf16[96,2048]{1,0:T(8,128)(2,1)S(1)}, u32[]{:S(2)}, u32[]{:S(2)}) %collective-permute-start.30) | collective-permute-done | bytes 393248 | tf_op jit(solution)/shard_map/ppermute | solution.py:86
  512.1 9.4 collective-permute-done.34
  521.6 21.9 %collective-permute-done.33 = bf16[96,2048]{1,0:T(8,128)(2,1)S(1)} collective-permute-done((bf16[96,2048]{1,0:T(8,128)(2,1)S(1)}, bf16[96,2048]{1,0:T(8,128)(2,1)S(1)}, u32[]{:S(2)}, u32[]{:S(2)}) %collective-permute-start.33) | collective-permute-done | bytes 393248 | tf_op jit(solution)/shard_map/ppermute | solution.py:86
  547.6 12.1 %convolution_convert_fusion.1 = bf16[2048,2816]{0,1:T(8,128)(2,1)} fusion(bf16[768,2048]{1,0:T(8,128)(2,1)S(1)} %constant_dynamic-update-slice_fusion.32, bf16[768,2816]{1,0:T(8,128)(2,1)S(1)} %bitcast.220), kind=kOutput, calls=%fused_computation.9 | convolution fusion | flops 8864137216 | bytes 19005440 | tf_op jit(solution)/shard_map/dot_general | solution.py:39
  559.7 22.8 %multiply_convert_fusion.1 = (bf16[768,2816]{1,0:T(8,128)(2,1)}, bf16[768,2816]{1,0:T(8,128)(2,1)}) fusion(f32[768,5632]{1,0:T(8,128)} %copy-done.1, bf16[768,2048]{1,0:T(8,128)(2,1)} %copy-done.61, bf16[2048,2816]{0,1:T(8,128)(2,1)} %all-gather.8.cloned.1.call-done), kind=kOutput, calls=%fused_computation.12 | convolution fusion | flops 8886484992 | bytes 40632320 | tf_op jit(solution)/shard_map/dot_general | solution.py:29
  582.5 8.0 pad_maximum_fusion
  590.5 24.4 %fusion.164 = f32[768,2048]{1,0:T(8,128)S(1)} fusion(bf16[768,5632]{1,0:T(8,128)(2,1)} %pad_maximum_fusion, bf16[2048,5632]{1,0:T(8,128)(2,1)} %all-gather.6.cloned.1.call-done), kind=kOutput, calls=%fused_computation.437 | convolution fusion | flops 17716740096 | bytes 38010880 | tf_op jit(solution)/shard_map/dot_general | solution.py:33
  624.6 24.4 %convolution_convert_fusion = bf16[2048,5632]{1,0:T(8,128)(2,1)} fusion(bf16[384,2048]{1,0:T(8,128)(2,1)} %collective-permute-done.27, bf16[384,2048]{1,0:T(8,128)(2,1)} %copy-done.42, bf16[768,2816]{1,0:T(8,128)(2,1)} %get-tuple-element.189, bf16[768,2816]{1,0:T(8,128)(2,1)S(1)} %bitcast.222), kind=kOutput, calls=%fused_computation.1 | convolution fusion | flops 17751867392 | bytes 34865152 | tf_op jit(solution)/shard_map/dot_general | solution.py:39
  649.0 5.1 collective-permute-done.41
  654.1 16.0 %reduce-scatter.4.cloned.1.call-done = bf16[512,2816]{0,1:T(8,128)(2,1)} async-done(((bf16[2048,2816]{0,1:T(8,128)(2,1)}), bf16[512,2816]{0,1:T(8,128)(2,1)}) %reduce-scatter.4.cloned.1.call-update) | async-done | bytes 2883600 | tf_op jit(solution)/shard_map/reduce_scatter | solution.py:99
  681.4 15.7 %collective-permute-done.43 = bf16[96,2048]{1,0:T(8,128)(2,1)S(1)} collective-permute-done((bf16[96,2048]{1,0:T(8,128)(2,1)S(1)}, bf16[96,2048]{1,0:T(8,128)(2,1)S(1)}, u32[]{:S(2)}, u32[]{:S(2)}) %collective-permute-start.43) | collective-permute-done | bytes 393248 | tf_op jit(solution)/shard_map/ppermute | solution.py:86
  697.2 9.2 collective-permute-done.44
  735.4 8.3 collective-permute-start.52
  754.3 7.8 convolution_convert_fusion.2
  762.2 7.8 dynamic_update_slice.168
  769.9 9.6 constant_dynamic-update-slice_fusion
  806.8 18.0 %collective-permute-done.54 = bf16[4,8,128,128]{2,3,1,0:T(8,128)(2,1)S(1)} collective-permute-done((bf16[4,8,128,128]{2,3,1,0:T(8,128)(2,1)S(1)}, bf16[4,8,128,128]{2,3,1,0:T(8,128)(2,1)S(1)}, u32[]{:S(2)}, u32[]{:S(2)}) %collective-permute-start.54) | collective-permute-done | bytes 1048608 | tf_op jit(solution)/shard_map/ppermute | solution.py:86
  834.6 10.7 %fusion.6 = (f32[2048]{0:T(1024)S(1)}, f32[1024,2048]{1,0:T(8,128)}) fusion(bf16[1024,2048]{1,0:T(8,128)(2,1)S(1)} %copy-done.3, f32[1024]{0:T(1024)S(1)} %copy-done.68, f32[1024,2048]{1,0:T(8,128)S(1)} %fusion.36, bf16[1024,1024]{0,1:T(8,128)(2,1)S(1)} %bitcast.231, bf16[2048,2048]{0,1:T(8,128)(2,1)} %all-gather.4.cloned.1.call-done), kind=kOutput, calls=%fused_computation.20 | convolution fusion | flops 4305451008 | bytes 27275264 | tf_op jit(solution)/shard_map/dot_general | solution.py:33
  849.9 28.0 %reduce-scatter.6.cloned.1.call-done = bf16[512,5632]{1,0:T(8,128)(2,1)} async-done(((bf16[2048,5632]{1,0:T(8,128)(2,1)}), bf16[512,5632]{1,0:T(8,128)(2,1)}) %reduce-scatter.6.cloned.1.call-update) | async-done | bytes 5767184 | tf_op jit(solution)/shard_map/reduce_scatter | solution.py:99
  902.6 21.2 %add_divide_fusion = (f32[2,256,5632]{2,1,0:T(8,128)}, f32[2,256,5632]{2,1,0:T(8,128)}, f32[2,256,5632]{2,1,0:T(8,128)}, f32[2,256,5632]{2,1,0:T(8,128)}) fusion(f32[2,256,5632]{2,1,0:T(8,128)S(1)} %bitcast.211, f32[2,256,5632]{2,1,0:T(8,128)} %param.41, bf16[1,256,5632]{2,1,0:T(8,128)(2,1)S(1)} %get-tuple-element.319, ...), kind=kLoop, calls=%fused_computation.7 | loop fusion | flops 37486592 | bytes 74973184 | tf_op jit(solution)/shard_map/div | solution.py:290
  924.5 14.7 %collective-permute-done.59 = bf16[128,2048]{1,0:T(8,128)(2,1)S(1)} collective-permute-done((bf16[128,2048]{1,0:T(8,128)(2,1)S(1)}, bf16[128,2048]{1,0:T(8,128)(2,1)S(1)}, u32[]{:S(2)}, u32[]{:S(2)}) %collective-permute-start.59) | collective-permute-done | bytes 524320 | tf_op jit(solution)/shard_map/ppermute | solution.py:86
  945.0 11.7 %add_divide_fusion.2 = (f32[5632,256]{1,0:T(8,128)}, f32[5632,256]{1,0:T(8,128)}, f32[5632,256]{1,0:T(8,128)}, f32[5632,256]{1,0:T(8,128)}) fusion(f32[5632,256]{1,0:T(8,128)} %param.43, f32[5632,256]{1,0:T(8,128)} %param.44, bf16[256,2816]{0,1:T(8,128)(2,1)S(1)} %get-tuple-element.201, bf16[256,2816]{0,1:T(8,128)(2,1)S(1)} %collective-permute-done.60, ...), kind=kLoop, calls=%fused_computation.24 | loop fusion | flops 30277632 | bytes 37486592 | tf_op jit(solution)/shard_map/div | solution.py:290
  956.7 32.4 %reduce-scatter.8.cloned.1.call-done = bf16[512,2688]{0,1:T(8,128)(2,1)} async-done(((bf16[2048,2688]{0,1:T(8,128)(2,1)}), bf16[512,2688]{0,1:T(8,128)(2,1)}) %reduce-scatter.8.cloned.1.call-update) | async-done | bytes 2752528 | tf_op jit(solution)/shard_map/reduce_scatter | solution.py:99
  1003.8 6.4 add_divide_fusion.4
  (624 shorter events, 348.6 us)
Async XLA Ops:
  7.2 101.9 %all-gather.4.cloned.1.call-start = ((), (), s32[]{:S(2)}) async-start(), calls=%async_computation.3 | async-start | bytes 10485760 | tf_op jit(solution)/shard_map/all_gather | solution.py:95
  18.8 384.6 %all-gather.6.cloned.1.call-start = ((), (), s32[]{:S(2)}) async-start(), calls=%async_computation.4 | async-start | bytes 28835840 | tf_op jit(solution)/shard_map/all_gather | solution.py:95
  28.1 14.2 %collective-permute-start.2 = (bf16[128,640]{1,0:T(8,128)(2,1)S(1)}, bf16[128,640]{1,0:T(8,128)(2,1)S(1)}, u32[]{:S(2)}, u32[]{:S(2)}) collective-permute-start(bf16[128,640]{1,0:T(8,128)(2,1)S(1)} %get-tuple-element.283), channel_id=1, source_target_pairs={{0,2},{1,3},{2,0},{3,1},{4,6},{5,7},{6,4},{7,5},{8,10},{9,11},{10,... | collective-permute-start | bytes 491528 | tf_op jit(solution)/shard_map/ppermute | solution.py:86
  61.0 384.2 %all-gather.8.cloned.1.call-start = ((), (), s32[]{:S(2)}) async-start(), calls=%async_computation.5 | async-start | bytes 14417920 | tf_op jit(solution)/shard_map/all_gather | solution.py:95
  109.1 16.6 %collective-permute-start.12 = (bf16[512,640]{1,0:T(8,128)(2,1)S(1)}, bf16[512,640]{1,0:T(8,128)(2,1)}, u32[]{:S(2)}, u32[]{:S(2)}) collective-permute-start(bf16[512,640]{1,0:T(8,128)(2,1)S(1)} %bitcast.226), channel_id=1, source_target_pairs={{0,16},{4,20},{8,24},{12,28},{16,0},{20,4},{24,8},{28,12},{1,17},{... | collective-permute-start | bytes 1966088 | tf_op jit(solution)/shard_map/ppermute | solution.py:204
  110.6 18.3 %collective-permute-start.11 = (bf16[512,640]{1,0:T(8,128)(2,1)S(1)}, bf16[512,640]{1,0:T(8,128)(2,1)}, u32[]{:S(2)}, u32[]{:S(2)}) collective-permute-start(bf16[512,640]{1,0:T(8,128)(2,1)S(1)} %bitcast.227), channel_id=1, source_target_pairs={{0,8},{4,12},{8,0},{12,4},{16,24},{20,28},{24,16},{28,20},{1,9},{5... | collective-permute-start | bytes 1966088 | tf_op jit(solution)/shard_map/ppermute | solution.py:204
  113.8 35.3 %collective-permute-start.6 = (bf16[128,2176]{1,0:T(8,128)(2,1)}, bf16[128,2176]{1,0:T(8,128)(2,1)}, u32[]{:S(2)}, u32[]{:S(2)}) collective-permute-start(bf16[128,2176]{1,0:T(8,128)(2,1)} %fusion.73), channel_id=1, source_target_pairs={{0,3},{1,2},{2,1},{3,0},{4,7},{5,6},{6,5},{7,4},{8,11},{9,10},{10,... | collective-permute-start | bytes 1671176 | tf_op jit(solution)/shard_map/ppermute | solution.py:86
  117.1 47.5 %collective-permute-start.5 = (bf16[128,2176]{1,0:T(8,128)(2,1)}, bf16[128,2176]{1,0:T(8,128)(2,1)}, u32[]{:S(2)}, u32[]{:S(2)}) collective-permute-start(bf16[128,2176]{1,0:T(8,128)(2,1)} %fusion.73), channel_id=1, source_target_pairs={{0,2},{1,3},{2,0},{3,1},{4,6},{5,7},{6,4},{7,5},{8,10},{9,11},{10,... | collective-permute-start | bytes 1671176 | tf_op jit(solution)/shard_map/ppermute | solution.py:86
  117.2 47.5 %collective-permute-start.4 = (bf16[128,2176]{1,0:T(8,128)(2,1)}, bf16[128,2176]{1,0:T(8,128)(2,1)}, u32[]{:S(2)}, u32[]{:S(2)}) collective-permute-start(bf16[128,2176]{1,0:T(8,128)(2,1)} %fusion.73), channel_id=1, source_target_pairs={{0,1},{1,0},{2,3},{3,2},{4,5},{5,4},{6,7},{7,6},{8,9},{9,8},{10,11... | collective-permute-start | bytes 1671176 | tf_op jit(solution)/shard_map/ppermute | solution.py:86
  127.4 17.2 %collective-permute-start.14 = (bf16[256,640]{1,0:T(8,128)(2,1)}, bf16[256,640]{1,0:T(8,128)(2,1)}, u32[]{:S(2)}, u32[]{:S(2)}) collective-permute-start(bf16[256,640]{1,0:T(8,128)(2,1)} %slice.304), channel_id=1, source_target_pairs={{0,8},{4,12},{8,0},{12,4},{16,24},{20,28},{24,16},{28,20},{1,9},{5... | collective-permute-start | bytes 983048 | tf_op jit(solution)/shard_map/ppermute | solution.py:204
  130.7 17.1 %collective-permute-start.13 = (bf16[256,640]{1,0:T(8,128)(2,1)}, bf16[256,640]{1,0:T(8,128)(2,1)}, u32[]{:S(2)}, u32[]{:S(2)}) collective-permute-start(bf16[256,640]{1,0:T(8,128)(2,1)} %slice.303), channel_id=1, source_target_pairs={{0,16},{4,20},{8,24},{12,28},{16,0},{20,4},{24,8},{28,12},{1,17},{... | collective-permute-start | bytes 983048 | tf_op jit(solution)/shard_map/ppermute | solution.py:204
  144.6 29.9 %collective-permute-start.18 = (bf16[256,2816]{0,1:T(8,128)(2,1)}, bf16[256,2816]{0,1:T(8,128)(2,1)}, u32[]{:S(2)}, u32[]{:S(2)}) collective-permute-start(bf16[256,2816]{0,1:T(8,128)(2,1)} %dynamic-slice_bitcast_fusion.2), channel_id=1, source_target_pairs={{0,4},{4,0},{8,12},{12,8},{16,20},{20,16},{24,28},{28,24},{1,5},{5... | collective-permute-start | bytes 4325384 | tf_op jit(solution)/shard_map/ppermute | solution.py:80
  177.0 493.0 %reduce-scatter.4.cloned.1.call-start = ((), (), s32[]{:S(2)}) async-start(), calls=%async_computation.6 | async-start | bytes 14417920 | tf_op jit(solution)/shard_map/reduce_scatter | solution.py:99
  199.9 49.4 %collective-permute-start.17 = (bf16[4,8,128,128]{3,2,1,0:T(8,128)(2,1)}, bf16[4,8,128,128]{3,2,1,0:T(8,128)(2,1)}, u32[]{:S(2)}, u32[]{:S(2)}) collective-permute-start(bf16[4,8,128,128]{3,2,1,0:T(8,128)(2,1)} %pad_maximum_fusion.11), channel_id=1, source_target_pairs={{0,2},{1,3},{2,0},{3,1},{4,6},{5,7},{6,4},{7,5},{8,10},{9,11},{10,... | collective-permute-start | bytes 3145736 | tf_op jit(solution)/shard_map/ppermute | solution.py:86
  199.9 71.7 %collective-permute-start.16 = (bf16[4,8,128,128]{3,2,1,0:T(8,128)(2,1)}, bf16[4,8,128,128]{3,2,1,0:T(8,128)(2,1)}, u32[]{:S(2)}, u32[]{:S(2)}) collective-permute-start(bf16[4,8,128,128]{3,2,1,0:T(8,128)(2,1)} %pad_maximum_fusion.11), channel_id=1, source_target_pairs={{0,1},{1,0},{2,3},{3,2},{4,5},{5,4},{6,7},{7,6},{8,9},{9,8},{10,11... | collective-permute-start | bytes 3145736 | tf_op jit(solution)/shard_map/ppermute | solution.py:86
  228.6 49.4 %collective-permute-start.19 = (bf16[4,8,128,128]{3,2,1,0:T(8,128)(2,1)}, bf16[4,8,128,128]{3,2,1,0:T(8,128)(2,1)}, u32[]{:S(2)}, u32[]{:S(2)}) collective-permute-start(bf16[4,8,128,128]{3,2,1,0:T(8,128)(2,1)} %pad_maximum_fusion.11), channel_id=1, source_target_pairs={{0,3},{1,2},{2,1},{3,0},{4,7},{5,6},{6,5},{7,4},{8,11},{9,10},{10,... | collective-permute-start | bytes 3145736 | tf_op jit(solution)/shard_map/ppermute | solution.py:86
  322.3 18.0 %collective-permute-start.23 = (bf16[96,2048]{1,0:T(8,128)(2,1)S(1)}, bf16[96,2048]{1,0:T(8,128)(2,1)S(1)}, u32[]{:S(2)}, u32[]{:S(2)}) collective-permute-start(bf16[96,2048]{1,0:T(8,128)(2,1)S(1)} %get-tuple-element.238), channel_id=1, source_target_pairs={{0,3},{1,2},{2,1},{3,0},{4,7},{5,6},{6,5},{7,4},{8,11},{9,10},{10,... | collective-permute-start | bytes 1179656 | tf_op jit(solution)/shard_map/ppermute | solution.py:86
  323.9 42.3 %collective-permute-start.22 = (bf16[96,2048]{1,0:T(8,128)(2,1)S(1)}, bf16[96,2048]{1,0:T(8,128)(2,1)S(1)}, u32[]{:S(2)}, u32[]{:S(2)}) collective-permute-start(bf16[96,2048]{1,0:T(8,128)(2,1)S(1)} %get-tuple-element.239), channel_id=1, source_target_pairs={{0,2},{1,3},{2,0},{3,1},{4,6},{5,7},{6,4},{7,5},{8,10},{9,11},{10,... | collective-permute-start | bytes 1179656 | tf_op jit(solution)/shard_map/ppermute | solution.py:86
  340.3 26.0 %collective-permute-start.21 = (bf16[96,2048]{1,0:T(8,128)(2,1)S(1)}, bf16[96,2048]{1,0:T(8,128)(2,1)S(1)}, u32[]{:S(2)}, u32[]{:S(2)}) collective-permute-start(bf16[96,2048]{1,0:T(8,128)(2,1)S(1)} %get-tuple-element.240), channel_id=1, source_target_pairs={{0,1},{1,0},{2,3},{3,2},{4,5},{5,4},{6,7},{7,6},{8,9},{9,8},{10,11... | collective-permute-start | bytes 1179656 | tf_op jit(solution)/shard_map/ppermute | solution.py:86
  369.7 17.5 %collective-permute-start.24 = (bf16[96,2048]{1,0:T(8,128)(2,1)S(1)}, bf16[96,2048]{1,0:T(8,128)(2,1)S(1)}, u32[]{:S(2)}, u32[]{:S(2)}) collective-permute-start(bf16[96,2048]{1,0:T(8,128)(2,1)S(1)} %get-tuple-element.236), channel_id=1, source_target_pairs={{0,1},{1,0},{2,3},{3,2},{4,5},{5,4},{6,7},{7,6},{8,9},{9,8},{10,11... | collective-permute-start | bytes 1179656 | tf_op jit(solution)/shard_map/ppermute | solution.py:86
  369.8 29.9 %collective-permute-start.25 = (bf16[96,2048]{1,0:T(8,128)(2,1)S(1)}, bf16[96,2048]{1,0:T(8,128)(2,1)S(1)}, u32[]{:S(2)}, u32[]{:S(2)}) collective-permute-start(bf16[96,2048]{1,0:T(8,128)(2,1)S(1)} %get-tuple-element.235), channel_id=1, source_target_pairs={{0,2},{1,3},{2,0},{3,1},{4,6},{5,7},{6,4},{7,5},{8,10},{9,11},{10,... | collective-permute-start | bytes 1179656 | tf_op jit(solution)/shard_map/ppermute | solution.py:86
  371.8 27.9 %collective-permute-start.26 = (bf16[96,2048]{1,0:T(8,128)(2,1)S(1)}, bf16[96,2048]{1,0:T(8,128)(2,1)S(1)}, u32[]{:S(2)}, u32[]{:S(2)}) collective-permute-start(bf16[96,2048]{1,0:T(8,128)(2,1)S(1)} %get-tuple-element.234), channel_id=1, source_target_pairs={{0,3},{1,2},{2,1},{3,0},{4,7},{5,6},{6,5},{7,4},{8,11},{9,10},{10,... | collective-permute-start | bytes 1179656 | tf_op jit(solution)/shard_map/ppermute | solution.py:86
  467.0 14.0 %collective-permute-start.31 = (bf16[96,2048]{1,0:T(8,128)(2,1)S(1)}, bf16[96,2048]{1,0:T(8,128)(2,1)S(1)}, u32[]{:S(2)}, u32[]{:S(2)}) collective-permute-start(bf16[96,2048]{1,0:T(8,128)(2,1)S(1)} %get-tuple-element.231), channel_id=1, source_target_pairs={{0,3},{1,2},{2,1},{3,0},{4,7},{5,6},{6,5},{7,4},{8,11},{9,10},{10,... | collective-permute-start | bytes 1179656 | tf_op jit(solution)/shard_map/ppermute | solution.py:86
  470.4 33.9 %collective-permute-start.30 = (bf16[96,2048]{1,0:T(8,128)(2,1)S(1)}, bf16[96,2048]{1,0:T(8,128)(2,1)S(1)}, u32[]{:S(2)}, u32[]{:S(2)}) collective-permute-start(bf16[96,2048]{1,0:T(8,128)(2,1)S(1)} %get-tuple-element.232), channel_id=1, source_target_pairs={{0,2},{1,3},{2,0},{3,1},{4,6},{5,7},{6,4},{7,5},{8,10},{9,11},{10,... | collective-permute-start | bytes 1179656 | tf_op jit(solution)/shard_map/ppermute | solution.py:86
  470.4 33.9 %collective-permute-start.29 = (bf16[96,2048]{1,0:T(8,128)(2,1)S(1)}, bf16[96,2048]{1,0:T(8,128)(2,1)S(1)}, u32[]{:S(2)}, u32[]{:S(2)}) collective-permute-start(bf16[96,2048]{1,0:T(8,128)(2,1)S(1)} %get-tuple-element.233), channel_id=1, source_target_pairs={{0,1},{1,0},{2,3},{3,2},{4,5},{5,4},{6,7},{7,6},{8,9},{9,8},{10,11... | collective-permute-start | bytes 1179656 | tf_op jit(solution)/shard_map/ppermute | solution.py:86
  507.6 36.5 %collective-permute-start.35 = (bf16[96,2048]{1,0:T(8,128)(2,1)S(1)}, bf16[96,2048]{1,0:T(8,128)(2,1)S(1)}, u32[]{:S(2)}, u32[]{:S(2)}) collective-permute-start(bf16[96,2048]{1,0:T(8,128)(2,1)S(1)} %get-tuple-element.226), channel_id=1, source_target_pairs={{0,4},{4,0},{8,12},{12,8},{16,20},{20,16},{24,28},{28,24},{1,5},{5... | collective-permute-start | bytes 1179656 | tf_op jit(solution)/shard_map/ppermute | solution.py:80
  507.7 13.9 %collective-permute-start.34 = (bf16[96,2048]{1,0:T(8,128)(2,1)S(1)}, bf16[96,2048]{1,0:T(8,128)(2,1)S(1)}, u32[]{:S(2)}, u32[]{:S(2)}) collective-permute-start(bf16[96,2048]{1,0:T(8,128)(2,1)S(1)} %get-tuple-element.227), channel_id=1, source_target_pairs={{0,3},{1,2},{2,1},{3,0},{4,7},{5,6},{6,5},{7,4},{8,11},{9,10},{10,... | collective-permute-start | bytes 1179656 | tf_op jit(solution)/shard_map/ppermute | solution.py:86
  510.1 33.4 %collective-permute-start.33 = (bf16[96,2048]{1,0:T(8,128)(2,1)S(1)}, bf16[96,2048]{1,0:T(8,128)(2,1)S(1)}, u32[]{:S(2)}, u32[]{:S(2)}) collective-permute-start(bf16[96,2048]{1,0:T(8,128)(2,1)S(1)} %get-tuple-element.228), channel_id=1, source_target_pairs={{0,2},{1,3},{2,0},{3,1},{4,6},{5,7},{6,4},{7,5},{8,10},{9,11},{10,... | collective-permute-start | bytes 1179656 | tf_op jit(solution)/shard_map/ppermute | solution.py:86
  510.1 33.4 %collective-permute-start.32 = (bf16[96,2048]{1,0:T(8,128)(2,1)S(1)}, bf16[96,2048]{1,0:T(8,128)(2,1)S(1)}, u32[]{:S(2)}, u32[]{:S(2)}) collective-permute-start(bf16[96,2048]{1,0:T(8,128)(2,1)S(1)} %get-tuple-element.229), channel_id=1, source_target_pairs={{0,1},{1,0},{2,3},{3,2},{4,5},{5,4},{6,7},{7,6},{8,9},{9,8},{10,11... | collective-permute-start | bytes 1179656 | tf_op jit(solution)/shard_map/ppermute | solution.py:86
  521.6 24.3 %collective-permute-start.38 = (bf16[96,2048]{1,0:T(8,128)(2,1)S(1)}, bf16[96,2048]{1,0:T(8,128)(2,1)S(1)}, u32[]{:S(2)}, u32[]{:S(2)}) collective-permute-start(bf16[96,2048]{1,0:T(8,128)(2,1)S(1)} %collective-permute-done.34), channel_id=1, source_target_pairs={{0,4},{4,0},{8,12},{12,8},{16,20},{20,16},{24,28},{28,24},{1,5},{5... | collective-permute-start | bytes 1179656 | tf_op jit(solution)/shard_map/ppermute | solution.py:80
  559.7 318.2 %reduce-scatter.6.cloned.1.call-start = ((), (), s32[]{:S(2)}) async-start(), calls=%async_computation.7 | async-start | bytes 28835840 | tf_op jit(solution)/shard_map/reduce_scatter | solution.py:99
  620.2 28.8 %collective-permute-start.42 = (bf16[96,2048]{1,0:T(8,128)(2,1)}, bf16[96,2048]{1,0:T(8,128)(2,1)}, u32[]{:S(2)}, u32[]{:S(2)}) collective-permute-start(bf16[96,2048]{1,0:T(8,128)(2,1)} %get-tuple-element.223), channel_id=1, source_target_pairs={{0,3},{1,2},{2,1},{3,0},{4,7},{5,6},{6,5},{7,4},{8,11},{9,10},{10,... | collective-permute-start | bytes 1179656 | tf_op jit(solution)/shard_map/ppermute | solution.py:86
  620.6 33.5 %collective-permute-start.41 = (bf16[96,2048]{1,0:T(8,128)(2,1)S(1)}, bf16[96,2048]{1,0:T(8,128)(2,1)}, u32[]{:S(2)}, u32[]{:S(2)}) collective-permute-start(bf16[96,2048]{1,0:T(8,128)(2,1)S(1)} %get-tuple-element.224), channel_id=1, source_target_pairs={{0,2},{1,3},{2,0},{3,1},{4,6},{5,7},{6,4},{7,5},{8,10},{9,11},{10,... | collective-permute-start | bytes 1179656 | tf_op jit(solution)/shard_map/ppermute | solution.py:86
  620.6 33.5 %collective-permute-start.40 = (bf16[96,2048]{1,0:T(8,128)(2,1)S(1)}, bf16[96,2048]{1,0:T(8,128)(2,1)}, u32[]{:S(2)}, u32[]{:S(2)}) collective-permute-start(bf16[96,2048]{1,0:T(8,128)(2,1)S(1)} %get-tuple-element.225), channel_id=1, source_target_pairs={{0,1},{1,0},{2,3},{3,2},{4,5},{5,4},{6,7},{7,6},{8,9},{9,8},{10,11... | collective-permute-start | bytes 1179656 | tf_op jit(solution)/shard_map/ppermute | solution.py:86
  670.1 319.0 %reduce-scatter.8.cloned.1.call-start = ((), (), s32[]{:S(2)}) async-start(), calls=%async_computation.8 | async-start | bytes 13762560 | tf_op jit(solution)/shard_map/reduce_scatter | solution.py:99
  676.6 29.8 %collective-permute-start.44 = (bf16[96,2048]{1,0:T(8,128)(2,1)S(1)}, bf16[96,2048]{1,0:T(8,128)(2,1)S(1)}, u32[]{:S(2)}, u32[]{:S(2)}) collective-permute-start(bf16[96,2048]{1,0:T(8,128)(2,1)S(1)} %get-tuple-element.220), channel_id=1, source_target_pairs={{0,2},{1,3},{2,0},{3,1},{4,6},{5,7},{6,4},{7,5},{8,10},{9,11},{10,... | collective-permute-start | bytes 1179656 | tf_op jit(solution)/shard_map/ppermute | solution.py:86
  679.1 18.0 %collective-permute-start.43 = (bf16[96,2048]{1,0:T(8,128)(2,1)S(1)}, bf16[96,2048]{1,0:T(8,128)(2,1)S(1)}, u32[]{:S(2)}, u32[]{:S(2)}) collective-permute-start(bf16[96,2048]{1,0:T(8,128)(2,1)S(1)} %get-tuple-element.221), channel_id=1, source_target_pairs={{0,1},{1,0},{2,3},{3,2},{4,5},{5,4},{6,7},{7,6},{8,9},{9,8},{10,11... | collective-permute-start | bytes 1179656 | tf_op jit(solution)/shard_map/ppermute | solution.py:86
  680.8 25.6 %collective-permute-start.45 = (bf16[96,2048]{1,0:T(8,128)(2,1)S(1)}, bf16[96,2048]{1,0:T(8,128)(2,1)S(1)}, u32[]{:S(2)}, u32[]{:S(2)}) collective-permute-start(bf16[96,2048]{1,0:T(8,128)(2,1)S(1)} %get-tuple-element.219), channel_id=1, source_target_pairs={{0,3},{1,2},{2,1},{3,0},{4,7},{5,6},{6,5},{7,4},{8,11},{9,10},{10,... | collective-permute-start | bytes 1179656 | tf_op jit(solution)/shard_map/ppermute | solution.py:86
  735.4 71.4 %collective-permute-start.52 = (bf16[4,8,128,128]{2,3,1,0:T(8,128)(2,1)}, bf16[4,8,128,128]{2,3,1,0:T(8,128)(2,1)}, u32[]{:S(2)}, u32[]{:S(2)}) collective-permute-start(bf16[4,8,128,128]{2,3,1,0:T(8,128)(2,1)} %pad_maximum_fusion.12), channel_id=1, source_target_pairs={{0,1},{1,0},{2,3},{3,2},{4,5},{5,4},{6,7},{7,6},{8,9},{9,8},{10,11... | collective-permute-start | bytes 3145736 | tf_op jit(solution)/shard_map/ppermute | solution.py:86
  744.8 62.0 %collective-permute-start.53 = (bf16[4,8,128,128]{2,3,1,0:T(8,128)(2,1)}, bf16[4,8,128,128]{2,3,1,0:T(8,128)(2,1)}, u32[]{:S(2)}, u32[]{:S(2)}) collective-permute-start(bf16[4,8,128,128]{2,3,1,0:T(8,128)(2,1)} %pad_maximum_fusion.13), channel_id=1, source_target_pairs={{0,2},{1,3},{2,0},{3,1},{4,6},{5,7},{6,4},{7,5},{8,10},{9,11},{10,... | collective-permute-start | bytes 3145736 | tf_op jit(solution)/shard_map/ppermute | solution.py:86
  801.0 23.8 %collective-permute-start.54 = (bf16[4,8,128,128]{2,3,1,0:T(8,128)(2,1)S(1)}, bf16[4,8,128,128]{2,3,1,0:T(8,128)(2,1)S(1)}, u32[]{:S(2)}, u32[]{:S(2)}) collective-permute-start(bf16[4,8,128,128]{2,3,1,0:T(8,128)(2,1)S(1)} %pad_maximum_fusion.14), channel_id=1, source_target_pairs={{0,3},{1,2},{2,1},{3,0},{4,7},{5,6},{6,5},{7,4},{8,11},{9,10},{10,... | collective-permute-start | bytes 3145736 | tf_op jit(solution)/shard_map/ppermute | solution.py:86
  885.3 12.7 %collective-permute-start.58 = (bf16[256,5632]{1,0:T(8,128)(2,1)}, bf16[256,5632]{1,0:T(8,128)(2,1)}, u32[]{:S(2)}, u32[]{:S(2)}) collective-permute-start(bf16[256,5632]{1,0:T(8,128)(2,1)} %constant_dynamic-slice_fusion.7), channel_id=1, source_target_pairs={{0,4},{4,0},{8,12},{12,8},{16,20},{20,16},{24,28},{28,24},{1,5},{5... | collective-permute-start | bytes 8650760 | tf_op jit(solution)/shard_map/ppermute | solution.py:80
  892.0 32.6 %collective-permute-start.56 = (bf16[128,2048]{1,0:T(8,128)(2,1)}, bf16[128,2048]{1,0:T(8,128)(2,1)}, u32[]{:S(2)}, u32[]{:S(2)}) collective-permute-start(bf16[128,2048]{1,0:T(8,128)(2,1)} %get-tuple-element.206), channel_id=1, source_target_pairs={{0,1},{1,0},{2,3},{3,2},{4,5},{5,4},{6,7},{7,6},{8,9},{9,8},{10,11... | collective-permute-start | bytes 1572872 | tf_op jit(solution)/shard_map/ppermute | solution.py:86
  893.4 31.1 %collective-permute-start.57 = (bf16[128,2048]{1,0:T(8,128)(2,1)}, bf16[128,2048]{1,0:T(8,128)(2,1)}, u32[]{:S(2)}, u32[]{:S(2)}) collective-permute-start(bf16[128,2048]{1,0:T(8,128)(2,1)} %get-tuple-element.208), channel_id=1, source_target_pairs={{0,2},{1,3},{2,0},{3,1},{4,6},{5,7},{6,4},{7,5},{8,10},{9,11},{10,... | collective-permute-start | bytes 1572872 | tf_op jit(solution)/shard_map/ppermute | solution.py:86
  923.9 15.4 %collective-permute-start.59 = (bf16[128,2048]{1,0:T(8,128)(2,1)S(1)}, bf16[128,2048]{1,0:T(8,128)(2,1)S(1)}, u32[]{:S(2)}, u32[]{:S(2)}) collective-permute-start(bf16[128,2048]{1,0:T(8,128)(2,1)S(1)} %get-tuple-element.73), channel_id=1, source_target_pairs={{0,3},{1,2},{2,1},{3,0},{4,7},{5,6},{6,5},{7,4},{8,11},{9,10},{10,... | collective-permute-start | bytes 1572872 | tf_op jit(solution)/shard_map/ppermute | solution.py:86
  997.2 16.9 %collective-permute-start.64 = (bf16[2,64,640]{2,1,0:T(8,128)(2,1)}, bf16[2,64,640]{2,1,0:T(8,128)(2,1)}, u32[]{:S(2)}, u32[]{:S(2)}) collective-permute-start(bf16[2,64,640]{2,1,0:T(8,128)(2,1)} %get-tuple-element.260), channel_id=1, source_target_pairs={{0,3},{1,2},{2,1},{3,0},{4,7},{5,6},{6,5},{7,4},{8,11},{9,10},{10,... | collective-permute-start | bytes 491528 | tf_op jit(solution)/shard_map/ppermute | solution.py:86
  1000.5 14.7 %collective-permute-start.63 = (bf16[2,64,640]{2,1,0:T(8,128)(2,1)}, bf16[2,64,640]{2,1,0:T(8,128)(2,1)}, u32[]{:S(2)}, u32[]{:S(2)}) collective-permute-start(bf16[2,64,640]{2,1,0:T(8,128)(2,1)} %get-tuple-element.261), channel_id=1, source_target_pairs={{0,2},{1,3},{2,0},{3,1},{4,6},{5,7},{6,4},{7,5},{8,10},{9,11},{10,... | collective-permute-start | bytes 491528 | tf_op jit(solution)/shard_map/ppermute | solution.py:86
  1000.5 14.7 %collective-permute-start.62 = (bf16[2,64,640]{2,1,0:T(8,128)(2,1)S(1)}, bf16[2,64,640]{2,1,0:T(8,128)(2,1)}, u32[]{:S(2)}, u32[]{:S(2)}) collective-permute-start(bf16[2,64,640]{2,1,0:T(8,128)(2,1)S(1)} %get-tuple-element.262), channel_id=1, source_target_pairs={{0,1},{1,0},{2,3},{3,2},{4,5},{5,4},{6,7},{7,6},{8,9},{9,8},{10,11... | collective-permute-start | bytes 491528 | tf_op jit(solution)/shard_map/ppermute | solution.py:86
  (143 other events, 2090.9 us)
Sparse Core Ops, SparseCore 0:
  18.9 90.1 all-gather.3
  111.6 217.4 all-gather.5
  331.5 113.6 all-gather.7
  559.8 110.2 reduce-scatter.3
  673.0 204.8 reduce-scatter.5
  881.2 107.7 reduce-scatter.7
